TPU v7x, 128 devices: a whole 4x4x4 slice. The times are simulated.
128 devices in a mesh: ens: 8 (over x, core), dom: 16 (over y, z).
Axes of the slice: x: 4, y: 4, z: 4, core: 2. Of those that a mesh axis runs over, the one named last changes fastest.
Arguments:
- obs_members: float32 [64, 256, 1024], P('dom', 'ens'), may hold values from -2.4 to 2.4
- innovations: float32 [64, 1024], P('dom'), may hold values from -24 to 24
- error_inverse: float32 [64, 1024], P('dom'), may hold values from 0.5 to 2
- loc_table: float32 [64], replicated, may hold values from 0.2 to 1
- counts: int32 [16, 5], replicated, may hold values from 0 to 4, as said below
- block_picks: int32 [16, 5, 4], replicated, may hold values from 0 to 3, as said below
- loc_index: int32 [16, 32, 5, 4], P('dom', 'ens'), may hold values from 0 to 63
- background: float32 [16, 32, 256, 1024], P('dom', 'ens'), may hold values from -6 to 6
Outputs:
- analysis: float32 [16, 32, 256, 1024], P('dom', 'ens')
Inputs may be any that keep to these rules, and one draw needn't show every extreme that they name: counts[t, 2] is 4 for every tile t, and in every draw one tile has 4 in every entry. Each block_picks[t, o, :] is a permutation of 0 .. 3.
All inputs are finite; a program needn't handle non-finite values.
Results may differ from a plain program's by a relative error of at most 0.0003.
Values sent between devices are 32-bit elements; how exact they have to be, the bound alone decides.
No kernel may reach another device: no remote copies, remote signals or barrier semaphores. Data moves between devices by JAX's collectives and lax.ppermute only.
A program may use at most 192 MiB of HBM per device.

v0:
```python
import jax
import jax.numpy as jnp
from jax import lax
from jax.sharding import PartitionSpec as P

NS_STEPS = 6


precise = lax.Precision.HIGHEST


def shifted(value, axis, steps):
    count = lax.axis_size(axis)
    pairs = [(source, (source + steps) % count) for source in range(count)]
    return lax.ppermute(value, axis, pairs)


def root_transform(gram_sum, drive_sum):
    members = gram_sum.shape[-1]
    identity = jnp.eye(members, dtype=jnp.float32)
    system = (members - 1.0) * identity + gram_sum
    norm_scale = jnp.sqrt(jnp.sum(system * system, axis=(1, 2)))[:, None, None]
    root_y = system / norm_scale
    root_q = jnp.broadcast_to(identity, system.shape)
    for iteration in range(NS_STEPS):
        half_step = 1.5 * identity - 0.5 * jnp.matmul(root_q, root_y, precision=precise)
        root_y = jnp.matmul(root_y, half_step, precision=precise)
        root_q = jnp.matmul(half_step, root_q, precision=precise)
    spread = jnp.sqrt((members - 1.0) / norm_scale) * root_q
    inner = jnp.einsum("pkl,pl->pk", root_q, drive_sum, precision=precise)
    mean_weights = jnp.einsum("pkl,pl->pk", root_q, inner, precision=precise) / norm_scale[:, :, 0]
    return spread + mean_weights[:, :, None]


def local(
    obs_members, innovations, error_inverse, loc_table, counts, block_picks, loc_index, background
):
    tile_count = lax.axis_size("dom")
    tile_index = lax.axis_index("dom")
    offsets = counts.shape[1]
    reach_tiles = (offsets - 1) // 2
    block_cap = obs_members.shape[0]
    slot_count = offsets * block_cap
    member_parts = []
    innov_parts = []
    inverse_parts = []
    full_owned = lax.all_gather(obs_members, "ens", axis=1, tiled=True)
    for offset in range(offsets):
        target = (tile_index + reach_tiles - offset) % tile_count
        picked_row = lax.dynamic_index_in_dim(block_picks, target, 0, keepdims=False)
        chosen = picked_row[offset]
        packet = (
            jnp.take(full_owned, chosen, axis=0),
            jnp.take(innovations, chosen, axis=0),
            jnp.take(error_inverse, chosen, axis=0),
        )
        if offset != reach_tiles:
            packet = shifted((packet[0], packet[1], packet[2]), "dom", reach_tiles - offset)
        member_parts.append(packet[0])
        innov_parts.append(packet[1])
        inverse_parts.append(packet[2])
    members = jnp.concatenate(member_parts, axis=0)
    innov_slots = jnp.concatenate(innov_parts, axis=0)
    inverse = jnp.concatenate(inverse_parts, axis=0)
    own_counts = lax.dynamic_index_in_dim(counts, tile_index, 0, keepdims=False)
    live_mask = (jnp.arange(block_cap, dtype=jnp.int32)[None, :] < own_counts[:, None]).astype(
        jnp.float32
    )
    bin_count = loc_table.shape[0]
    lookup = (loc_index[0][..., None] == jnp.arange(bin_count, dtype=jnp.int32)).astype(jnp.float32)
    table_weight = jnp.sum(lookup * loc_table, axis=-1)
    points = table_weight.shape[0]
    slot_weight = (table_weight * live_mask[None]).reshape(points, slot_count)

    def one_point(weight_row):
        obs_weight = weight_row[:, None] * inverse
        weighted = members * obs_weight[:, None, :]
        gram_sum = jnp.einsum("skn,sln->kl", weighted, members, precision=precise)
        drive_sum = jnp.einsum("skn,sn->k", weighted, innov_slots, precision=precise)
        return (gram_sum, drive_sum)

    grams, drives = lax.map(one_point, slot_weight)
    transform = root_transform(grams, drives)
    analysis = jnp.einsum("pkm,pkg->pmg", transform, background[0], precision=precise)
    return analysis[None]


def solution(mesh):
    placed = (
        P("dom", "ens", None),
        P("dom", None),
        P("dom", None),
        P(),
        P(),
        P(),
        P("dom", "ens", None, None),
        P("dom", "ens", None, None),
    )
    return jax.shard_map(
        local, mesh=mesh, in_specs=placed, out_specs=P("dom", "ens", None, None), check_vma=False
    )
```

profile of v0, /device:TPU:1, one launch (start us, length us, event | category | flops | bytes accessed | tf_op | source)
XLA Modules:
  0.0 675.9 jit_solution(17737724715704963526)
XLA Ops:
  8.5 36.3 %all-gather.2.cloned.1.call-done = f32[4,256,1024]{2,1,0:T(8,128)} async-done(((f32[4,32,1024]{2,1,0:T(8,128)}), f32[4,256,1024]{2,1,0:T(8,128)}) %all-gather.2.cloned.1.call-update) | async-done | bytes 4194320 | tf_op jit(solution)/shard_map/all_gather | solution.py:47
  44.8 5.0 gather_fusion.5
  49.8 5.1 broadcast_select_fusion.3
  62.7 5.1 broadcast_select_fusion.2
  73.1 5.0 broadcast_select_fusion.1
  82.5 5.1 gather_fusion.9
  87.6 5.2 broadcast_select_fusion
  101.6 242.7 %collective-permute-done.11 = f32[4,1024]{1,0:T(4,128)S(1)} collective-permute-done((f32[4,1024]{1,0:T(4,128)S(1)}, f32[4,1024]{1,0:T(4,128)S(1)}, u32[]{:S(2)}, u32[]{:S(2)}) %collective-permute-start.11) | collective-permute-done | bytes 16416 | tf_op jit(solution)/shard_map/ppermute | solution.py:15
  345.5 73.7 %collective-permute-done.10 = f32[4,1024]{1,0:T(4,128)S(1)} collective-permute-done((f32[4,1024]{1,0:T(4,128)S(1)}, f32[4,1024]{1,0:T(4,128)S(1)}, u32[]{:S(2)}, u32[]{:S(2)}) %collective-permute-start.10) | collective-permute-done | bytes 16416 | tf_op jit(solution)/shard_map/ppermute | solution.py:15
  419.7 5.4 collective-permute-done.9
  425.2 6.1 collective-permute-done.8
  438.0 5.9 collective-permute-done.1
  444.5 6.1 collective-permute-done
  467.5 7.0 %copy-done.2 = f32[20,256,1024]{2,1,0:T(8,128)} copy-done((f32[20,256,1024]{2,1,0:T(8,128)}, f32[20,256,1024]{2,1,0:T(8,128)S(1)}, u32[]{:S(2)}) %copy-start.2) | copy-done | bytes 20971544
  474.4 166.6 %while.12 = (s32[]{:T(128)}, f32[4,256,256]{2,1,0:T(8,128)S(1)}, f32[4,256]{1,0:T(4,128)S(1)}, f32[4,20]{1,0:T(4,128)S(1)}, f32[20,1024]{1,0:T(8,128)S(1)}, /*in...) while((s32[]{:T(128)}, f32[4,256,256]{2,1,0:T(8,128)S(1)}, ...), condition=%wide.region_2.5_spmd, body=%wide.region_1.4_spmd.sunk | while | flops 16179548160 | bytes 63606612 | solution.py:82
  474.5 19.1 %fusion.95 = f32[1,256]{1,0:T(1,128)S(1)} fusion(f32[20,256,1024]{2,1,0:T(8,128)} %get-tuple-element.146, f32[20,1024]{1,0:T(8,128)S(1)} %broadcast_multiply_fusion.3, f32[20,1024,1]{1,0,2:T(8,128)S(1)} %bitcast.72), kind=kOutput, calls=%fused_computation.23.clone.1 | convolution fusion | flops 68157440 | bytes 21136384 | tf_op jit(solution)/shard_map/while/body/eval_jaxpr/skn,sn->k/dot_general | solution.py:79
  493.7 22.3 %fusion.94 = f32[4,256,256]{2,1,0:T(8,128)S(1)} fusion(f32[4,256,256]{2,1,0:T(8,128)S(1)} %get-tuple-element.133, s32[]{:T(128)} %get-tuple-element.132, f32[20,256,1024]{2,1,0:T(8,128)} %get-tuple-element.146, f32[20,1024]{1,0:T(8,128)S(1)} %broadcast_multiply_fusion.3), kind=kOutput, calls=%fused_computation.22.clone.1 | convolution fusion | flops 16111370240 | bytes 42304000 | tf_op jit(solution)/shard_map/while/body/eval_jaxpr/skn,sln->kl/dot_general | solution.py:78
  516.1 19.1 %fusion.95 = f32[1,256]{1,0:T(1,128)S(1)} fusion(f32[20,256,1024]{2,1,0:T(8,128)} %get-tuple-element.146, f32[20,1024]{1,0:T(8,128)S(1)} %broadcast_multiply_fusion.3, f32[20,1024,1]{1,0,2:T(8,128)S(1)} %bitcast.72), kind=kOutput, calls=%fused_computation.23.clone.1 | convolution fusion | flops 68157440 | bytes 21136384 | tf_op jit(solution)/shard_map/while/body/eval_jaxpr/skn,sn->k/dot_general | solution.py:79
  535.3 22.3 %fusion.94 = f32[4,256,256]{2,1,0:T(8,128)S(1)} fusion(f32[4,256,256]{2,1,0:T(8,128)S(1)} %get-tuple-element.133, s32[]{:T(128)} %get-tuple-element.132, f32[20,256,1024]{2,1,0:T(8,128)} %get-tuple-element.146, f32[20,1024]{1,0:T(8,128)S(1)} %broadcast_multiply_fusion.3), kind=kOutput, calls=%fused_computation.22.clone.1 | convolution fusion | flops 16111370240 | bytes 42304000 | tf_op jit(solution)/shard_map/while/body/eval_jaxpr/skn,sln->kl/dot_general | solution.py:78
  557.7 19.1 %fusion.95 = f32[1,256]{1,0:T(1,128)S(1)} fusion(f32[20,256,1024]{2,1,0:T(8,128)} %get-tuple-element.146, f32[20,1024]{1,0:T(8,128)S(1)} %broadcast_multiply_fusion.3, f32[20,1024,1]{1,0,2:T(8,128)S(1)} %bitcast.72), kind=kOutput, calls=%fused_computation.23.clone.1 | convolution fusion | flops 68157440 | bytes 21136384 | tf_op jit(solution)/shard_map/while/body/eval_jaxpr/skn,sn->k/dot_general | solution.py:79
  576.9 22.3 %fusion.94 = f32[4,256,256]{2,1,0:T(8,128)S(1)} fusion(f32[4,256,256]{2,1,0:T(8,128)S(1)} %get-tuple-element.133, s32[]{:T(128)} %get-tuple-element.132, f32[20,256,1024]{2,1,0:T(8,128)} %get-tuple-element.146, f32[20,1024]{1,0:T(8,128)S(1)} %broadcast_multiply_fusion.3), kind=kOutput, calls=%fused_computation.22.clone.1 | convolution fusion | flops 16111370240 | bytes 42304000 | tf_op jit(solution)/shard_map/while/body/eval_jaxpr/skn,sln->kl/dot_general | solution.py:78
  599.3 19.1 %fusion.95 = f32[1,256]{1,0:T(1,128)S(1)} fusion(f32[20,256,1024]{2,1,0:T(8,128)} %get-tuple-element.146, f32[20,1024]{1,0:T(8,128)S(1)} %broadcast_multiply_fusion.3, f32[20,1024,1]{1,0,2:T(8,128)S(1)} %bitcast.72), kind=kOutput, calls=%fused_computation.23.clone.1 | convolution fusion | flops 68157440 | bytes 21136384 | tf_op jit(solution)/shard_map/while/body/eval_jaxpr/skn,sn->k/dot_general | solution.py:79
  618.5 22.3 %fusion.94 = f32[4,256,256]{2,1,0:T(8,128)S(1)} fusion(f32[4,256,256]{2,1,0:T(8,128)S(1)} %get-tuple-element.133, s32[]{:T(128)} %get-tuple-element.132, f32[20,256,1024]{2,1,0:T(8,128)} %get-tuple-element.146, f32[20,1024]{1,0:T(8,128)S(1)} %broadcast_multiply_fusion.3), kind=kOutput, calls=%fused_computation.22.clone.1 | convolution fusion | flops 16111370240 | bytes 42304000 | tf_op jit(solution)/shard_map/while/body/eval_jaxpr/skn,sln->kl/dot_general | solution.py:78
  663.4 5.4 fusion.18
  (127 shorter events, 76.8 us)
Async XLA Ops:
  6.5 86.3 %copy-start = (f32[4,1024]{1,0:T(4,128)S(1)}, f32[4,1024]{1,0:T(4,128)}, u32[]{:S(2)}) copy-start(f32[4,1024]{1,0:T(4,128)} %param.16) | copy-start | bytes 49156
  6.5 38.3 %all-gather.2.cloned.1.call-start = ((), (), s32[]{:S(2)}) async-start(), calls=%async_computation | async-start | bytes 4718592 | tf_op jit(solution)/shard_map/all_gather | solution.py:47
  54.9 400.7 %collective-permute-start.4 = (f32[4,256,1024]{2,1,0:T(8,128)}, f32[4,256,1024]{2,1,0:T(8,128)}, u32[]{:S(2)}, u32[]{:S(2)}) collective-permute-start(f32[4,256,1024]{2,1,0:T(8,128)} %broadcast_select_fusion.3), channel_id=1, source_target_pairs={{0,2},{1,3},{2,4},{3,5},{4,6},{5,7},{6,8},{7,9},{8,10},{9,11},{10,... | collective-permute-start | bytes 12582920 | tf_op jit(solution)/shard_map/ppermute | solution.py:15
  67.8 390.3 %collective-permute-start.5 = (f32[4,256,1024]{2,1,0:T(8,128)}, f32[4,256,1024]{2,1,0:T(8,128)}, u32[]{:S(2)}, u32[]{:S(2)}) collective-permute-start(f32[4,256,1024]{2,1,0:T(8,128)} %broadcast_select_fusion.2), channel_id=1, source_target_pairs={{0,1},{1,2},{2,3},{3,4},{4,5},{5,6},{6,7},{7,8},{8,9},{9,10},{10,1... | collective-permute-start | bytes 12582920 | tf_op jit(solution)/shard_map/ppermute | solution.py:15
  78.1 384.4 %collective-permute-start.6 = (f32[4,256,1024]{2,1,0:T(8,128)}, f32[4,256,1024]{2,1,0:T(8,128)}, u32[]{:S(2)}, u32[]{:S(2)}) collective-permute-start(f32[4,256,1024]{2,1,0:T(8,128)} %broadcast_select_fusion.1), channel_id=1, source_target_pairs={{0,15},{1,0},{2,1},{3,2},{4,3},{5,4},{6,5},{7,6},{8,7},{9,8},{10,9... | collective-permute-start | bytes 12582920 | tf_op jit(solution)/shard_map/ppermute | solution.py:15
  87.6 5.8 copy-start.3
  87.6 331.7 %copy-start.7 = (s32[16,5]{0,1:T(8,128)S(1)}, s32[16,5]{0,1:T(8,128)}, u32[]{:S(2)}) copy-start(s32[16,5]{0,1:T(8,128)} %param.18) | copy-start | bytes 964
  87.6 337.5 %copy-start.6 = (s32[1,4,5,4]{2,3,1,0:T(4,128)S(1)}, s32[1,4,5,4]{2,3,1,0:T(4,128)}, u32[]{:S(2)}) copy-start(s32[1,4,5,4]{2,3,1,0:T(4,128)} %param.20) | copy-start | bytes 964
  87.6 343.7 %copy-start.8 = (f32[64]{0:T(128)S(1)}, f32[64]{0:T(128)}, u32[]{:S(2)}) copy-start(f32[64]{0:T(128)} %param.17) | copy-start | bytes 772
  92.8 372.2 %collective-permute-start.7 = (f32[4,256,1024]{2,1,0:T(8,128)}, f32[4,256,1024]{2,1,0:T(8,128)}, u32[]{:S(2)}, u32[]{:S(2)}) collective-permute-start(f32[4,256,1024]{2,1,0:T(8,128)} %broadcast_select_fusion), channel_id=1, source_target_pairs={{0,14},{1,15},{2,0},{3,1},{4,2},{5,3},{6,4},{7,5},{8,6},{9,7},{10,... | collective-permute-start | bytes 12582920 | tf_op jit(solution)/shard_map/ppermute | solution.py:15
  94.0 250.3 %collective-permute-start.11 = (f32[4,1024]{1,0:T(4,128)S(1)}, f32[4,1024]{1,0:T(4,128)S(1)}, u32[]{:S(2)}, u32[]{:S(2)}) collective-permute-start(f32[4,1024]{1,0:T(4,128)S(1)} %get-tuple-element.68), channel_id=1, source_target_pairs={{0,14},{1,15},{2,0},{3,1},{4,2},{5,3},{6,4},{7,5},{8,6},{9,7},{10,... | collective-permute-start | bytes 49160 | tf_op jit(solution)/shard_map/ppermute | solution.py:15
  344.4 74.8 %collective-permute-start.10 = (f32[4,1024]{1,0:T(4,128)S(1)}, f32[4,1024]{1,0:T(4,128)S(1)}, u32[]{:S(2)}, u32[]{:S(2)}) collective-permute-start(f32[4,1024]{1,0:T(4,128)S(1)} %get-tuple-element.70), channel_id=1, source_target_pairs={{0,15},{1,0},{2,1},{3,2},{4,3},{5,4},{6,5},{7,6},{8,7},{9,8},{10,9... | collective-permute-start | bytes 49160 | tf_op jit(solution)/shard_map/ppermute | solution.py:15
  419.2 5.9 collective-permute-start.9
  425.1 6.2 collective-permute-start.8
  431.3 4.1 collective-permute-start.3
  435.4 2.6 collective-permute-start.2
  438.0 5.9 collective-permute-start.1
  443.9 6.6 collective-permute-start
  458.1 3.5 copy-start.4
  467.5 7.0 %copy-start.2 = (f32[20,256,1024]{2,1,0:T(8,128)}, f32[20,256,1024]{2,1,0:T(8,128)S(1)}, u32[]{:S(2)}) copy-start(f32[20,256,1024]{2,1,0:T(8,128)S(1)} %constant_dynamic-update-slice_fusion) | copy-start | bytes 62914564
  659.0 4.4 copy-start.5
  663.4 5.4 copy-start.1
Sparse Core Ops, SparseCore 0:
  9.1 35.6 all-gather.1
where the time goes:
time: 689 us; the launch traced here: 676 us
  waiting for transfers between devices  383 us (56%)
  matrix products  193 us (28%)
  local copies, waits for them, and re-layouts  50.5 us (7%)
  other arithmetic  22.6 us (3%)
  between operations  14.1 us (2%)
  starting transfers between devices  12.1 us (2%)
    ppermute x12, waiting for transfers between devices, shifted(): return lax.ppermute(value, axis, pairs)  346 us
    dot_general x4, matrix products, one_point(): gram_sum = jnp.einsum('skn,sln->kl', weighted, members, precision=precise)  89.2 us
    dot_general x4, matrix products, one_point(): jnp.einsum('skn,sn->k', weighted, innov_slots, precision=precise)  76.6 us
    all_gather x1, waiting for transfers between devices, local(): full_owned = lax.all_gather(obs_members, 'ens', axis=1, tiled=True)  36.3 us
    gather x5, local copies, waits for them, and re-layouts, local(): jnp.take(full_owned, chosen, axis=0)  24.9 us
    select_n x4, other arithmetic, local(): jnp.take(full_owned, chosen, axis=0)  20.4 us
    unnamed x21, local copies, waits for them, and re-layouts  15.4 us
  transfers between devices with their start and end apart: 13, of which 9 were waited for; matrix products, arithmetic and copies ran while one was open for 8% of the time, Pallas kernels for 0%

commit v1 on v0

v1 whole, which is shorter than its diff:
```python
import jax
import jax.numpy as jnp
from jax import lax
from jax.experimental import pallas as pl
from jax.experimental.pallas import tpu as pltpu
from jax.sharding import PartitionSpec as P

F32 = jnp.float32
BF16 = jnp.bfloat16
HALF_ROWS = 136
NT = (((1,), (1,)), ((), ()))
NN = (((1,), (0,)), ((), ()))


def split2(value):
    high = value.astype(BF16)
    low = (value - high.astype(F32)).astype(BF16)
    return high, low


def dot3(left, right, dims=NN):
    def one(a, b):
        return lax.dot_general(a, b, dims, preferred_element_type=F32)

    return one(left[0], right[0]) + (one(left[0], right[1]) + one(left[1], right[0]))


def iota2(shape, axis):
    return lax.broadcasted_iota(jnp.int32, shape, axis)


def block_kernel(*refs):
    parts = refs[:8]
    inverse_ref, innov_ref, out_ref, high_ref, low_ref = refs[8:]
    place = lax.axis_index("ens")
    chip, core = place // 2, lax.rem(place, 2)
    for index, part in enumerate(parts):
        side = core if index < 4 else 1 - core
        row = pl.multiple_of(side * 128 + lax.rem(chip + 4 - index % 4, 4) * 32, 32)
        high, low = split2(part[...])
        high_ref[pl.ds(row, 32), :] = high
        low_ref[pl.ds(row, 32), :] = low
    inverse = inverse_ref[pl.ds(chip, 1), :]
    innov = innov_ref[pl.ds(chip, 1), :]

    def rows(start, count):
        at = pl.ds(start if isinstance(start, int) else pl.multiple_of(start, 64), count)
        return high_ref[at, :], low_ref[at, :]

    def weighted(pair):
        return split2((pair[0].astype(F32) + pair[1].astype(F32)) * inverse)

    own = rows(core * 128, 128)
    square = dot3(weighted(own), own, NT)
    cross = dot3(weighted(rows(core * 64, 64)), rows(128, 128), NT)
    pull = split2(jnp.broadcast_to(inverse * innov, (16, innov.shape[1])))
    drive = dot3(pull, own, NT)[0:1]
    top = square[:64]
    bottom = pltpu.roll(square[64:], 64, 1)
    row, col = iota2((64, 128), 0), iota2((64, 128), 1)
    packed = jnp.where((col < 64) & (col > row), bottom, top)
    diagonal = jnp.sum(jnp.where(row == col, bottom, 0.0), axis=0, keepdims=True)
    extra_row = iota2((8, 128), 0)
    extra = jnp.where(extra_row == 0, diagonal, jnp.where(extra_row == 1, drive, 0.0))
    out_ref[0:64, :] = packed
    out_ref[64:128, :] = cross
    out_ref[128:136, :] = extra


def combine_kernel(weight_ref, own_ref, first_ref, second_ref, third_ref, mine_ref, other_ref):
    sources = (own_ref, first_ref, second_ref, third_ref)

    def band(step, carry):
        at = pl.ds(pl.multiple_of(step * 8, 8), 8)
        tiles = [source[slot, at, :] for source in sources for slot in range(5)]
        for point in range(8):
            total = tiles[0] * weight_ref[point, 0]
            for slot in range(1, 20):
                total += tiles[slot] * weight_ref[point, slot]
            if point < 4:
                mine_ref[point, at, :] = total
            else:
                other_ref[point - 4, at, :] = total
        return carry

    lax.fori_loop(0, HALF_ROWS // 8, band, 0)


def unpack_square(packed, diagonal):
    row, col = iota2((64, 128), 0), iota2((64, 128), 1)
    flipped = jnp.transpose(jnp.concatenate([packed, jnp.zeros_like(packed)], axis=0))
    top = jnp.where((col < 64) & (col > row), flipped[:64], packed)
    upper = pltpu.roll(packed, 64, 1)
    lower = pltpu.roll(flipped[:64], 64, 1)
    middle = jnp.broadcast_to(pltpu.roll(diagonal, 64, 1)[0:1], (64, 128))
    shifted = col - 64
    corner = jnp.where(shifted > row, upper, jnp.where(shifted < row, lower, middle))
    bottom = jnp.where(col < 64, flipped[64:], corner)
    return jnp.concatenate([top, bottom], axis=0)


def analysis_kernel(mine_ref, theirs_ref, back_ref, out_ref, held, made, in_sem, out_sem):
    points = back_ref.shape[0]

    def chunks():
        for chip in range(4):
            for side in range(2):
                yield chip * 2 + side, (chip * 2 + side) * 32, side * 128 + chip * 32

    def fetch(point, index, outer, inner):
        return pltpu.make_async_copy(
            back_ref.at[point, pl.ds(outer, 32), :],
            held.at[point, pl.ds(inner, 32), :],
            in_sem.at[point, index],
        )

    def leave(point, index, outer, inner):
        return pltpu.make_async_copy(
            made.at[point, pl.ds(inner, 32), :],
            out_ref.at[point, pl.ds(outer, 32), :],
            out_sem.at[point, index],
        )

    for point in range(points):
        for chunk in chunks():
            fetch(point, *chunk).start()

    first = lax.rem(lax.axis_index("ens"), 2) == 0
    identity = (iota2((256, 256), 0) == iota2((256, 256), 1)).astype(F32)
    every = range(points)
    start, scale, drives = [], [], []
    for point in every:
        mine, theirs = mine_ref[point], theirs_ref[point]
        low = jnp.where(first, mine, theirs)
        high = jnp.where(first, theirs, mine)
        cross = jnp.concatenate([low[64:128], high[64:128]], axis=0)
        gram = jnp.concatenate(
            [
                jnp.concatenate([unpack_square(low[:64], low[128:136]), cross], axis=1),
                jnp.concatenate(
                    [jnp.transpose(cross), unpack_square(high[:64], high[128:136])], axis=1
                ),
            ],
            axis=0,
        )
        system = 255.0 * identity + gram
        inverse_norm = lax.rsqrt(jnp.sum(system * system, axis=(0, 1), keepdims=True))
        start.append(system * inverse_norm)
        scale.append(inverse_norm)
        drives.append(jnp.concatenate([low[129:130], high[129:130]], axis=1))

    def two_steps(value, pair):
        squared = [dot3(pair[i], pair[i]) for i in every]
        squared_pair = [split2(squared[i]) for i in every]
        rest = [
            split2(1.6875 * identity - 0.5625 * value[i] + 0.0625 * squared[i]) for i in every
        ]
        return [
            dot3(squared_pair[i], rest[i]) + (2.25 * identity - 2.4375 * value[i]) for i in every
        ]

    pair = [split2(start[i]) for i in every]
    root = two_steps(start, pair)
    root_pair = [split2(root[i]) for i in every]
    value = [dot3(split2(dot3(pair[i], root_pair[i])), root_pair[i]) for i in every]
    pair = [split2(value[i]) for i in every]
    factor_pair = [split2(f) for f in two_steps(value, pair)]
    root_pair = [split2(dot3(factor_pair[i], root_pair[i])) for i in every]
    value = [dot3(split2(dot3(pair[i], factor_pair[i])), factor_pair[i]) for i in every]
    pair = [split2(value[i]) for i in every]
    factor_pair = [split2(f) for f in two_steps(value, pair)]
    root = [dot3(factor_pair[i], root_pair[i]) for i in every]
    for point in every:
        inner = jnp.sum(root[point] * drives[point], axis=1, keepdims=True)
        mean = jnp.sum(root[point] * inner, axis=0, keepdims=True) * scale[point]
        transform = split2(jnp.sqrt(255.0 * scale[point]) * root[point] + mean)
        for chunk in chunks():
            fetch(point, *chunk).wait()
        for part in range(4):
            lanes = pl.ds(part * 256, 256)
            made[point, :, lanes] = dot3(transform, split2(held[point, :, lanes]))
        for chunk in chunks():
            leave(point, *chunk).start()
    for point in every:
        for chunk in chunks():
            leave(point, *chunk).wait()


def along_x(value, steps, swap=0):
    pairs = [(e, ((e // 2 + steps) % 4) * 2 + ((e % 2) ^ swap)) for e in range(8)]
    return lax.ppermute(value, "ens", pairs)


def along_dom(value, steps):
    return lax.ppermute(value, "dom", [(s, (s + steps) % 16) for s in range(16)])


def other_core(value):
    return along_x(value, 0, 1)


def point_weights(loc_table, counts, block_picks, loc_index, tile, chip):
    own_counts = lax.dynamic_index_in_dim(counts, tile, 0, keepdims=False)
    own_picks = lax.dynamic_index_in_dim(block_picks, tile, 0, keepdims=False)
    bins = jnp.arange(loc_table.shape[0], dtype=jnp.int32)
    table = jnp.sum(
        jnp.where(loc_index[..., None] == bins, loc_table, 0.0), axis=-1
    )
    live = jnp.arange(4, dtype=jnp.int32)[None, :] < own_counts[:, None]
    block = lax.rem(chip + 4 - jnp.arange(4, dtype=jnp.int32), 4)
    chosen = live[None] & (own_picks[None] == block[:, None, None])
    weight = jnp.sum(jnp.where(chosen[None], table[:, None], 0.0), axis=-1)
    return weight.reshape(loc_index.shape[0], 20)


def local(
    obs_members, innovations, error_inverse, loc_table, counts, block_picks, loc_index, background
):
    place = lax.axis_index("ens")
    tile = lax.axis_index("dom")
    chip = place // 2
    vmem = pl.BlockSpec(memory_space=pltpu.VMEM)

    def block_of(steps):
        return lax.dynamic_index_in_dim(
            obs_members, lax.rem(chip + steps, 4), 0, keepdims=False
        )

    parts = [block_of(0)] + [along_x(block_of(steps), steps) for steps in (1, 2, 3)]
    parts = parts + [other_core(part) for part in parts]
    weight = point_weights(loc_table, counts, block_picks, loc_index[0], tile, chip)
    weight = jnp.concatenate([weight, other_core(weight)], axis=0)
    half = pl.pallas_call(
        block_kernel,
        out_shape=jax.ShapeDtypeStruct((HALF_ROWS, 128), F32),
        in_specs=[vmem] * 10,
        out_specs=vmem,
        scratch_shapes=[pltpu.VMEM((256, 1024), BF16), pltpu.VMEM((256, 1024), BF16)],
        compiler_params=pltpu.CompilerParams(vmem_limit_bytes=16 << 20),
        name="block_matrices",
    )(*parts, error_inverse, innovations)
    halves = jnp.stack([half if o == 2 else along_dom(half, 2 - o) for o in range(5)])
    arrived = [along_x(halves, steps) for steps in (1, 2, 3)]
    shape = jax.ShapeDtypeStruct((4, HALF_ROWS, 128), F32)
    mine, other = pl.pallas_call(
        combine_kernel,
        out_shape=(shape, shape),
        in_specs=[pl.BlockSpec(memory_space=pltpu.SMEM)] + [vmem] * 4,
        out_specs=(vmem, vmem),
        compiler_params=pltpu.CompilerParams(vmem_limit_bytes=16 << 20),
        name="combine_points",
    )(weight, halves, *arrived)
    theirs = other_core(other)
    points, members, cells = background.shape[1:]
    analysis = pl.pallas_call(
        analysis_kernel,
        out_shape=jax.ShapeDtypeStruct((points, members, cells), F32),
        in_specs=[vmem, vmem, pl.BlockSpec(memory_space=pl.ANY)],
        out_specs=pl.BlockSpec(memory_space=pl.ANY),
        scratch_shapes=[
            pltpu.VMEM((points, members, cells), F32),
            pltpu.VMEM((points, members, cells), F32),
            pltpu.SemaphoreType.DMA((points, 8)),
            pltpu.SemaphoreType.DMA((points, 8)),
        ],
        compiler_params=pltpu.CompilerParams(vmem_limit_bytes=40 << 20),
        name="root_and_analysis",
    )(mine, theirs, background[0])
    return analysis[None]


def solution(mesh):
    placed = (
        P("dom", "ens", None),
        P("dom", None),
        P("dom", None),
        P(),
        P(),
        P(),
        P("dom", "ens", None, None),
        P("dom", "ens", None, None),
    )
    return jax.shard_map(
        local, mesh=mesh, in_specs=placed, out_specs=P("dom", "ens", None, None), check_vma=False
    )
```

time: 689 us -> 75.2 us (0.11); the launches traced: 676 us -> 74.8 us
  waiting for transfers between devices: 383 us -> 24.7 us
  matrix products: 193 us -> 0 us
  local copies, waits for them, and re-layouts: 50.5 us -> 6.86 us
  other arithmetic: 22.6 us -> 0.96 us
  Pallas kernels: 0 us -> 18.2 us
  between operations: 14.1 us -> 0.27 us
  starting transfers between devices: 12.1 us -> 23.7 us
    ppermute x12 -> x16, waiting for transfers between devices: 346 us -> 24.7 us  [the longest x12 18.3 us: along_x(): return lax.ppermute(value, 'ens', pairs)]
    dot_general x28 -> x0, matrix products: 193 us -> none  [the longest x4 89.2 us: one_point(): gram_sum = jnp.einsum('skn,sln->kl', weighted, members, precision=precise)]
    all_gather x1 -> x0, waiting for transfers between devices: 36.3 us -> none  [local(): full_owned = lax.all_gather(obs_members, 'ens', axis=1, tiled=True)]
    gather x15 -> x0, local copies, waits for them, and re-layouts: 30.6 us -> none  [the longest x5 24.9 us: local(): jnp.take(full_owned, chosen, axis=0)]
    select_n x14 -> x0, other arithmetic: 20.8 us -> none  [the longest x4 20.4 us: local(): jnp.take(full_owned, chosen, axis=0)]
    pallas_call x0 -> x3, Pallas kernels: none -> 18.2 us  [the longest x1 15.4 us: local(): pl.pallas_call(analysis_kernel, out_shape=jax.ShapeDtypeStruct((points, m...]
    unnamed x21 -> x12, local copies, waits for them, and re-layouts: 15.4 us -> 3.65 us
    ppermute x12 -> x16, starting transfers between devices: 12.1 us -> 23.7 us  [the longest x12 14.5 us: along_x(): return lax.ppermute(value, 'ens', pairs)]
  transfers between devices with their start and end apart: 13 -> 16, of which waited for: 9 -> 9; matrix products, arithmetic and copies ran while one was open for 8% -> 4% of each run, Pallas kernels for 0% -> 0%
where the time goes in v1:
time: 75.2 us; the launch traced here: 74.8 us
  waiting for transfers between devices  24.7 us (33%)
  starting transfers between devices  23.7 us (32%)
  Pallas kernels  18.2 us (24%)
  local copies, waits for them, and re-layouts  6.86 us (9%)
  other arithmetic  0.96 us (1%)
    ppermute x12, waiting for transfers between devices, along_x(): return lax.ppermute(value, 'ens', pairs)  18.3 us
    pallas_call x1, Pallas kernels, local(): pl.pallas_call(analysis_kernel, out_shape=jax.ShapeDtypeStruct((points, m...  15.4 us
    ppermute x12, starting transfers between devices, along_x(): return lax.ppermute(value, 'ens', pairs)  14.5 us
    ppermute x4, starting transfers between devices, along_dom(): lax.ppermute(value, 'dom', [(s, (s + steps) % 16) for s in range(16)])  9.25 us
    ppermute x4, waiting for transfers between devices, along_dom(): lax.ppermute(value, 'dom', [(s, (s + steps) % 16) for s in range(16)])  6.47 us
    unnamed x12, local copies, waits for them, and re-layouts  3.65 us
    pallas_call x1, Pallas kernels, local(): pl.pallas_call(combine_kernel, out_shape=(shape, shape), in_specs=[pl.Blo...  1.87 us
  transfers between devices with their start and end apart: 16, of which 9 were waited for; matrix products, arithmetic and copies ran while one was open for 4% of the time, Pallas kernels for 0%

profile of v1, /device:TPU:1, one launch (start us, length us, event | category | flops | bytes accessed | tf_op | source)
XLA Modules:
  0.0 74.8 jit_solution(4792712229102682565)
XLA Ops:
  0.0 1.1 %dynamic-slice_bitcast_fusion = (f32[32,1024]{1,0:T(8,128)S(1)}, f32[32,1024]{1,0:T(8,128)S(1)}, f32[32,1024]{1,0:T(8,128)S(1)}, f32[32,1024]{1,0:T(8,128)S(1)}) fusion(f32[4,32,1024]{2,1,0:T(8,128)} %param.8, s32[]{:T(128)S(6)} %select_n.39, s32[]{:T(128)S(6)} %select_n.37, s32[]{:T(128)S(6)} %select_n.36, s32[]{:T(128)S(6)} %select_n.38), kind=kLoop, calls=%fused_computation | loop fusion | bytes 1048592 | tf_op jit(solution)/shard_map/jit(dynamic_index_in_dim)/squeeze | solution.py:225
  1.2 3.4 %collective-permute-start.3 = (f32[32,1024]{1,0:T(8,128)S(1)}, f32[32,1024]{1,0:T(8,128)S(1)}, u32[]{:S(2)}, u32[]{:S(2)}) collective-permute-start(f32[32,1024]{1,0:T(8,128)S(1)} %get-tuple-element.9), channel_id=1, source_target_pairs={{0,96},{16,112},{32,0},{48,16},{64,32},{80,48},{96,64},{112,80},{1... | collective-permute-start | bytes 393224 | tf_op jit(solution)/shard_map/ppermute | solution.py:191
  4.5 1.7 %collective-permute-start.2 = (f32[32,1024]{1,0:T(8,128)S(1)}, f32[32,1024]{1,0:T(8,128)S(1)}, u32[]{:S(2)}, u32[]{:S(2)}) collective-permute-start(f32[32,1024]{1,0:T(8,128)S(1)} %get-tuple-element.12), channel_id=1, source_target_pairs={{0,64},{16,80},{32,96},{48,112},{64,0},{80,16},{96,32},{112,48},{1... | collective-permute-start | bytes 393224 | tf_op jit(solution)/shard_map/ppermute | solution.py:191
  6.3 1.5 %collective-permute-start.4 = (f32[32,1024]{1,0:T(8,128)S(1)}, f32[32,1024]{1,0:T(8,128)S(1)}, u32[]{:S(2)}, u32[]{:S(2)}) collective-permute-start(f32[32,1024]{1,0:T(8,128)S(1)} %get-tuple-element.11.refs_0_), channel_id=1, source_target_pairs={{0,16},{16,0},{32,48},{48,32},{64,80},{80,64},{96,112},{112,96},{1... | collective-permute-start | bytes 393224 | tf_op jit(solution)/shard_map/ppermute | solution.py:191
  7.9 0.9 %dynamic-slice_reduce_fusion = s32[5]{0:T(128)S(1)} fusion(s32[16,5]{0,1:T(8,128)} %param.12, s32[]{:T(128)S(6)} %select_n.32), kind=kLoop, calls=%fused_computation.14 | loop fusion | bytes 44 | tf_op jit(solution)/shard_map/jit(dynamic_index_in_dim)/dynamic_slice | solution.py:203
  9.6 0.8 %select_reduce_fusion = f32[4,5,4]{2,1,0:T(8,128)S(1)} fusion(f32[64]{0:T(128)} %param.11, s32[4,5,4]{2,1,0:T(8,128)S(1)} %copy.13), kind=kLoop, calls=%fused_computation.9 | loop fusion | flops 15280 | bytes 896 | tf_op jit(solution)/shard_map/reduce_sum | solution.py:206
  10.7 1.0 %collective-permute-done.1.refs_1_ = f32[32,1024]{1,0:T(8,128)S(1)} collective-permute-done((f32[32,1024]{1,0:T(8,128)S(1)}, f32[32,1024]{1,0:T(8,128)S(1)}, u32[]{:S(2)}, u32[]{:S(2)}) %collective-permute-start.1) | collective-permute-done | bytes 131104 | tf_op jit(solution)/shard_map/ppermute | solution.py:191
  11.7 2.8 %collective-permute-start.5 = (f32[32,1024]{1,0:T(8,128)S(1)}, f32[32,1024]{1,0:T(8,128)S(1)}, u32[]{:S(2)}, u32[]{:S(2)}) collective-permute-start(f32[32,1024]{1,0:T(8,128)S(1)} %collective-permute-done.1.refs_1_), channel_id=1, source_target_pairs={{0,16},{16,0},{32,48},{48,32},{64,80},{80,64},{96,112},{112,96},{1... | collective-permute-start | bytes 393224 | tf_op jit(solution)/shard_map/ppermute | solution.py:191
  14.5 1.0 %collective-permute-done.5.refs_5_ = f32[32,1024]{1,0:T(8,128)S(1)} collective-permute-done((f32[32,1024]{1,0:T(8,128)S(1)}, f32[32,1024]{1,0:T(8,128)S(1)}, u32[]{:S(2)}, u32[]{:S(2)}) %collective-permute-start.5) | collective-permute-done | bytes 131104 | tf_op jit(solution)/shard_map/ppermute | solution.py:191
  17.3 1.0 %block_matrices.1 = f32[136,128]{1,0:T(8,128)S(1)} custom-call(f32[32,1024]{1,0:T(8,128)S(1)} %get-tuple-element.11.refs_0_, f32[32,1024]{1,0:T(8,128)S(1)} %collective-permute-done.1.refs_1_, f32[32,1024]{1,0:T(8,128)S(1)} %collective-permute-done.2.refs_2_, f32[32,1024]{1,0:T(8,128)S(1)} %collective-permute-done.3.refs_3_, ...), custom_call_target="tpu_custom_call" | custom-call | tf_op jit(solution)/shard_map/block_matrices/pallas_call | solution.py:233
  18.3 3.7 %collective-permute-start.8 = (f32[136,128]{1,0:T(8,128)S(1)}, f32[136,128]{1,0:T(8,128)S(1)}, u32[]{:S(2)}, u32[]{:S(2)}) collective-permute-start(f32[136,128]{1,0:T(8,128)S(1)} %block_matrices.1), channel_id=1, source_target_pairs={{0,2},{1,3},{2,4},{3,5},{4,6},{5,7},{6,8},{7,9},{8,10},{9,11},{10,... | collective-permute-start | bytes 208904 | tf_op jit(solution)/shard_map/ppermute | solution.py:195
  21.9 2.5 %collective-permute-start.11 = (f32[136,128]{1,0:T(8,128)S(1)}, f32[136,128]{1,0:T(8,128)S(1)}, u32[]{:S(2)}, u32[]{:S(2)}) collective-permute-start(f32[136,128]{1,0:T(8,128)S(1)} %block_matrices.1), channel_id=1, source_target_pairs={{0,14},{1,15},{2,0},{3,1},{4,2},{5,3},{6,4},{7,5},{8,6},{9,7},{10,... | collective-permute-start | bytes 208904 | tf_op jit(solution)/shard_map/ppermute | solution.py:195
  24.5 3.0 %collective-permute-start.10 = (f32[136,128]{1,0:T(8,128)S(1)}, f32[136,128]{1,0:T(8,128)S(1)}, u32[]{:S(2)}, u32[]{:S(2)}) collective-permute-start(f32[136,128]{1,0:T(8,128)S(1)} %block_matrices.1), channel_id=1, source_target_pairs={{0,15},{1,0},{2,1},{3,2},{4,3},{5,4},{6,5},{7,6},{8,7},{9,8},{10,9... | collective-permute-start | bytes 208904 | tf_op jit(solution)/shard_map/ppermute | solution.py:195
  27.5 6.5 %collective-permute-done.9 = f32[136,128]{1,0:T(8,128)S(1)} collective-permute-done((f32[136,128]{1,0:T(8,128)S(1)}, f32[136,128]{1,0:T(8,128)S(1)}, u32[]{:S(2)}, u32[]{:S(2)}) %collective-permute-start.9) | collective-permute-done | bytes 69664 | tf_op jit(solution)/shard_map/ppermute | solution.py:195
  34.2 1.4 %collective-permute-start.12 = (f32[5,136,128]{2,1,0:T(8,128)S(1)}, f32[5,136,128]{2,1,0:T(8,128)S(1)}, u32[]{:S(2)}, u32[]{:S(2)}) collective-permute-start(f32[5,136,128]{2,1,0:T(8,128)S(1)} %bitcast_dynamic-update-slice_fusion.own_ref), channel_id=1, source_target_pairs={{0,32},{16,48},{32,64},{48,80},{64,96},{80,112},{96,0},{112,16},{1... | collective-permute-start | bytes 1044488 | tf_op jit(solution)/shard_map/ppermute | solution.py:191
  35.8 2.7 %collective-permute-start = (f32[4,20]{1,0:T(4,128)S(1)}, f32[4,20]{1,0:T(4,128)S(1)}, u32[]{:S(2)}, u32[]{:S(2)}) collective-permute-start(f32[4,20]{1,0:T(4,128)S(1)} %reshape.38), channel_id=1, source_target_pairs={{0,16},{16,0},{32,48},{48,32},{64,80},{80,64},{96,112},{112,96},{1... | collective-permute-start | bytes 968 | tf_op jit(solution)/shard_map/ppermute | solution.py:191
  38.5 0.8 %collective-permute-done = f32[4,20]{1,0:T(4,128)S(1)} collective-permute-done((f32[4,20]{1,0:T(4,128)S(1)}, f32[4,20]{1,0:T(4,128)S(1)}, u32[]{:S(2)}, u32[]{:S(2)}) %collective-permute-start) | collective-permute-done | bytes 352 | tf_op jit(solution)/shard_map/ppermute | solution.py:191
  39.4 2.2 %collective-permute-done.14.third_ref = f32[5,136,128]{2,1,0:T(8,128)S(1)} collective-permute-done((f32[5,136,128]{2,1,0:T(8,128)S(1)}, f32[5,136,128]{2,1,0:T(8,128)S(1)}, u32[]{:S(2)}, u32[]{:S(2)}) %collective-permute-start.14) | collective-permute-done | bytes 348192 | tf_op jit(solution)/shard_map/ppermute | solution.py:191
  41.6 1.2 %collective-permute-done.13.second_ref = f32[5,136,128]{2,1,0:T(8,128)S(1)} collective-permute-done((f32[5,136,128]{2,1,0:T(8,128)S(1)}, f32[5,136,128]{2,1,0:T(8,128)S(1)}, u32[]{:S(2)}, u32[]{:S(2)}) %collective-permute-start.13) | collective-permute-done | bytes 348192 | tf_op jit(solution)/shard_map/ppermute | solution.py:191
  42.8 10.4 %collective-permute-done.12.first_ref = f32[5,136,128]{2,1,0:T(8,128)S(1)} collective-permute-done((f32[5,136,128]{2,1,0:T(8,128)S(1)}, f32[5,136,128]{2,1,0:T(8,128)S(1)}, u32[]{:S(2)}, u32[]{:S(2)}) %collective-permute-start.12) | collective-permute-done | bytes 348192 | tf_op jit(solution)/shard_map/ppermute | solution.py:191
  53.3 1.9 %combine_points.1 = (f32[4,136,128]{2,1,0:T(8,128)S(1)}, f32[4,136,128]{2,1,0:T(8,128)S(1)}) custom-call(f32[8,20]{1,0:T(8,128)S(1)} %pad_maximum_fusion.weight_ref, f32[5,136,128]{2,1,0:T(8,128)S(1)} %bitcast_dynamic-update-slice_fusion.own_ref, f32[5,136,128]{2,1,0:T(8,128)S(1)} %collective-permute-done.12.first_ref, ...), custom_call_target="tpu_custom_call" | custom-call | tf_op jit(solution)/shard_map/combine_points/pallas_call | solution.py:245
  55.9 1.2 %collective-permute-done.15.theirs_ref = f32[4,136,128]{2,1,0:T(8,128)S(1)} collective-permute-done((f32[4,136,128]{2,1,0:T(8,128)S(1)}, f32[4,136,128]{2,1,0:T(8,128)S(1)}, u32[]{:S(2)}, u32[]{:S(2)}) %collective-permute-start.15) | collective-permute-done | bytes 278560 | tf_op jit(solution)/shard_map/ppermute | solution.py:191
  57.1 2.2 %copy-done.1 = f32[1,4,256,1024]{3,2,1,0:T(8,128)S(1)} copy-done((f32[1,4,256,1024]{3,2,1,0:T(8,128)S(1)}, f32[1,4,256,1024]{3,2,1,0:T(8,128)}, u32[]{:S(2)}) %copy-start.1) | copy-done | bytes 4194328
  59.3 15.4 %root_and_analysis.1 = f32[4,256,1024]{2,1,0:T(8,128)} custom-call(f32[4,136,128]{2,1,0:T(8,128)S(1)} %get-tuple-element.7.mine_ref, f32[4,136,128]{2,1,0:T(8,128)S(1)} %collective-permute-done.15.theirs_ref, f32[4,256,1024]{2,1,0:T(8,128)S(1)} %bitcast.22), custom_call_target="tpu_custom_call" | custom-call | tf_op jit(solution)/shard_map/root_and_analysis/pallas_call | solution.py:255
  (37 shorter events, 4.2 us)
Async XLA Ops:
  0.0 7.8 %copy-start = (s32[16,5,4]{0,2,1:T(4,128)S(1)}, s32[16,5,4]{0,2,1:T(4,128)}, u32[]{:S(2)}) copy-start(s32[16,5,4]{0,2,1:T(4,128)} %param.13) | copy-start | bytes 3844
  1.2 9.4 %collective-permute-start.3 = (f32[32,1024]{1,0:T(8,128)S(1)}, f32[32,1024]{1,0:T(8,128)S(1)}, u32[]{:S(2)}, u32[]{:S(2)}) collective-permute-start(f32[32,1024]{1,0:T(8,128)S(1)} %get-tuple-element.9), channel_id=1, source_target_pairs={{0,96},{16,112},{32,0},{48,16},{64,32},{80,48},{96,64},{112,80},{1... | collective-permute-start | bytes 393224 | tf_op jit(solution)/shard_map/ppermute | solution.py:191
  4.5 7.2 %collective-permute-start.1 = (f32[32,1024]{1,0:T(8,128)S(1)}, f32[32,1024]{1,0:T(8,128)S(1)}, u32[]{:S(2)}, u32[]{:S(2)}) collective-permute-start(f32[32,1024]{1,0:T(8,128)S(1)} %get-tuple-element.10), channel_id=1, source_target_pairs={{0,32},{16,48},{32,64},{48,80},{64,96},{80,112},{96,0},{112,16},{1... | collective-permute-start | bytes 393224 | tf_op jit(solution)/shard_map/ppermute | solution.py:191
  4.5 9.9 %collective-permute-start.2 = (f32[32,1024]{1,0:T(8,128)S(1)}, f32[32,1024]{1,0:T(8,128)S(1)}, u32[]{:S(2)}, u32[]{:S(2)}) collective-permute-start(f32[32,1024]{1,0:T(8,128)S(1)} %get-tuple-element.12), channel_id=1, source_target_pairs={{0,64},{16,80},{32,96},{48,112},{64,0},{80,16},{96,32},{112,48},{1... | collective-permute-start | bytes 393224 | tf_op jit(solution)/shard_map/ppermute | solution.py:191
  6.3 8.2 %collective-permute-start.4 = (f32[32,1024]{1,0:T(8,128)S(1)}, f32[32,1024]{1,0:T(8,128)S(1)}, u32[]{:S(2)}, u32[]{:S(2)}) collective-permute-start(f32[32,1024]{1,0:T(8,128)S(1)} %get-tuple-element.11.refs_0_), channel_id=1, source_target_pairs={{0,16},{16,0},{32,48},{48,32},{64,80},{80,64},{96,112},{112,96},{1... | collective-permute-start | bytes 393224 | tf_op jit(solution)/shard_map/ppermute | solution.py:191
  10.6 3.9 %collective-permute-start.7 = (f32[32,1024]{1,0:T(8,128)S(1)}, f32[32,1024]{1,0:T(8,128)S(1)}, u32[]{:S(2)}, u32[]{:S(2)}) collective-permute-start(f32[32,1024]{1,0:T(8,128)S(1)} %collective-permute-done.3.refs_3_), channel_id=1, source_target_pairs={{0,16},{16,0},{32,48},{48,32},{64,80},{80,64},{96,112},{112,96},{1... | collective-permute-start | bytes 393224 | tf_op jit(solution)/shard_map/ppermute | solution.py:191
  11.7 3.7 %collective-permute-start.5 = (f32[32,1024]{1,0:T(8,128)S(1)}, f32[32,1024]{1,0:T(8,128)S(1)}, u32[]{:S(2)}, u32[]{:S(2)}) collective-permute-start(f32[32,1024]{1,0:T(8,128)S(1)} %collective-permute-done.1.refs_1_), channel_id=1, source_target_pairs={{0,16},{16,0},{32,48},{48,32},{64,80},{80,64},{96,112},{112,96},{1... | collective-permute-start | bytes 393224 | tf_op jit(solution)/shard_map/ppermute | solution.py:191
  14.5 1.3 %collective-permute-start.6 = (f32[32,1024]{1,0:T(8,128)S(1)}, f32[32,1024]{1,0:T(8,128)S(1)}, u32[]{:S(2)}, u32[]{:S(2)}) collective-permute-start(f32[32,1024]{1,0:T(8,128)S(1)} %collective-permute-done.2.refs_2_), channel_id=1, source_target_pairs={{0,16},{16,0},{32,48},{48,32},{64,80},{80,64},{96,112},{112,96},{1... | collective-permute-start | bytes 393224 | tf_op jit(solution)/shard_map/ppermute | solution.py:191
  15.8 0.7 copy-start.2
  16.5 0.7 copy-start.3
  18.3 9.3 %collective-permute-start.8 = (f32[136,128]{1,0:T(8,128)S(1)}, f32[136,128]{1,0:T(8,128)S(1)}, u32[]{:S(2)}, u32[]{:S(2)}) collective-permute-start(f32[136,128]{1,0:T(8,128)S(1)} %block_matrices.1), channel_id=1, source_target_pairs={{0,2},{1,3},{2,4},{3,5},{4,6},{5,7},{6,8},{7,9},{8,10},{9,11},{10,... | collective-permute-start | bytes 208904 | tf_op jit(solution)/shard_map/ppermute | solution.py:195
  21.9 12.1 %collective-permute-start.11 = (f32[136,128]{1,0:T(8,128)S(1)}, f32[136,128]{1,0:T(8,128)S(1)}, u32[]{:S(2)}, u32[]{:S(2)}) collective-permute-start(f32[136,128]{1,0:T(8,128)S(1)} %block_matrices.1), channel_id=1, source_target_pairs={{0,14},{1,15},{2,0},{3,1},{4,2},{5,3},{6,4},{7,5},{8,6},{9,7},{10,... | collective-permute-start | bytes 208904 | tf_op jit(solution)/shard_map/ppermute | solution.py:195
  24.5 9.5 %collective-permute-start.10 = (f32[136,128]{1,0:T(8,128)S(1)}, f32[136,128]{1,0:T(8,128)S(1)}, u32[]{:S(2)}, u32[]{:S(2)}) collective-permute-start(f32[136,128]{1,0:T(8,128)S(1)} %block_matrices.1), channel_id=1, source_target_pairs={{0,15},{1,0},{2,1},{3,2},{4,3},{5,4},{6,5},{7,6},{8,7},{9,8},{10,9... | collective-permute-start | bytes 208904 | tf_op jit(solution)/shard_map/ppermute | solution.py:195
  27.5 6.5 %collective-permute-start.9 = (f32[136,128]{1,0:T(8,128)S(1)}, f32[136,128]{1,0:T(8,128)S(1)}, u32[]{:S(2)}, u32[]{:S(2)}) collective-permute-start(f32[136,128]{1,0:T(8,128)S(1)} %block_matrices.1), channel_id=1, source_target_pairs={{0,1},{1,2},{2,3},{3,4},{4,5},{5,6},{6,7},{7,8},{8,9},{9,10},{10,1... | collective-permute-start | bytes 208904 | tf_op jit(solution)/shard_map/ppermute | solution.py:195
  34.1 7.5 %collective-permute-start.14 = (f32[5,136,128]{2,1,0:T(8,128)S(1)}, f32[5,136,128]{2,1,0:T(8,128)S(1)}, u32[]{:S(2)}, u32[]{:S(2)}) collective-permute-start(f32[5,136,128]{2,1,0:T(8,128)S(1)} %bitcast_dynamic-update-slice_fusion.own_ref), channel_id=1, source_target_pairs={{0,96},{16,112},{32,0},{48,16},{64,32},{80,48},{96,64},{112,80},{1... | collective-permute-start | bytes 1044488 | tf_op jit(solution)/shard_map/ppermute | solution.py:191
  34.2 8.6 %collective-permute-start.13 = (f32[5,136,128]{2,1,0:T(8,128)S(1)}, f32[5,136,128]{2,1,0:T(8,128)S(1)}, u32[]{:S(2)}, u32[]{:S(2)}) collective-permute-start(f32[5,136,128]{2,1,0:T(8,128)S(1)} %bitcast_dynamic-update-slice_fusion.own_ref), channel_id=1, source_target_pairs={{0,64},{16,80},{32,96},{48,112},{64,0},{80,16},{96,32},{112,48},{1... | collective-permute-start | bytes 1044488 | tf_op jit(solution)/shard_map/ppermute | solution.py:191
  34.2 19.0 %collective-permute-start.12 = (f32[5,136,128]{2,1,0:T(8,128)S(1)}, f32[5,136,128]{2,1,0:T(8,128)S(1)}, u32[]{:S(2)}, u32[]{:S(2)}) collective-permute-start(f32[5,136,128]{2,1,0:T(8,128)S(1)} %bitcast_dynamic-update-slice_fusion.own_ref), channel_id=1, source_target_pairs={{0,32},{16,48},{32,64},{48,80},{64,96},{80,112},{96,0},{112,16},{1... | collective-permute-start | bytes 1044488 | tf_op jit(solution)/shard_map/ppermute | solution.py:191
  35.8 3.6 %collective-permute-start = (f32[4,20]{1,0:T(4,128)S(1)}, f32[4,20]{1,0:T(4,128)S(1)}, u32[]{:S(2)}, u32[]{:S(2)}) collective-permute-start(f32[4,20]{1,0:T(4,128)S(1)} %reshape.38), channel_id=1, source_target_pairs={{0,16},{16,0},{32,48},{48,32},{64,80},{80,64},{96,112},{112,96},{1... | collective-permute-start | bytes 968 | tf_op jit(solution)/shard_map/ppermute | solution.py:191
  55.1 1.9 %collective-permute-start.15 = (f32[4,136,128]{2,1,0:T(8,128)S(1)}, f32[4,136,128]{2,1,0:T(8,128)S(1)}, u32[]{:S(2)}, u32[]{:S(2)}) collective-permute-start(f32[4,136,128]{2,1,0:T(8,128)S(1)} %get-tuple-element.8), channel_id=1, source_target_pairs={{0,16},{16,0},{32,48},{48,32},{64,80},{80,64},{96,112},{112,96},{1... | collective-permute-start | bytes 835592 | tf_op jit(solution)/shard_map/ppermute | solution.py:191
  57.1 2.2 %copy-start.1 = (f32[1,4,256,1024]{3,2,1,0:T(8,128)S(1)}, f32[1,4,256,1024]{3,2,1,0:T(8,128)}, u32[]{:S(2)}) copy-start(f32[1,4,256,1024]{3,2,1,0:T(8,128)} %param.15) | copy-start | bytes 12582916

commit v2 on v1

--- a/solution.py
+++ b/solution.py
@@ -8,6 +8,7 @@
 F32 = jnp.float32
 BF16 = jnp.bfloat16
 HALF_ROWS = 136
+PACKED_ROWS = 2 * HALF_ROWS
 NT = (((1,), (1,)), ((), ()))
 NN = (((1,), (0,)), ((), ()))
 
@@ -31,17 +32,16 @@
 
 def block_kernel(*refs):
     parts = refs[:8]
-    inverse_ref, innov_ref, out_ref, high_ref, low_ref = refs[8:]
+    scaled_ref, out_ref, high_ref, low_ref = refs[8:]
     place = lax.axis_index("ens")
     chip, core = place // 2, lax.rem(place, 2)
     for index, part in enumerate(parts):
         side = core if index < 4 else 1 - core
-        row = pl.multiple_of(side * 128 + lax.rem(chip + 4 - index % 4, 4) * 32, 32)
+        row = pl.multiple_of(side * 128 + lax.rem(chip + (0, 3, 1, 2)[index % 4], 4) * 32, 32)
         high, low = split2(part[...])
         high_ref[pl.ds(row, 32), :] = high
         low_ref[pl.ds(row, 32), :] = low
-    inverse = inverse_ref[pl.ds(chip, 1), :]
-    innov = innov_ref[pl.ds(chip, 1), :]
+    inverse = scaled_ref[0:1, :]
 
     def rows(start, count):
         at = pl.ds(start if isinstance(start, int) else pl.multiple_of(start, 64), count)
@@ -50,40 +50,53 @@
     def weighted(pair):
         return split2((pair[0].astype(F32) + pair[1].astype(F32)) * inverse)
 
-    own = rows(core * 128, 128)
-    square = dot3(weighted(own), own, NT)
-    cross = dot3(weighted(rows(core * 64, 64)), rows(128, 128), NT)
-    pull = split2(jnp.broadcast_to(inverse * innov, (16, innov.shape[1])))
-    drive = dot3(pull, own, NT)[0:1]
-    top = square[:64]
-    bottom = pltpu.roll(square[64:], 64, 1)
+    pull = split2(jnp.broadcast_to(scaled_ref[1:2, :], (16, scaled_ref.shape[1])))
+    pairs = [rows(0, 128), rows(128, 128)]
+    heavy = [weighted(pair) for pair in pairs]
+    across = dot3(heavy[0], pairs[1], NT)
     row, col = iota2((64, 128), 0), iota2((64, 128), 1)
-    packed = jnp.where((col < 64) & (col > row), bottom, top)
-    diagonal = jnp.sum(jnp.where(row == col, bottom, 0.0), axis=0, keepdims=True)
     extra_row = iota2((8, 128), 0)
-    extra = jnp.where(extra_row == 0, diagonal, jnp.where(extra_row == 1, drive, 0.0))
-    out_ref[0:64, :] = packed
-    out_ref[64:128, :] = cross
-    out_ref[128:136, :] = extra
-
-
-def combine_kernel(weight_ref, own_ref, first_ref, second_ref, third_ref, mine_ref, other_ref):
-    sources = (own_ref, first_ref, second_ref, third_ref)
-
-    def band(step, carry):
-        at = pl.ds(pl.multiple_of(step * 8, 8), 8)
-        tiles = [source[slot, at, :] for source in sources for slot in range(5)]
-        for point in range(8):
-            total = tiles[0] * weight_ref[point, 0]
-            for slot in range(1, 20):
-                total += tiles[slot] * weight_ref[point, slot]
-            if point < 4:
-                mine_ref[point, at, :] = total
-            else:
-                other_ref[point - 4, at, :] = total
-        return carry
-
-    lax.fori_loop(0, HALF_ROWS // 8, band, 0)
+    for side in range(2):
+        square = dot3(heavy[side], pairs[side], NT)
+        drive = dot3(pull, pairs[side], NT)[0:1]
+        top = square[:64]
+        bottom = pltpu.roll(square[64:], 64, 1)
+        base = side * HALF_ROWS
+        out_ref[base : base + 64, :] = jnp.where((col < 64) & (col > row), bottom, top)
+        out_ref[base + 64 : base + 128, :] = across[side * 64 : side * 64 + 64]
+        diagonal = jnp.sum(jnp.where(row == col, bottom, 0.0), axis=0, keepdims=True)
+        out_ref[base + 128 : base + 136, :] = jnp.where(
+            extra_row == 0, diagonal, jnp.where(extra_row == 1, drive, 0.0)
+        )
+
+
+def combine_kernel(weight_ref, same, beside, far, far_near, far_opposite, out_ref):
+    place = lax.axis_index("ens")
+    chip, core = place // 2, lax.rem(place, 2)
+    ahead = lax.rem(chip + 2, 4)
+    near = lax.rem(chip + 3 - 2 * core, 4)
+    swapped = lax.rem(chip + 1 + 2 * core, 4)
+    tiles = [
+        *[(beside.at[i], 1 + 2 * core, b) for i, b in enumerate((chip, near, swapped, ahead))],
+        (far, 4 * core, chip),
+        (far_near.at[0], 4 * core, near),
+        (far_near.at[1], 4 - 4 * core, near),
+        (far_opposite, 4 * core, ahead),
+        (same.at[1], 2, near),
+        (same.at[3 * core], 2, lax.rem(chip + 2 * core, 4)),
+    ]
+
+    for band in range(5):
+        at = pl.ds(band * 56, 56 if band < 4 else 48)
+        for pair in range(2):
+            totals = [None, None]
+            for ref, offset, block in tiles:
+                tile = ref[at, :]
+                for side in range(2):
+                    term = tile * weight_ref[2 * pair + side, offset * 4 + block]
+                    totals[side] = term if totals[side] is None else totals[side] + term
+            for side in range(2):
+                out_ref[2 * pair + side, at, :] = totals[side]
 
 
 def unpack_square(packed, diagonal):
@@ -125,14 +138,12 @@
         for chunk in chunks():
             fetch(point, *chunk).start()
 
-    first = lax.rem(lax.axis_index("ens"), 2) == 0
     identity = (iota2((256, 256), 0) == iota2((256, 256), 1)).astype(F32)
     every = range(points)
     start, scale, drives = [], [], []
     for point in every:
-        mine, theirs = mine_ref[point], theirs_ref[point]
-        low = jnp.where(first, mine, theirs)
-        high = jnp.where(first, theirs, mine)
+        whole = mine_ref[point] + theirs_ref[point]
+        low, high = whole[:HALF_ROWS], whole[HALF_ROWS:]
         cross = jnp.concatenate([low[64:128], high[64:128]], axis=0)
         gram = jnp.concatenate(
             [
@@ -191,25 +202,31 @@
     return lax.ppermute(value, "ens", pairs)
 
 
-def along_dom(value, steps):
-    return lax.ppermute(value, "dom", [(s, (s + steps) % 16) for s in range(16)])
-
-
 def other_core(value):
     return along_x(value, 0, 1)
 
 
-def point_weights(loc_table, counts, block_picks, loc_index, tile, chip):
+def both_ways(value, axis, steps):
+    pairs = []
+    for e in range(8):
+        for t in range(16):
+            way = steps if e % 2 == 0 else -steps
+            if axis == "dom":
+                pairs.append((e * 16 + t, e * 16 + (t + way) % 16))
+            else:
+                pairs.append((e * 16 + t, (((e // 2 + way) % 4) * 2 + e % 2) * 16 + t))
+    return lax.ppermute(value, ("ens", "dom"), pairs)
+
+
+def block_weights(loc_table, counts, block_picks, loc_index, tile):
     own_counts = lax.dynamic_index_in_dim(counts, tile, 0, keepdims=False)
     own_picks = lax.dynamic_index_in_dim(block_picks, tile, 0, keepdims=False)
     bins = jnp.arange(loc_table.shape[0], dtype=jnp.int32)
-    table = jnp.sum(
-        jnp.where(loc_index[..., None] == bins, loc_table, 0.0), axis=-1
-    )
-    live = jnp.arange(4, dtype=jnp.int32)[None, :] < own_counts[:, None]
-    block = lax.rem(chip + 4 - jnp.arange(4, dtype=jnp.int32), 4)
-    chosen = live[None] & (own_picks[None] == block[:, None, None])
-    weight = jnp.sum(jnp.where(chosen[None], table[:, None], 0.0), axis=-1)
+    four = jnp.arange(4, dtype=jnp.int32)
+    live = four[None, :] < own_counts[:, None]
+    chosen = live[:, None, :] & (own_picks[:, None, :] == four[None, :, None])
+    hit = (loc_index[:, :, None, :, None] == bins) & chosen[None, ..., None]
+    weight = jnp.sum(jnp.where(hit, loc_table, 0.0), axis=(3, 4))
     return weight.reshape(loc_index.shape[0], 20)
 
 
@@ -226,44 +243,62 @@
             obs_members, lax.rem(chip + steps, 4), 0, keepdims=False
         )
 
-    parts = [block_of(0)] + [along_x(block_of(steps), steps) for steps in (1, 2, 3)]
+    inverse = lax.dynamic_slice_in_dim(error_inverse, chip, 1, 0)
+    pull = inverse * lax.dynamic_slice_in_dim(innovations, chip, 1, 0)
+    scaled = jnp.concatenate([inverse, pull], axis=0)
+    order = (1, 3, 2)
+    sent = dict(zip(order, [along_x(block_of(steps), steps) for steps in order]))
+    parts = [block_of(0)] + [sent[steps] for steps in order]
     parts = parts + [other_core(part) for part in parts]
-    weight = point_weights(loc_table, counts, block_picks, loc_index[0], tile, chip)
-    weight = jnp.concatenate([weight, other_core(weight)], axis=0)
-    half = pl.pallas_call(
+    whole = pl.pallas_call(
         block_kernel,
-        out_shape=jax.ShapeDtypeStruct((HALF_ROWS, 128), F32),
-        in_specs=[vmem] * 10,
+        out_shape=jax.ShapeDtypeStruct((PACKED_ROWS, 128), F32),
+        in_specs=[vmem] * 9,
         out_specs=vmem,
         scratch_shapes=[pltpu.VMEM((256, 1024), BF16), pltpu.VMEM((256, 1024), BF16)],
         compiler_params=pltpu.CompilerParams(vmem_limit_bytes=16 << 20),
         name="block_matrices",
-    )(*parts, error_inverse, innovations)
-    halves = jnp.stack([half if o == 2 else along_dom(half, 2 - o) for o in range(5)])
-    arrived = [along_x(halves, steps) for steps in (1, 2, 3)]
-    shape = jax.ShapeDtypeStruct((4, HALF_ROWS, 128), F32)
-    mine, other = pl.pallas_call(
+    )(*parts, scaled)
+    whole, local_index, counts, block_picks = lax.optimization_barrier(
+        (whole, loc_index[0], counts, block_picks)
+    )
+    far = both_ways(whole, "dom", 2)
+    near = both_ways(whole, "ens", 1)
+    opposite = along_x(whole, 2)
+    weight = block_weights(loc_table, counts, block_picks, local_index, tile)
+    near, opposite, far, weight = lax.optimization_barrier((near, opposite, far, weight))
+    same = jnp.stack([whole, near, other_core(near), opposite])
+    far_both = jnp.stack([far, other_core(far)])
+    weights = (weight, other_core(weight))
+    same, far, far_both, weights = lax.optimization_barrier((same, far, far_both, weights))
+    far_opposite = along_x(far, 2)
+    far_near = both_ways(far_both, "ens", 1)
+    beside = both_ways(same, "dom", 1)
+    combine = pl.pallas_call(
         combine_kernel,
-        out_shape=(shape, shape),
-        in_specs=[pl.BlockSpec(memory_space=pltpu.SMEM)] + [vmem] * 4,
-        out_specs=(vmem, vmem),
+        out_shape=jax.ShapeDtypeStruct((4, PACKED_ROWS, 128), F32),
+        in_specs=[pl.BlockSpec(memory_space=pltpu.SMEM)] + [vmem] * 5,
+        out_specs=vmem,
         compiler_params=pltpu.CompilerParams(vmem_limit_bytes=16 << 20),
+        cost_estimate=pl.CostEstimate(flops=6000000, bytes_accessed=2000000, transcendentals=0),
         name="combine_points",
-    )(weight, halves, *arrived)
-    theirs = other_core(other)
+    )
+    sources = (same, beside, far, far_near, far_opposite)
+    theirs = other_core(combine(weights[1], *sources))
+    mine = combine(weights[0], *sources)
     points, members, cells = background.shape[1:]
     analysis = pl.pallas_call(
         analysis_kernel,
         out_shape=jax.ShapeDtypeStruct((points, members, cells), F32),
-        in_specs=[vmem, vmem, pl.BlockSpec(memory_space=pl.ANY)],
-        out_specs=pl.BlockSpec(memory_space=pl.ANY),
+        in_specs=[vmem, vmem, pl.BlockSpec(memory_space=pltpu.HBM)],
+        out_specs=pl.BlockSpec(memory_space=pltpu.HBM),
         scratch_shapes=[
             pltpu.VMEM((points, members, cells), F32),
             pltpu.VMEM((points, members, cells), F32),
             pltpu.SemaphoreType.DMA((points, 8)),
             pltpu.SemaphoreType.DMA((points, 8)),
         ],
-        compiler_params=pltpu.CompilerParams(vmem_limit_bytes=40 << 20),
+        compiler_params=pltpu.CompilerParams(vmem_limit_bytes=52 << 20),
         name="root_and_analysis",
     )(mine, theirs, background[0])
     return analysis[None]

time: 75.2 us -> 57.1 us (0.76)
  waiting for transfers between devices: 24.7 us -> 10.3 us
  Pallas kernels: 18.2 us -> 13.5 us
  starting transfers between devices: 23.7 us -> 27.5 us
  local copies, waits for them, and re-layouts: 6.86 us -> 3.18 us
  other arithmetic: 0.96 us -> 1.97 us
    ppermute x12 -> x13, waiting for transfers between devices: 18.3 us -> 9.7 us  [along_x(): return lax.ppermute(value, 'ens', pairs)]
    ppermute x4, waiting for transfers between devices: 6.47 us -> 0.6 us  [both_ways(): return lax.ppermute(value, ('ens', 'dom'), pairs)]
    pallas_call x1, Pallas kernels: 15.4 us -> 10 us  [local(): pl.pallas_call(analysis_kernel, out_shape=jax.ShapeDtypeStruct((points, m...]
    unnamed x12 -> x2, local copies, waits for them, and re-layouts: 3.65 us -> 0.01 us
    ppermute x4, starting transfers between devices: 9.25 us -> 11.9 us  [both_ways(): return lax.ppermute(value, ('ens', 'dom'), pairs)]
    ppermute x12 -> x13, starting transfers between devices: 14.5 us -> 15.5 us  [along_x(): return lax.ppermute(value, 'ens', pairs)]
    optimization_barrier x0 -> x1, local copies, waits for them, and re-layouts: none -> 0.81 us  [local(): lax.optimization_barrier((whole, loc_index[0], counts, block_picks))]
    pallas_call x2 -> x3, Pallas kernels: 2.88 us -> 3.5 us  [the longest x1 1.44 us: local(): pl.pallas_call(block_kernel, out_shape=jax.ShapeDtypeStruct((PACKED_ROWS,...]
  transfers between devices with their start and end apart: 16 -> 17, of which waited for: 9 -> 8; matrix products, arithmetic and copies ran while one was open for 4% -> 7% of each run, Pallas kernels for 0% -> 2%
where the time goes in v2:
time: 57.1 us; the launch traced here: 56.7 us
  starting transfers between devices  27.5 us (48%)
  Pallas kernels  13.5 us (24%)
  waiting for transfers between devices  10.3 us (18%)
  local copies, waits for them, and re-layouts  3.18 us (6%)
  other arithmetic  1.97 us (3%)
    ppermute x13, starting transfers between devices, along_x(): return lax.ppermute(value, 'ens', pairs)  15.5 us
    ppermute x4, starting transfers between devices, both_ways(): return lax.ppermute(value, ('ens', 'dom'), pairs)  11.9 us
    pallas_call x1, Pallas kernels, local(): pl.pallas_call(analysis_kernel, out_shape=jax.ShapeDtypeStruct((points, m...  10 us
    ppermute x13, waiting for transfers between devices, along_x(): return lax.ppermute(value, 'ens', pairs)  9.7 us
    pallas_call x1, Pallas kernels, local(): pl.pallas_call(block_kernel, out_shape=jax.ShapeDtypeStruct((PACKED_ROWS,...  1.44 us
  transfers between devices with their start and end apart: 17, of which 8 were waited for; matrix products, arithmetic and copies ran while one was open for 7% of the time, Pallas kernels for 2%

profile of v2, /device:TPU:1, one launch (start us, length us, event | category | flops | bytes accessed | tf_op | source)
XLA Modules:
  0.0 56.7 jit_solution(9111199754981997797)
XLA Ops:
  0.0 1.1 %dynamic-slice_bitcast_fusion = (f32[32,1024]{1,0:T(8,128)S(1)}, f32[32,1024]{1,0:T(8,128)S(1)}, f32[32,1024]{1,0:T(8,128)S(1)}, f32[32,1024]{1,0:T(8,128)S(1)}) fusion(f32[4,32,1024]{2,1,0:T(8,128)} %param.8, s32[]{:T(128)S(6)} %select_n.36, s32[]{:T(128)S(6)} %select_n.34, s32[]{:T(128)S(6)} %select_n.33, s32[]{:T(128)S(6)} %select_n.35), kind=kLoop, calls=%fused_computation.3 | loop fusion | bytes 1048592 | tf_op jit(solution)/shard_map/jit(dynamic_index_in_dim)/squeeze | solution.py:242
  1.1 3.7 %collective-permute-start.2 = (f32[32,1024]{1,0:T(8,128)S(1)}, f32[32,1024]{1,0:T(8,128)S(1)}, u32[]{:S(2)}, u32[]{:S(2)}) collective-permute-start(f32[32,1024]{1,0:T(8,128)S(1)} %get-tuple-element.31), channel_id=1, source_target_pairs={{0,64},{16,80},{32,96},{48,112},{64,0},{80,16},{96,32},{112,48},{1... | collective-permute-start | bytes 393224 | tf_op jit(solution)/shard_map/ppermute | solution.py:202
  5.1 2.4 %collective-permute-start.1 = (f32[32,1024]{1,0:T(8,128)S(1)}, f32[32,1024]{1,0:T(8,128)S(1)}, u32[]{:S(2)}, u32[]{:S(2)}) collective-permute-start(f32[32,1024]{1,0:T(8,128)S(1)} %get-tuple-element.34), channel_id=1, source_target_pairs={{0,96},{16,112},{32,0},{48,16},{64,32},{80,48},{96,64},{112,80},{1... | collective-permute-start | bytes 393224 | tf_op jit(solution)/shard_map/ppermute | solution.py:202
  7.5 1.5 %collective-permute-start.3 = (f32[32,1024]{1,0:T(8,128)S(1)}, f32[32,1024]{1,0:T(8,128)S(1)}, u32[]{:S(2)}, u32[]{:S(2)}) collective-permute-start(f32[32,1024]{1,0:T(8,128)S(1)} %get-tuple-element.33.refs_0_), channel_id=1, source_target_pairs={{0,16},{16,0},{32,48},{48,32},{64,80},{80,64},{96,112},{112,96},{1... | collective-permute-start | bytes 393224 | tf_op jit(solution)/shard_map/ppermute | solution.py:202
  9.0 1.1 %collective-permute-start.6 = (f32[32,1024]{1,0:T(8,128)S(1)}, f32[32,1024]{1,0:T(8,128)S(1)}, u32[]{:S(2)}, u32[]{:S(2)}) collective-permute-start(f32[32,1024]{1,0:T(8,128)S(1)} %collective-permute-done.2.refs_3_), channel_id=1, source_target_pairs={{0,16},{16,0},{32,48},{48,32},{64,80},{80,64},{96,112},{112,96},{1... | collective-permute-start | bytes 393224 | tf_op jit(solution)/shard_map/ppermute | solution.py:202
  10.1 0.9 %collective-permute-done.refs_1_ = f32[32,1024]{1,0:T(8,128)S(1)} collective-permute-done((f32[32,1024]{1,0:T(8,128)S(1)}, f32[32,1024]{1,0:T(8,128)S(1)}, u32[]{:S(2)}, u32[]{:S(2)}) %collective-permute-start) | collective-permute-done | bytes 131104 | tf_op jit(solution)/shard_map/ppermute | solution.py:202
  11.0 1.4 %collective-permute-start.4 = (f32[32,1024]{1,0:T(8,128)S(1)}, f32[32,1024]{1,0:T(8,128)S(1)}, u32[]{:S(2)}, u32[]{:S(2)}) collective-permute-start(f32[32,1024]{1,0:T(8,128)S(1)} %collective-permute-done.refs_1_), channel_id=1, source_target_pairs={{0,16},{16,0},{32,48},{48,32},{64,80},{80,64},{96,112},{112,96},{1... | collective-permute-start | bytes 393224 | tf_op jit(solution)/shard_map/ppermute | solution.py:202
  12.4 0.7 %constant_dynamic-slice_fusion.1 = (f32[1,1024]{1,0:T(1,128)S(1)}, f32[1,1024]{1,0:T(1,128)S(1)}) fusion(f32[4,1024]{1,0:T(4,128)} %param.10, s32[]{:T(128)S(6)} %select_n.37, f32[4,1024]{1,0:T(4,128)} %param.9), kind=kLoop, calls=%fused_computation.15 | loop fusion | flops 1024 | bytes 16388 | tf_op jit(solution)/shard_map/dynamic_slice | solution.py:246
  13.8 1.4 %block_matrices.1 = f32[272,128]{1,0:T(8,128)S(1)} custom-call(f32[32,1024]{1,0:T(8,128)S(1)} %get-tuple-element.33.refs_0_, f32[32,1024]{1,0:T(8,128)S(1)} %collective-permute-done.refs_1_, f32[32,1024]{1,0:T(8,128)S(1)} %collective-permute-done.1.refs_2_, f32[32,1024]{1,0:T(8,128)S(1)} %collective-permute-done.2.refs_3_, ...), custom_call_target="tpu_custom_call" | custom-call | tf_op jit(solution)/shard_map/block_matrices/pallas_call | solution.py:253
  15.2 6.3 %collective-permute-start.9 = (f32[272,128]{1,0:T(8,128)S(1)}, f32[272,128]{1,0:T(8,128)S(1)}, u32[]{:S(2)}, u32[]{:S(2)}) collective-permute-start(f32[272,128]{1,0:T(8,128)S(1)} %block_matrices.1), channel_id=1, source_target_pairs={{0,2},{1,3},{2,4},{3,5},{4,6},{5,7},{6,8},{7,9},{8,10},{9,11},{10,... | collective-permute-start | bytes 417800 | tf_op jit(solution)/shard_map/ppermute | solution.py:218
  21.5 1.5 %collective-permute-start.8 = (f32[272,128]{1,0:T(8,128)S(1)}, f32[272,128]{1,0:T(8,128)S(1)}, u32[]{:S(2)}, u32[]{:S(2)}) collective-permute-start(f32[272,128]{1,0:T(8,128)S(1)} %block_matrices.1), channel_id=1, source_target_pairs={{0,64},{16,80},{32,96},{48,112},{64,0},{80,16},{96,32},{112,48},{1... | collective-permute-start | bytes 417800 | tf_op jit(solution)/shard_map/ppermute | solution.py:202
  23.1 1.8 %collective-permute-start.7 = (f32[272,128]{1,0:T(8,128)S(1)}, f32[272,128]{1,0:T(8,128)S(1)}, u32[]{:S(2)}, u32[]{:S(2)}) collective-permute-start(f32[272,128]{1,0:T(8,128)S(1)} %block_matrices.1), channel_id=1, source_target_pairs={{0,32},{1,33},{2,34},{3,35},{4,36},{5,37},{6,38},{7,39},{8,40},{9,... | collective-permute-start | bytes 417800 | tf_op jit(solution)/shard_map/ppermute | solution.py:218
  24.9 0.9 %dynamic-slice_reduce_fusion = s32[5]{0:T(128)S(1)} fusion(s32[16,5]{0,1:T(8,128)} %param.12, s32[]{:T(128)S(6)} %select_n.38), kind=kLoop, calls=%fused_computation.11 | loop fusion | bytes 44 | tf_op jit(solution)/shard_map/jit(dynamic_index_in_dim)/dynamic_slice | solution.py:222
  26.1 0.8 %copy.15 = s32[4,5,4]{2,1,0:T(8,128)S(1)} copy(s32[4,5,4]{1,2,0:T(4,128)} %bitcast.25) | data formatting | bytes 640 | tf_op jit(solution)/shard_map/optimization_barrier | solution.py:262
  27.0 1.0 %select_reduce_fusion = f32[4,5,4]{2,1,0:T(8,128)S(1)} fusion(f32[64]{0:T(128)} %param.11, pred[5,4,4]{2,1,0:T(4,128)(4,1)S(1)} %fusion, pred[4,5,4,64]{3,2,1,0:T(4,128)(4,1)S(1)} %iota_compare_fusion), kind=kLoop, calls=%fused_computation.2 | loop fusion | flops 61360 | bytes 5776 | tf_op jit(solution)/shard_map/reduce_sum | solution.py:229
  28.1 0.6 %collective-permute-done.7 = f32[272,128]{1,0:T(8,128)S(1)} collective-permute-done((f32[272,128]{1,0:T(8,128)S(1)}, f32[272,128]{1,0:T(8,128)S(1)}, u32[]{:S(2)}, u32[]{:S(2)}) %collective-permute-start.7) | collective-permute-done | bytes 139296 | tf_op jit(solution)/shard_map/ppermute | solution.py:218
  30.5 2.0 %collective-permute-start.13 = (f32[4,272,128]{2,1,0:T(8,128)S(1)}, f32[4,272,128]{2,1,0:T(8,128)S(1)}, u32[]{:S(2)}, u32[]{:S(2)}) collective-permute-start(f32[4,272,128]{2,1,0:T(8,128)S(1)} %pad_maximum_fusion.same), channel_id=1, source_target_pairs={{0,1},{1,2},{2,3},{3,4},{4,5},{5,6},{6,7},{7,8},{8,9},{9,10},{10,1... | collective-permute-start | bytes 1671176 | tf_op jit(solution)/shard_map/ppermute | solution.py:218
  32.5 1.8 %collective-permute-start.14 = (f32[2,272,128]{2,1,0:T(8,128)S(1)}, f32[2,272,128]{2,1,0:T(8,128)S(1)}, u32[]{:S(2)}, u32[]{:S(2)}) collective-permute-start(f32[2,272,128]{2,1,0:T(8,128)S(1)} %pad_maximum_fusion.1), channel_id=1, source_target_pairs={{0,32},{1,33},{2,34},{3,35},{4,36},{5,37},{6,38},{7,39},{8,40},{9,... | collective-permute-start | bytes 835592 | tf_op jit(solution)/shard_map/ppermute | solution.py:218
  34.8 6.8 %collective-permute-done.15.far_opposite = f32[272,128]{1,0:T(8,128)S(1)} collective-permute-done((f32[272,128]{1,0:T(8,128)S(1)}, f32[272,128]{1,0:T(8,128)S(1)}, u32[]{:S(2)}, u32[]{:S(2)}) %collective-permute-start.15) | collective-permute-done | bytes 139296 | tf_op jit(solution)/shard_map/ppermute | solution.py:202
  41.6 1.0 %combine_points.3 = f32[4,272,128]{2,1,0:T(8,128)S(1)} custom-call(f32[4,20]{1,0:T(4,128)S(1)} %collective-permute-done.12.weight_ref, f32[4,272,128]{2,1,0:T(8,128)S(1)} %pad_maximum_fusion.same, f32[4,272,128]{2,1,0:T(8,128)S(1)} %collective-permute-done.13.beside, f32[272,128]{1,0:T(8,128)S(1)} %collective-permute-done.9.far, ...), custom_call_target="tpu_custom_call" | custom-call | flops 6000000 | bytes 2000000 | tf_op jit(solution)/shard_map/combine_points/pallas_call | solution.py:287
  42.6 2.3 %collective-permute-start.16 = (f32[4,272,128]{2,1,0:T(8,128)S(1)}, f32[4,272,128]{2,1,0:T(8,128)S(1)}, u32[]{:S(2)}, u32[]{:S(2)}) collective-permute-start(f32[4,272,128]{2,1,0:T(8,128)S(1)} %combine_points.3), channel_id=1, source_target_pairs={{0,16},{16,0},{32,48},{48,32},{64,80},{80,64},{96,112},{112,96},{1... | collective-permute-start | bytes 1671176 | tf_op jit(solution)/shard_map/ppermute | solution.py:202
  44.9 1.0 %combine_points.2.mine_ref = f32[4,272,128]{2,1,0:T(8,128)S(1)} custom-call(f32[4,20]{1,0:T(4,128)S(1)} %reshape.38.weight_ref, f32[4,272,128]{2,1,0:T(8,128)S(1)} %pad_maximum_fusion.same, f32[4,272,128]{2,1,0:T(8,128)S(1)} %collective-permute-done.13.beside, f32[272,128]{1,0:T(8,128)S(1)} %collective-permute-done.9.far, ...), custom_call_target="tpu_custom_call" | custom-call | flops 6000000 | bytes 2000000 | tf_op jit(solution)/shard_map/combine_points/pallas_call | solution.py:288
  46.0 0.6 collective-permute-done.16.theirs_ref
  46.5 10.0 %root_and_analysis.1 = f32[4,256,1024]{2,1,0:T(8,128)} custom-call(f32[4,272,128]{2,1,0:T(8,128)S(1)} %combine_points.2.mine_ref, f32[4,272,128]{2,1,0:T(8,128)S(1)} %collective-permute-done.16.theirs_ref, f32[4,256,1024]{2,1,0:T(8,128)} %bitcast.20), custom_call_target="tpu_custom_call" | custom-call | tf_op jit(solution)/shard_map/root_and_analysis/pallas_call | solution.py:290
  (31 shorter events, 3.7 us)
Async XLA Ops:
  0.0 25.8 %copy-start = (s32[16,5,4]{0,2,1:T(4,128)S(1)}, s32[16,5,4]{0,2,1:T(4,128)}, u32[]{:S(2)}) copy-start(s32[16,5,4]{0,2,1:T(4,128)} %param.13) | copy-start | bytes 3844
  1.1 7.8 %collective-permute-start.2 = (f32[32,1024]{1,0:T(8,128)S(1)}, f32[32,1024]{1,0:T(8,128)S(1)}, u32[]{:S(2)}, u32[]{:S(2)}) collective-permute-start(f32[32,1024]{1,0:T(8,128)S(1)} %get-tuple-element.31), channel_id=1, source_target_pairs={{0,64},{16,80},{32,96},{48,112},{64,0},{80,16},{96,32},{112,48},{1... | collective-permute-start | bytes 393224 | tf_op jit(solution)/shard_map/ppermute | solution.py:202
  4.8 6.2 %collective-permute-start = (f32[32,1024]{1,0:T(8,128)S(1)}, f32[32,1024]{1,0:T(8,128)S(1)}, u32[]{:S(2)}, u32[]{:S(2)}) collective-permute-start(f32[32,1024]{1,0:T(8,128)S(1)} %get-tuple-element.32), channel_id=1, source_target_pairs={{0,32},{16,48},{32,64},{48,80},{64,96},{80,112},{96,0},{112,16},{1... | collective-permute-start | bytes 393224 | tf_op jit(solution)/shard_map/ppermute | solution.py:202
  5.1 7.3 %collective-permute-start.1 = (f32[32,1024]{1,0:T(8,128)S(1)}, f32[32,1024]{1,0:T(8,128)S(1)}, u32[]{:S(2)}, u32[]{:S(2)}) collective-permute-start(f32[32,1024]{1,0:T(8,128)S(1)} %get-tuple-element.34), channel_id=1, source_target_pairs={{0,96},{16,112},{32,0},{48,16},{64,32},{80,48},{96,64},{112,80},{1... | collective-permute-start | bytes 393224 | tf_op jit(solution)/shard_map/ppermute | solution.py:202
  7.5 5.7 %collective-permute-start.3 = (f32[32,1024]{1,0:T(8,128)S(1)}, f32[32,1024]{1,0:T(8,128)S(1)}, u32[]{:S(2)}, u32[]{:S(2)}) collective-permute-start(f32[32,1024]{1,0:T(8,128)S(1)} %get-tuple-element.33.refs_0_), channel_id=1, source_target_pairs={{0,16},{16,0},{32,48},{48,32},{64,80},{80,64},{96,112},{112,96},{1... | collective-permute-start | bytes 393224 | tf_op jit(solution)/shard_map/ppermute | solution.py:202
  9.0 4.2 %collective-permute-start.6 = (f32[32,1024]{1,0:T(8,128)S(1)}, f32[32,1024]{1,0:T(8,128)S(1)}, u32[]{:S(2)}, u32[]{:S(2)}) collective-permute-start(f32[32,1024]{1,0:T(8,128)S(1)} %collective-permute-done.2.refs_3_), channel_id=1, source_target_pairs={{0,16},{16,0},{32,48},{48,32},{64,80},{80,64},{96,112},{112,96},{1... | collective-permute-start | bytes 393224 | tf_op jit(solution)/shard_map/ppermute | solution.py:202
  11.0 2.4 %collective-permute-start.4 = (f32[32,1024]{1,0:T(8,128)S(1)}, f32[32,1024]{1,0:T(8,128)S(1)}, u32[]{:S(2)}, u32[]{:S(2)}) collective-permute-start(f32[32,1024]{1,0:T(8,128)S(1)} %collective-permute-done.refs_1_), channel_id=1, source_target_pairs={{0,16},{16,0},{32,48},{48,32},{64,80},{80,64},{96,112},{112,96},{1... | collective-permute-start | bytes 393224 | tf_op jit(solution)/shard_map/ppermute | solution.py:202
  12.4 1.3 %collective-permute-start.5 = (f32[32,1024]{1,0:T(8,128)S(1)}, f32[32,1024]{1,0:T(8,128)S(1)}, u32[]{:S(2)}, u32[]{:S(2)}) collective-permute-start(f32[32,1024]{1,0:T(8,128)S(1)} %collective-permute-done.1.refs_2_), channel_id=1, source_target_pairs={{0,16},{16,0},{32,48},{48,32},{64,80},{80,64},{96,112},{112,96},{1... | collective-permute-start | bytes 393224 | tf_op jit(solution)/shard_map/ppermute | solution.py:202
  15.2 12.9 %collective-permute-start.9 = (f32[272,128]{1,0:T(8,128)S(1)}, f32[272,128]{1,0:T(8,128)S(1)}, u32[]{:S(2)}, u32[]{:S(2)}) collective-permute-start(f32[272,128]{1,0:T(8,128)S(1)} %block_matrices.1), channel_id=1, source_target_pairs={{0,2},{1,3},{2,4},{3,5},{4,6},{5,7},{6,8},{7,9},{8,10},{9,11},{10,... | collective-permute-start | bytes 417800 | tf_op jit(solution)/shard_map/ppermute | solution.py:218
  21.5 6.6 %collective-permute-start.8 = (f32[272,128]{1,0:T(8,128)S(1)}, f32[272,128]{1,0:T(8,128)S(1)}, u32[]{:S(2)}, u32[]{:S(2)}) collective-permute-start(f32[272,128]{1,0:T(8,128)S(1)} %block_matrices.1), channel_id=1, source_target_pairs={{0,64},{16,80},{32,96},{48,112},{64,0},{80,16},{96,32},{112,48},{1... | collective-permute-start | bytes 417800 | tf_op jit(solution)/shard_map/ppermute | solution.py:202
  23.1 5.7 %collective-permute-start.7 = (f32[272,128]{1,0:T(8,128)S(1)}, f32[272,128]{1,0:T(8,128)S(1)}, u32[]{:S(2)}, u32[]{:S(2)}) collective-permute-start(f32[272,128]{1,0:T(8,128)S(1)} %block_matrices.1), channel_id=1, source_target_pairs={{0,32},{1,33},{2,34},{3,35},{4,36},{5,37},{6,38},{7,39},{8,40},{9,... | collective-permute-start | bytes 417800 | tf_op jit(solution)/shard_map/ppermute | solution.py:218
  28.7 1.4 %collective-permute-start.10 = (f32[272,128]{1,0:T(8,128)S(1)}, f32[272,128]{1,0:T(8,128)S(1)}, u32[]{:S(2)}, u32[]{:S(2)}) collective-permute-start(f32[272,128]{1,0:T(8,128)S(1)} %collective-permute-done.7), channel_id=1, source_target_pairs={{0,16},{16,0},{32,48},{48,32},{64,80},{80,64},{96,112},{112,96},{1... | collective-permute-start | bytes 417800 | tf_op jit(solution)/shard_map/ppermute | solution.py:202
  29.1 1.4 %collective-permute-start.11 = (f32[272,128]{1,0:T(8,128)S(1)}, f32[272,128]{1,0:T(8,128)S(1)}, u32[]{:S(2)}, u32[]{:S(2)}) collective-permute-start(f32[272,128]{1,0:T(8,128)S(1)} %collective-permute-done.9.far), channel_id=1, source_target_pairs={{0,16},{16,0},{32,48},{48,32},{64,80},{80,64},{96,112},{112,96},{1... | collective-permute-start | bytes 417800 | tf_op jit(solution)/shard_map/ppermute | solution.py:202
  29.2 1.3 %collective-permute-start.12 = (f32[4,20]{1,0:T(4,128)S(1)}, f32[4,20]{1,0:T(4,128)S(1)}, u32[]{:S(2)}, u32[]{:S(2)}) collective-permute-start(f32[4,20]{1,0:T(4,128)S(1)} %reshape.38.weight_ref), channel_id=1, source_target_pairs={{0,16},{16,0},{32,48},{48,32},{64,80},{80,64},{96,112},{112,96},{1... | collective-permute-start | bytes 968 | tf_op jit(solution)/shard_map/ppermute | solution.py:202
  30.5 11.0 %collective-permute-start.13 = (f32[4,272,128]{2,1,0:T(8,128)S(1)}, f32[4,272,128]{2,1,0:T(8,128)S(1)}, u32[]{:S(2)}, u32[]{:S(2)}) collective-permute-start(f32[4,272,128]{2,1,0:T(8,128)S(1)} %pad_maximum_fusion.same), channel_id=1, source_target_pairs={{0,1},{1,2},{2,3},{3,4},{4,5},{5,6},{6,7},{7,8},{8,9},{9,10},{10,1... | collective-permute-start | bytes 1671176 | tf_op jit(solution)/shard_map/ppermute | solution.py:218
  32.5 9.0 %collective-permute-start.14 = (f32[2,272,128]{2,1,0:T(8,128)S(1)}, f32[2,272,128]{2,1,0:T(8,128)S(1)}, u32[]{:S(2)}, u32[]{:S(2)}) collective-permute-start(f32[2,272,128]{2,1,0:T(8,128)S(1)} %pad_maximum_fusion.1), channel_id=1, source_target_pairs={{0,32},{1,33},{2,34},{3,35},{4,36},{5,37},{6,38},{7,39},{8,40},{9,... | collective-permute-start | bytes 835592 | tf_op jit(solution)/shard_map/ppermute | solution.py:218
  34.3 7.3 %collective-permute-start.15 = (f32[272,128]{1,0:T(8,128)S(1)}, f32[272,128]{1,0:T(8,128)S(1)}, u32[]{:S(2)}, u32[]{:S(2)}) collective-permute-start(f32[272,128]{1,0:T(8,128)S(1)} %collective-permute-done.9.far), channel_id=1, source_target_pairs={{0,64},{16,80},{32,96},{48,112},{64,0},{80,16},{96,32},{112,48},{1... | collective-permute-start | bytes 417800 | tf_op jit(solution)/shard_map/ppermute | solution.py:202
  42.6 3.9 %collective-permute-start.16 = (f32[4,272,128]{2,1,0:T(8,128)S(1)}, f32[4,272,128]{2,1,0:T(8,128)S(1)}, u32[]{:S(2)}, u32[]{:S(2)}) collective-permute-start(f32[4,272,128]{2,1,0:T(8,128)S(1)} %combine_points.3), channel_id=1, source_target_pairs={{0,16},{16,0},{32,48},{48,32},{64,80},{80,64},{96,112},{112,96},{1... | collective-permute-start | bytes 1671176 | tf_op jit(solution)/shard_map/ppermute | solution.py:202

commit v3 on v2

--- a/solution.py
+++ b/solution.py
@@ -7,8 +7,8 @@
 
 F32 = jnp.float32
 BF16 = jnp.bfloat16
-HALF_ROWS = 136
-PACKED_ROWS = 2 * HALF_ROWS
+EXTRA = 256
+PACKED_ROWS = EXTRA + 8
 NT = (((1,), (1,)), ((), ()))
 NN = (((1,), (0,)), ((), ()))
 
@@ -26,48 +26,49 @@
     return one(left[0], right[0]) + (one(left[0], right[1]) + one(left[1], right[0]))
 
 
+def dot3_rows(left, right):
+    rows = left[0].shape[0]
+    both = jnp.dot(jnp.concatenate(left, axis=0), right[0], preferred_element_type=F32)
+    return both[:rows] + (both[rows:] + jnp.dot(left[0], right[1], preferred_element_type=F32))
+
+
 def iota2(shape, axis):
     return lax.broadcasted_iota(jnp.int32, shape, axis)
 
 
 def block_kernel(*refs):
     parts = refs[:8]
-    scaled_ref, out_ref, high_ref, low_ref = refs[8:]
+    scaled_ref, out_ref, high_ref, low_ref, heavy_high_ref, heavy_low_ref = refs[8:]
     place = lax.axis_index("ens")
     chip, core = place // 2, lax.rem(place, 2)
+    inverse = scaled_ref[0:1, :]
     for index, part in enumerate(parts):
         side = core if index < 4 else 1 - core
-        row = pl.multiple_of(side * 128 + lax.rem(chip + (0, 3, 1, 2)[index % 4], 4) * 32, 32)
-        high, low = split2(part[...])
-        high_ref[pl.ds(row, 32), :] = high
-        low_ref[pl.ds(row, 32), :] = low
-    inverse = scaled_ref[0:1, :]
-
-    def rows(start, count):
-        at = pl.ds(start if isinstance(start, int) else pl.multiple_of(start, 64), count)
-        return high_ref[at, :], low_ref[at, :]
-
-    def weighted(pair):
-        return split2((pair[0].astype(F32) + pair[1].astype(F32)) * inverse)
-
+        behind = lax.rem(chip + (0, 3, 1, 2)[index % 4], 4)
+        at = pl.ds(pl.multiple_of(side * 128 + behind * 32, 32), 32)
+        value = part[...]
+        high_ref[at, :], low_ref[at, :] = split2(value)
+        heavy_high_ref[at, :], heavy_low_ref[at, :] = split2(value * inverse)
     pull = split2(jnp.broadcast_to(scaled_ref[1:2, :], (16, scaled_ref.shape[1])))
-    pairs = [rows(0, 128), rows(128, 128)]
-    heavy = [weighted(pair) for pair in pairs]
-    across = dot3(heavy[0], pairs[1], NT)
+    heavy = (
+        jnp.concatenate([heavy_high_ref[...], pull[0]], axis=0),
+        jnp.concatenate([heavy_low_ref[...], pull[1]], axis=0),
+    )
+    product = dot3(heavy, (high_ref[...], low_ref[...]), NT)
     row, col = iota2((64, 128), 0), iota2((64, 128), 1)
     extra_row = iota2((8, 128), 0)
+    extra = jnp.zeros((8, 128), F32)
     for side in range(2):
-        square = dot3(heavy[side], pairs[side], NT)
-        drive = dot3(pull, pairs[side], NT)[0:1]
-        top = square[:64]
-        bottom = pltpu.roll(square[64:], 64, 1)
-        base = side * HALF_ROWS
+        lanes = slice(side * 128, side * 128 + 128)
+        top = product[side * 128 : side * 128 + 64, lanes]
+        bottom = pltpu.roll(product[side * 128 + 64 : side * 128 + 128, lanes], 64, 1)
+        base = side * 128
         out_ref[base : base + 64, :] = jnp.where((col < 64) & (col > row), bottom, top)
-        out_ref[base + 64 : base + 128, :] = across[side * 64 : side * 64 + 64]
+        out_ref[base + 64 : base + 128, :] = product[side * 64 : side * 64 + 64, 128:]
         diagonal = jnp.sum(jnp.where(row == col, bottom, 0.0), axis=0, keepdims=True)
-        out_ref[base + 128 : base + 136, :] = jnp.where(
-            extra_row == 0, diagonal, jnp.where(extra_row == 1, drive, 0.0)
-        )
+        extra = jnp.where(extra_row == 2 * side, diagonal, extra)
+        extra = jnp.where(extra_row == 2 * side + 1, product[256:257, lanes], extra)
+    out_ref[EXTRA:PACKED_ROWS, :] = extra
 
 
 def combine_kernel(weight_ref, same, beside, far, far_near, far_opposite, out_ref):
@@ -87,13 +88,14 @@
     ]
 
     for band in range(5):
-        at = pl.ds(band * 56, 56 if band < 4 else 48)
+        at = pl.ds(band * 56, 56 if band < 4 else 40)
         for pair in range(2):
             totals = [None, None]
             for ref, offset, block in tiles:
                 tile = ref[at, :]
                 for side in range(2):
-                    term = tile * weight_ref[2 * pair + side, offset * 4 + block]
+                    row = (2 * pair + side) * 20 + offset * 4 + block
+                    term = tile * weight_ref[pl.ds(row, 1), :]
                     totals[side] = term if totals[side] is None else totals[side] + term
             for side in range(2):
                 out_ref[2 * pair + side, at, :] = totals[side]
@@ -105,7 +107,7 @@
     top = jnp.where((col < 64) & (col > row), flipped[:64], packed)
     upper = pltpu.roll(packed, 64, 1)
     lower = pltpu.roll(flipped[:64], 64, 1)
-    middle = jnp.broadcast_to(pltpu.roll(diagonal, 64, 1)[0:1], (64, 128))
+    middle = pltpu.roll(jnp.broadcast_to(diagonal, (64, 128)), 64, 1)
     shifted = col - 64
     corner = jnp.where(shifted > row, upper, jnp.where(shifted < row, lower, middle))
     bottom = jnp.where(col < 64, flipped[64:], corner)
@@ -140,28 +142,28 @@
 
     identity = (iota2((256, 256), 0) == iota2((256, 256), 1)).astype(F32)
     every = range(points)
-    start, scale, drives = [], [], []
+    start, scale, drives, squares = [], [], [], []
     for point in every:
         whole = mine_ref[point] + theirs_ref[point]
-        low, high = whole[:HALF_ROWS], whole[HALF_ROWS:]
-        cross = jnp.concatenate([low[64:128], high[64:128]], axis=0)
+        extra = whole[EXTRA:]
+        cross = jnp.concatenate([whole[64:128], whole[192:256]], axis=0)
+        corners = [unpack_square(whole[:64], extra[0:1]), unpack_square(whole[128:192], extra[2:3])]
         gram = jnp.concatenate(
             [
-                jnp.concatenate([unpack_square(low[:64], low[128:136]), cross], axis=1),
-                jnp.concatenate(
-                    [jnp.transpose(cross), unpack_square(high[:64], high[128:136])], axis=1
-                ),
+                jnp.concatenate([corners[0], cross], axis=1),
+                jnp.concatenate([jnp.transpose(cross), corners[1]], axis=1),
             ],
             axis=0,
         )
         system = 255.0 * identity + gram
         inverse_norm = lax.rsqrt(jnp.sum(system * system, axis=(0, 1), keepdims=True))
+        system_pair = split2(system)
+        squares.append(dot3(system_pair, system_pair) * (inverse_norm * inverse_norm))
         start.append(system * inverse_norm)
         scale.append(inverse_norm)
-        drives.append(jnp.concatenate([low[129:130], high[129:130]], axis=1))
-
-    def two_steps(value, pair):
-        squared = [dot3(pair[i], pair[i]) for i in every]
+        drives.append(jnp.concatenate([extra[1:2], extra[3:4]], axis=1))
+
+    def two_steps(value, squared):
         squared_pair = [split2(squared[i]) for i in every]
         rest = [
             split2(1.6875 * identity - 0.5625 * value[i] + 0.0625 * squared[i]) for i in every
@@ -171,25 +173,26 @@
         ]
 
     pair = [split2(start[i]) for i in every]
-    root = two_steps(start, pair)
+    root = two_steps(start, squares)
     root_pair = [split2(root[i]) for i in every]
     value = [dot3(split2(dot3(pair[i], root_pair[i])), root_pair[i]) for i in every]
     pair = [split2(value[i]) for i in every]
-    factor_pair = [split2(f) for f in two_steps(value, pair)]
+    factor_pair = [split2(f) for f in two_steps(value, [dot3(pair[i], pair[i]) for i in every])]
     root_pair = [split2(dot3(factor_pair[i], root_pair[i])) for i in every]
     value = [dot3(split2(dot3(pair[i], factor_pair[i])), factor_pair[i]) for i in every]
     pair = [split2(value[i]) for i in every]
-    factor_pair = [split2(f) for f in two_steps(value, pair)]
+    for point in every:
+        for chunk in chunks():
+            fetch(point, *chunk).wait()
+    factor_pair = [split2(f) for f in two_steps(value, [dot3(pair[i], pair[i]) for i in every])]
     root = [dot3(factor_pair[i], root_pair[i]) for i in every]
     for point in every:
         inner = jnp.sum(root[point] * drives[point], axis=1, keepdims=True)
         mean = jnp.sum(root[point] * inner, axis=0, keepdims=True) * scale[point]
         transform = split2(jnp.sqrt(255.0 * scale[point]) * root[point] + mean)
-        for chunk in chunks():
-            fetch(point, *chunk).wait()
-        for part in range(4):
-            lanes = pl.ds(part * 256, 256)
-            made[point, :, lanes] = dot3(transform, split2(held[point, :, lanes]))
+        for part in range(2):
+            lanes = pl.ds(part * 512, 512)
+            made[point, :, lanes] = dot3_rows(transform, split2(held[point, :, lanes]))
         for chunk in chunks():
             leave(point, *chunk).start()
     for point in every:
@@ -218,9 +221,8 @@
     return lax.ppermute(value, ("ens", "dom"), pairs)
 
 
-def block_weights(loc_table, counts, block_picks, loc_index, tile):
+def block_weights(loc_table, counts, own_picks, loc_index, tile):
     own_counts = lax.dynamic_index_in_dim(counts, tile, 0, keepdims=False)
-    own_picks = lax.dynamic_index_in_dim(block_picks, tile, 0, keepdims=False)
     bins = jnp.arange(loc_table.shape[0], dtype=jnp.int32)
     four = jnp.arange(4, dtype=jnp.int32)
     live = four[None, :] < own_counts[:, None]
@@ -238,24 +240,23 @@
     chip = place // 2
     vmem = pl.BlockSpec(memory_space=pltpu.VMEM)
 
-    def block_of(steps):
-        return lax.dynamic_index_in_dim(
-            obs_members, lax.rem(chip + steps, 4), 0, keepdims=False
-        )
+    def block_of(blocks, steps):
+        return lax.dynamic_index_in_dim(blocks, lax.rem(chip + steps, 4), 0, keepdims=False)
 
     inverse = lax.dynamic_slice_in_dim(error_inverse, chip, 1, 0)
     pull = inverse * lax.dynamic_slice_in_dim(innovations, chip, 1, 0)
     scaled = jnp.concatenate([inverse, pull], axis=0)
     order = (1, 3, 2)
-    sent = dict(zip(order, [along_x(block_of(steps), steps) for steps in order]))
-    parts = [block_of(0)] + [sent[steps] for steps in order]
+    sent = [block_of(obs_members, steps) for steps in order]
+    *sent, obs_members = lax.optimization_barrier((*sent, obs_members))
+    parts = [block_of(obs_members, 0)] + [along_x(part, steps) for part, steps in zip(sent, order)]
     parts = parts + [other_core(part) for part in parts]
     whole = pl.pallas_call(
         block_kernel,
         out_shape=jax.ShapeDtypeStruct((PACKED_ROWS, 128), F32),
         in_specs=[vmem] * 9,
         out_specs=vmem,
-        scratch_shapes=[pltpu.VMEM((256, 1024), BF16), pltpu.VMEM((256, 1024), BF16)],
+        scratch_shapes=[pltpu.VMEM((256, 1024), BF16)] * 4,
         compiler_params=pltpu.CompilerParams(vmem_limit_bytes=16 << 20),
         name="block_matrices",
     )(*parts, scaled)
@@ -264,12 +265,18 @@
     )
     far = both_ways(whole, "dom", 2)
     near = both_ways(whole, "ens", 1)
-    opposite = along_x(whole, 2)
-    weight = block_weights(loc_table, counts, block_picks, local_index, tile)
-    near, opposite, far, weight = lax.optimization_barrier((near, opposite, far, weight))
-    same = jnp.stack([whole, near, other_core(near), opposite])
-    far_both = jnp.stack([far, other_core(far)])
-    weights = (weight, other_core(weight))
+    own_picks = lax.dynamic_index_in_dim(block_picks, tile, 0, keepdims=False)
+    later, own_picks = lax.optimization_barrier((whole, own_picks))
+    opposite = along_x(later, 2)
+    weight = block_weights(loc_table, counts, own_picks, local_index, tile)
+    near, far = lax.optimization_barrier((near, far))
+    near_swapped, far_swapped = other_core(near), other_core(far)
+    weights = [
+        jnp.broadcast_to(part.reshape(-1, 1), (part.size, 128))
+        for part in (weight, other_core(weight))
+    ]
+    same = jnp.stack([whole, near, near_swapped, opposite])
+    far_both = jnp.stack([far, far_swapped])
     same, far, far_both, weights = lax.optimization_barrier((same, far, far_both, weights))
     far_opposite = along_x(far, 2)
     far_near = both_ways(far_both, "ens", 1)
@@ -277,7 +284,7 @@
     combine = pl.pallas_call(
         combine_kernel,
         out_shape=jax.ShapeDtypeStruct((4, PACKED_ROWS, 128), F32),
-        in_specs=[pl.BlockSpec(memory_space=pltpu.SMEM)] + [vmem] * 5,
+        in_specs=[vmem] * 6,
         out_specs=vmem,
         compiler_params=pltpu.CompilerParams(vmem_limit_bytes=16 << 20),
         cost_estimate=pl.CostEstimate(flops=6000000, bytes_accessed=2000000, transcendentals=0),

time: 57.1 us -> 54.5 us (0.954)
  starting transfers between devices: 27.5 us -> 24.6 us
  Pallas kernels: 13.5 us -> 11.3 us
  waiting for transfers between devices: 10.3 us -> 11.5 us
  local copies, waits for them, and re-layouts: 3.18 us -> 4.34 us
    ppermute x13, starting transfers between devices: 15.5 us -> 13.3 us  [along_x(): return lax.ppermute(value, 'ens', pairs)]
    ppermute x13, waiting for transfers between devices: 9.7 us -> 11.5 us  [along_x(): return lax.ppermute(value, 'ens', pairs)]
    squeeze x1 -> x2, local copies, waits for them, and re-layouts: 1.14 us -> 1.98 us  [block_of(): lax.dynamic_index_in_dim(blocks, lax.rem(chip + steps, 4), 0, keepdims=Fa...]
    pallas_call x1, Pallas kernels: 1.03 us -> 0.39 us  [local(): mine = combine(weights[0], *sources)]
    ppermute x4, starting transfers between devices: 11.9 us -> 11.3 us  [both_ways(): return lax.ppermute(value, ('ens', 'dom'), pairs)]
    pallas_call x1, Pallas kernels: 1.03 us -> 0.41 us  [local(): theirs = other_core(combine(weights[1], *sources))]
    pallas_call x1, Pallas kernels: 10 us -> 9.41 us  [local(): pl.pallas_call(analysis_kernel, out_shape=jax.ShapeDtypeStruct((points, m...]
    ppermute x4, waiting for transfers between devices: 0.6 us -> 0.01 us  [both_ways(): return lax.ppermute(value, ('ens', 'dom'), pairs)]
  transfers between devices with their start and end apart: 17 -> 17, of which waited for: 8 -> 6; matrix products, arithmetic and copies ran while one was open for 7% -> 9% of each run, Pallas kernels for 2% -> 1%
where the time goes in v3:
time: 54.5 us; the launch traced here: 54.1 us
  starting transfers between devices  24.6 us (45%)
  waiting for transfers between devices  11.5 us (21%)
  Pallas kernels  11.3 us (21%)
  local copies, waits for them, and re-layouts  4.34 us (8%)
  other arithmetic  1.98 us (4%)
    ppermute x13, starting transfers between devices, along_x(): return lax.ppermute(value, 'ens', pairs)  13.3 us
    ppermute x13, waiting for transfers between devices, along_x(): return lax.ppermute(value, 'ens', pairs)  11.5 us
    ppermute x4, starting transfers between devices, both_ways(): return lax.ppermute(value, ('ens', 'dom'), pairs)  11.3 us
    pallas_call x1, Pallas kernels, local(): pl.pallas_call(analysis_kernel, out_shape=jax.ShapeDtypeStruct((points, m...  9.41 us
    squeeze x2, local copies, waits for them, and re-layouts, block_of(): lax.dynamic_index_in_dim(blocks, lax.rem(chip + steps, 4), 0, keepdims=Fa...  1.98 us
    pallas_call x1, Pallas kernels, local(): pl.pallas_call(block_kernel, out_shape=jax.ShapeDtypeStruct((PACKED_ROWS,...  1.09 us
  transfers between devices with their start and end apart: 17, of which 6 were waited for; matrix products, arithmetic and copies ran while one was open for 9% of the time, Pallas kernels for 1%

profile of v3, /device:TPU:1, one launch (start us, length us, event | category | flops | bytes accessed | tf_op | source)
XLA Modules:
  0.0 54.1 jit_solution(3705216230821744662)
XLA Ops:
  0.0 1.1 %dynamic-slice_bitcast_fusion.1 = (f32[32,1024]{1,0:T(8,128)S(1)}, f32[32,1024]{1,0:T(8,128)S(1)}, f32[32,1024]{1,0:T(8,128)S(1)}) fusion(f32[4,32,1024]{2,1,0:T(8,128)} %param.8, s32[]{:T(128)S(6)} %select_n.35, s32[]{:T(128)S(6)} %select_n.34, s32[]{:T(128)S(6)} %select_n.33), kind=kLoop, calls=%fused_computation.4 | loop fusion | bytes 786444 | tf_op jit(solution)/shard_map/jit(dynamic_index_in_dim)/squeeze | solution.py:244
  1.1 2.1 %collective-permute-start = (f32[32,1024]{1,0:T(8,128)S(1)}, f32[32,1024]{1,0:T(8,128)S(1)}, u32[]{:S(2)}, u32[]{:S(2)}) collective-permute-start(f32[32,1024]{1,0:T(8,128)S(1)} %get-tuple-element.23), channel_id=1, source_target_pairs={{0,32},{16,48},{32,64},{48,80},{64,96},{80,112},{96,0},{112,16},{1... | collective-permute-start | bytes 393224 | tf_op jit(solution)/shard_map/ppermute | solution.py:205
  3.2 1.3 %collective-permute-start.1 = (f32[32,1024]{1,0:T(8,128)S(1)}, f32[32,1024]{1,0:T(8,128)S(1)}, u32[]{:S(2)}, u32[]{:S(2)}) collective-permute-start(f32[32,1024]{1,0:T(8,128)S(1)} %get-tuple-element.24), channel_id=1, source_target_pairs={{0,96},{16,112},{32,0},{48,16},{64,32},{80,48},{96,64},{112,80},{1... | collective-permute-start | bytes 393224 | tf_op jit(solution)/shard_map/ppermute | solution.py:205
  4.5 1.6 %collective-permute-start.2 = (f32[32,1024]{1,0:T(8,128)S(1)}, f32[32,1024]{1,0:T(8,128)S(1)}, u32[]{:S(2)}, u32[]{:S(2)}) collective-permute-start(f32[32,1024]{1,0:T(8,128)S(1)} %get-tuple-element.25), channel_id=1, source_target_pairs={{0,64},{16,80},{32,96},{48,112},{64,0},{80,16},{96,32},{112,48},{1... | collective-permute-start | bytes 393224 | tf_op jit(solution)/shard_map/ppermute | solution.py:205
  6.2 0.9 %dynamic-slice_bitcast_fusion.refs_0_ = f32[32,1024]{1,0:T(8,128)S(1)} fusion(f32[4,32,1024]{2,1,0:T(8,128)} %param.8, s32[]{:T(128)S(6)} %select_n.36), kind=kLoop, calls=%fused_computation.3 | loop fusion | bytes 262148 | tf_op jit(solution)/shard_map/jit(dynamic_index_in_dim)/squeeze | solution.py:244
  7.1 1.6 %collective-permute-start.3 = (f32[32,1024]{1,0:T(8,128)S(1)}, f32[32,1024]{1,0:T(8,128)S(1)}, u32[]{:S(2)}, u32[]{:S(2)}) collective-permute-start(f32[32,1024]{1,0:T(8,128)S(1)} %dynamic-slice_bitcast_fusion.refs_0_), channel_id=1, source_target_pairs={{0,16},{16,0},{32,48},{48,32},{64,80},{80,64},{96,112},{112,96},{1... | collective-permute-start | bytes 393224 | tf_op jit(solution)/shard_map/ppermute | solution.py:205
  8.9 1.3 %collective-permute-start.5 = (f32[32,1024]{1,0:T(8,128)S(1)}, f32[32,1024]{1,0:T(8,128)S(1)}, u32[]{:S(2)}, u32[]{:S(2)}) collective-permute-start(f32[32,1024]{1,0:T(8,128)S(1)} %collective-permute-done.1.refs_2_), channel_id=1, source_target_pairs={{0,16},{16,0},{32,48},{48,32},{64,80},{80,64},{96,112},{112,96},{1... | collective-permute-start | bytes 393224 | tf_op jit(solution)/shard_map/ppermute | solution.py:205
  10.2 1.4 %collective-permute-done.2.refs_3_ = f32[32,1024]{1,0:T(8,128)S(1)} collective-permute-done((f32[32,1024]{1,0:T(8,128)S(1)}, f32[32,1024]{1,0:T(8,128)S(1)}, u32[]{:S(2)}, u32[]{:S(2)}) %collective-permute-start.2) | collective-permute-done | bytes 131104 | tf_op jit(solution)/shard_map/ppermute | solution.py:205
  11.5 1.4 %collective-permute-start.6 = (f32[32,1024]{1,0:T(8,128)S(1)}, f32[32,1024]{1,0:T(8,128)S(1)}, u32[]{:S(2)}, u32[]{:S(2)}) collective-permute-start(f32[32,1024]{1,0:T(8,128)S(1)} %collective-permute-done.2.refs_3_), channel_id=1, source_target_pairs={{0,16},{16,0},{32,48},{48,32},{64,80},{80,64},{96,112},{112,96},{1... | collective-permute-start | bytes 393224 | tf_op jit(solution)/shard_map/ppermute | solution.py:205
  13.9 1.1 %block_matrices.1 = f32[264,128]{1,0:T(8,128)S(1)} custom-call(f32[32,1024]{1,0:T(8,128)S(1)} %dynamic-slice_bitcast_fusion.refs_0_, f32[32,1024]{1,0:T(8,128)S(1)} %collective-permute-done.refs_1_, f32[32,1024]{1,0:T(8,128)S(1)} %collective-permute-done.1.refs_2_, f32[32,1024]{1,0:T(8,128)S(1)} %collective-permute-done.2.refs_3_, ...), custom_call_target="tpu_custom_call" | custom-call | tf_op jit(solution)/shard_map/block_matrices/pallas_call | solution.py:254
  15.0 6.1 %collective-permute-start.8 = (f32[264,128]{1,0:T(8,128)S(1)}, f32[264,128]{1,0:T(8,128)S(1)}, u32[]{:S(2)}, u32[]{:S(2)}) collective-permute-start(f32[264,128]{1,0:T(8,128)S(1)} %block_matrices.1), channel_id=1, source_target_pairs={{0,2},{1,3},{2,4},{3,5},{4,6},{5,7},{6,8},{7,9},{8,10},{9,11},{10,... | collective-permute-start | bytes 405512 | tf_op jit(solution)/shard_map/ppermute | solution.py:221
  21.1 2.1 %collective-permute-start.7 = (f32[264,128]{1,0:T(8,128)S(1)}, f32[264,128]{1,0:T(8,128)S(1)}, u32[]{:S(2)}, u32[]{:S(2)}) collective-permute-start(f32[264,128]{1,0:T(8,128)S(1)} %block_matrices.1), channel_id=1, source_target_pairs={{0,32},{1,33},{2,34},{3,35},{4,36},{5,37},{6,38},{7,39},{8,40},{9,... | collective-permute-start | bytes 405512 | tf_op jit(solution)/shard_map/ppermute | solution.py:221
  23.2 0.9 %dynamic-slice_reduce_fusion = s32[5]{0:T(128)S(1)} fusion(s32[16,5]{0,1:T(8,128)} %param.12, s32[]{:T(128)S(6)} %select_n.38), kind=kLoop, calls=%fused_computation.11 | loop fusion | bytes 44 | tf_op jit(solution)/shard_map/jit(dynamic_index_in_dim)/dynamic_slice | solution.py:225
  24.3 0.8 %copy.16 = s32[4,5,4]{2,1,0:T(8,128)S(1)} copy(s32[4,5,4]{1,2,0:T(4,128)} %bitcast.25) | data formatting | bytes 640 | tf_op jit(solution)/shard_map/optimization_barrier | solution.py:263
  26.6 1.0 %select_reduce_fusion = f32[4,5,4]{2,1,0:T(8,128)S(1)} fusion(f32[64]{0:T(128)} %param.11, pred[5,4,4]{2,1,0:T(4,128)(4,1)S(1)} %fusion, pred[4,5,4,64]{3,2,1,0:T(4,128)(4,1)S(1)} %iota_compare_fusion), kind=kLoop, calls=%fused_computation.2 | loop fusion | flops 61360 | bytes 5776 | tf_op jit(solution)/shard_map/reduce_sum | solution.py:231
  27.8 1.0 %collective-permute-done.12 = f32[4,20]{1,0:T(4,128)S(1)} collective-permute-done((f32[4,20]{1,0:T(4,128)S(1)}, f32[4,20]{1,0:T(4,128)S(1)}, u32[]{:S(2)}, u32[]{:S(2)}) %collective-permute-start.12) | collective-permute-done | bytes 352 | tf_op jit(solution)/shard_map/ppermute | solution.py:205
  29.0 1.7 %collective-permute-done.10 = f32[264,128]{1,0:T(8,128)S(1)} collective-permute-done((f32[264,128]{1,0:T(8,128)S(1)}, f32[264,128]{1,0:T(8,128)S(1)}, u32[]{:S(2)}, u32[]{:S(2)}) %collective-permute-start.10) | collective-permute-done | bytes 135200 | tf_op jit(solution)/shard_map/ppermute | solution.py:205
  30.9 1.9 %collective-permute-start.13 = (f32[4,264,128]{2,1,0:T(8,128)S(1)}, f32[4,264,128]{2,1,0:T(8,128)S(1)}, u32[]{:S(2)}, u32[]{:S(2)}) collective-permute-start(f32[4,264,128]{2,1,0:T(8,128)S(1)} %pad_maximum_fusion.same), channel_id=1, source_target_pairs={{0,1},{1,2},{2,3},{3,4},{4,5},{5,6},{6,7},{7,8},{8,9},{9,10},{10,1... | collective-permute-start | bytes 1622024 | tf_op jit(solution)/shard_map/ppermute | solution.py:221
  32.7 1.2 %collective-permute-start.14 = (f32[2,264,128]{2,1,0:T(8,128)S(1)}, f32[2,264,128]{2,1,0:T(8,128)S(1)}, u32[]{:S(2)}, u32[]{:S(2)}) collective-permute-start(f32[2,264,128]{2,1,0:T(8,128)S(1)} %pad_maximum_fusion.1), channel_id=1, source_target_pairs={{0,32},{1,33},{2,34},{3,35},{4,36},{5,37},{6,38},{7,39},{8,40},{9,... | collective-permute-start | bytes 811016 | tf_op jit(solution)/shard_map/ppermute | solution.py:221
  34.0 1.1 %collective-permute-start.15 = (f32[264,128]{1,0:T(8,128)S(1)}, f32[264,128]{1,0:T(8,128)S(1)}, u32[]{:S(2)}, u32[]{:S(2)}) collective-permute-start(f32[264,128]{1,0:T(8,128)S(1)} %collective-permute-done.8.far), channel_id=1, source_target_pairs={{0,64},{16,80},{32,96},{48,112},{64,0},{80,16},{96,32},{112,48},{1... | collective-permute-start | bytes 405512 | tf_op jit(solution)/shard_map/ppermute | solution.py:205
  35.1 6.1 %collective-permute-done.15.far_opposite = f32[264,128]{1,0:T(8,128)S(1)} collective-permute-done((f32[264,128]{1,0:T(8,128)S(1)}, f32[264,128]{1,0:T(8,128)S(1)}, u32[]{:S(2)}, u32[]{:S(2)}) %collective-permute-start.15) | collective-permute-done | bytes 135200 | tf_op jit(solution)/shard_map/ppermute | solution.py:205
  41.6 1.4 %collective-permute-start.16 = (f32[4,264,128]{2,1,0:T(8,128)S(1)}, f32[4,264,128]{2,1,0:T(8,128)S(1)}, u32[]{:S(2)}, u32[]{:S(2)}) collective-permute-start(f32[4,264,128]{2,1,0:T(8,128)S(1)} %combine_points.3), channel_id=1, source_target_pairs={{0,16},{16,0},{32,48},{48,32},{64,80},{80,64},{96,112},{112,96},{1... | collective-permute-start | bytes 1622024 | tf_op jit(solution)/shard_map/ppermute | solution.py:205
  43.3 1.2 %collective-permute-done.16.theirs_ref = f32[4,264,128]{2,1,0:T(8,128)S(1)} collective-permute-done((f32[4,264,128]{2,1,0:T(8,128)S(1)}, f32[4,264,128]{2,1,0:T(8,128)S(1)}, u32[]{:S(2)}, u32[]{:S(2)}) %collective-permute-start.16) | collective-permute-done | bytes 540704 | tf_op jit(solution)/shard_map/ppermute | solution.py:205
  44.5 9.4 %root_and_analysis.1 = f32[4,256,1024]{2,1,0:T(8,128)} custom-call(f32[4,264,128]{2,1,0:T(8,128)S(1)} %combine_points.2.mine_ref, f32[4,264,128]{2,1,0:T(8,128)S(1)} %collective-permute-done.16.theirs_ref, f32[4,256,1024]{2,1,0:T(8,128)} %bitcast.20), custom_call_target="tpu_custom_call" | custom-call | tf_op jit(solution)/shard_map/root_and_analysis/pallas_call | solution.py:297
  (36 shorter events, 4.3 us)
Async XLA Ops:
  0.0 24.0 %copy-start = (s32[16,5,4]{0,2,1:T(4,128)S(1)}, s32[16,5,4]{0,2,1:T(4,128)}, u32[]{:S(2)}) copy-start(s32[16,5,4]{0,2,1:T(4,128)} %param.13) | copy-start | bytes 3844
  1.1 7.6 %collective-permute-start = (f32[32,1024]{1,0:T(8,128)S(1)}, f32[32,1024]{1,0:T(8,128)S(1)}, u32[]{:S(2)}, u32[]{:S(2)}) collective-permute-start(f32[32,1024]{1,0:T(8,128)S(1)} %get-tuple-element.23), channel_id=1, source_target_pairs={{0,32},{16,48},{32,64},{48,80},{64,96},{80,112},{96,0},{112,16},{1... | collective-permute-start | bytes 393224 | tf_op jit(solution)/shard_map/ppermute | solution.py:205
  3.2 5.7 %collective-permute-start.1 = (f32[32,1024]{1,0:T(8,128)S(1)}, f32[32,1024]{1,0:T(8,128)S(1)}, u32[]{:S(2)}, u32[]{:S(2)}) collective-permute-start(f32[32,1024]{1,0:T(8,128)S(1)} %get-tuple-element.24), channel_id=1, source_target_pairs={{0,96},{16,112},{32,0},{48,16},{64,32},{80,48},{96,64},{112,80},{1... | collective-permute-start | bytes 393224 | tf_op jit(solution)/shard_map/ppermute | solution.py:205
  4.5 7.0 %collective-permute-start.2 = (f32[32,1024]{1,0:T(8,128)S(1)}, f32[32,1024]{1,0:T(8,128)S(1)}, u32[]{:S(2)}, u32[]{:S(2)}) collective-permute-start(f32[32,1024]{1,0:T(8,128)S(1)} %get-tuple-element.25), channel_id=1, source_target_pairs={{0,64},{16,80},{32,96},{48,112},{64,0},{80,16},{96,32},{112,48},{1... | collective-permute-start | bytes 393224 | tf_op jit(solution)/shard_map/ppermute | solution.py:205
  7.1 6.6 %collective-permute-start.3 = (f32[32,1024]{1,0:T(8,128)S(1)}, f32[32,1024]{1,0:T(8,128)S(1)}, u32[]{:S(2)}, u32[]{:S(2)}) collective-permute-start(f32[32,1024]{1,0:T(8,128)S(1)} %dynamic-slice_bitcast_fusion.refs_0_), channel_id=1, source_target_pairs={{0,16},{16,0},{32,48},{48,32},{64,80},{80,64},{96,112},{112,96},{1... | collective-permute-start | bytes 393224 | tf_op jit(solution)/shard_map/ppermute | solution.py:205
  8.7 5.0 %collective-permute-start.4 = (f32[32,1024]{1,0:T(8,128)S(1)}, f32[32,1024]{1,0:T(8,128)S(1)}, u32[]{:S(2)}, u32[]{:S(2)}) collective-permute-start(f32[32,1024]{1,0:T(8,128)S(1)} %collective-permute-done.refs_1_), channel_id=1, source_target_pairs={{0,16},{16,0},{32,48},{48,32},{64,80},{80,64},{96,112},{112,96},{1... | collective-permute-start | bytes 393224 | tf_op jit(solution)/shard_map/ppermute | solution.py:205
  8.9 4.8 %collective-permute-start.5 = (f32[32,1024]{1,0:T(8,128)S(1)}, f32[32,1024]{1,0:T(8,128)S(1)}, u32[]{:S(2)}, u32[]{:S(2)}) collective-permute-start(f32[32,1024]{1,0:T(8,128)S(1)} %collective-permute-done.1.refs_2_), channel_id=1, source_target_pairs={{0,16},{16,0},{32,48},{48,32},{64,80},{80,64},{96,112},{112,96},{1... | collective-permute-start | bytes 393224 | tf_op jit(solution)/shard_map/ppermute | solution.py:205
  11.5 2.4 %collective-permute-start.6 = (f32[32,1024]{1,0:T(8,128)S(1)}, f32[32,1024]{1,0:T(8,128)S(1)}, u32[]{:S(2)}, u32[]{:S(2)}) collective-permute-start(f32[32,1024]{1,0:T(8,128)S(1)} %collective-permute-done.2.refs_3_), channel_id=1, source_target_pairs={{0,16},{16,0},{32,48},{48,32},{64,80},{80,64},{96,112},{112,96},{1... | collective-permute-start | bytes 393224 | tf_op jit(solution)/shard_map/ppermute | solution.py:205
  15.0 11.0 %collective-permute-start.8 = (f32[264,128]{1,0:T(8,128)S(1)}, f32[264,128]{1,0:T(8,128)S(1)}, u32[]{:S(2)}, u32[]{:S(2)}) collective-permute-start(f32[264,128]{1,0:T(8,128)S(1)} %block_matrices.1), channel_id=1, source_target_pairs={{0,2},{1,3},{2,4},{3,5},{4,6},{5,7},{6,8},{7,9},{8,10},{9,11},{10,... | collective-permute-start | bytes 405512 | tf_op jit(solution)/shard_map/ppermute | solution.py:221
  21.1 4.9 %collective-permute-start.7 = (f32[264,128]{1,0:T(8,128)S(1)}, f32[264,128]{1,0:T(8,128)S(1)}, u32[]{:S(2)}, u32[]{:S(2)}) collective-permute-start(f32[264,128]{1,0:T(8,128)S(1)} %block_matrices.1), channel_id=1, source_target_pairs={{0,32},{1,33},{2,34},{3,35},{4,36},{5,37},{6,38},{7,39},{8,40},{9,... | collective-permute-start | bytes 405512 | tf_op jit(solution)/shard_map/ppermute | solution.py:221
  25.2 5.4 %collective-permute-start.10 = (f32[264,128]{1,0:T(8,128)S(1)}, f32[264,128]{1,0:T(8,128)S(1)}, u32[]{:S(2)}, u32[]{:S(2)}) collective-permute-start(f32[264,128]{1,0:T(8,128)S(1)} %block_matrices.1), channel_id=1, source_target_pairs={{0,64},{16,80},{32,96},{48,112},{64,0},{80,16},{96,32},{112,48},{1... | collective-permute-start | bytes 405512 | tf_op jit(solution)/shard_map/ppermute | solution.py:205
  26.0 3.0 %collective-permute-start.11 = (f32[264,128]{1,0:T(8,128)S(1)}, f32[264,128]{1,0:T(8,128)S(1)}, u32[]{:S(2)}, u32[]{:S(2)}) collective-permute-start(f32[264,128]{1,0:T(8,128)S(1)} %collective-permute-done.8.far), channel_id=1, source_target_pairs={{0,16},{16,0},{32,48},{48,32},{64,80},{80,64},{96,112},{112,96},{1... | collective-permute-start | bytes 405512 | tf_op jit(solution)/shard_map/ppermute | solution.py:205
  26.1 4.6 %collective-permute-start.9 = (f32[264,128]{1,0:T(8,128)S(1)}, f32[264,128]{1,0:T(8,128)S(1)}, u32[]{:S(2)}, u32[]{:S(2)}) collective-permute-start(f32[264,128]{1,0:T(8,128)S(1)} %collective-permute-done.7), channel_id=1, source_target_pairs={{0,16},{16,0},{32,48},{48,32},{64,80},{80,64},{96,112},{112,96},{1... | collective-permute-start | bytes 405512 | tf_op jit(solution)/shard_map/ppermute | solution.py:205
  27.7 1.2 %collective-permute-start.12 = (f32[4,20]{1,0:T(4,128)S(1)}, f32[4,20]{1,0:T(4,128)S(1)}, u32[]{:S(2)}, u32[]{:S(2)}) collective-permute-start(f32[4,20]{1,0:T(4,128)S(1)} %reshape.40), channel_id=1, source_target_pairs={{0,16},{16,0},{32,48},{48,32},{64,80},{80,64},{96,112},{112,96},{1... | collective-permute-start | bytes 968 | tf_op jit(solution)/shard_map/ppermute | solution.py:205
  30.9 10.3 %collective-permute-start.13 = (f32[4,264,128]{2,1,0:T(8,128)S(1)}, f32[4,264,128]{2,1,0:T(8,128)S(1)}, u32[]{:S(2)}, u32[]{:S(2)}) collective-permute-start(f32[4,264,128]{2,1,0:T(8,128)S(1)} %pad_maximum_fusion.same), channel_id=1, source_target_pairs={{0,1},{1,2},{2,3},{3,4},{4,5},{5,6},{6,7},{7,8},{8,9},{9,10},{10,1... | collective-permute-start | bytes 1622024 | tf_op jit(solution)/shard_map/ppermute | solution.py:221
  32.7 8.4 %collective-permute-start.14 = (f32[2,264,128]{2,1,0:T(8,128)S(1)}, f32[2,264,128]{2,1,0:T(8,128)S(1)}, u32[]{:S(2)}, u32[]{:S(2)}) collective-permute-start(f32[2,264,128]{2,1,0:T(8,128)S(1)} %pad_maximum_fusion.1), channel_id=1, source_target_pairs={{0,32},{1,33},{2,34},{3,35},{4,36},{5,37},{6,38},{7,39},{8,40},{9,... | collective-permute-start | bytes 811016 | tf_op jit(solution)/shard_map/ppermute | solution.py:221
  34.0 7.2 %collective-permute-start.15 = (f32[264,128]{1,0:T(8,128)S(1)}, f32[264,128]{1,0:T(8,128)S(1)}, u32[]{:S(2)}, u32[]{:S(2)}) collective-permute-start(f32[264,128]{1,0:T(8,128)S(1)} %collective-permute-done.8.far), channel_id=1, source_target_pairs={{0,64},{16,80},{32,96},{48,112},{64,0},{80,16},{96,32},{112,48},{1... | collective-permute-start | bytes 405512 | tf_op jit(solution)/shard_map/ppermute | solution.py:205
  41.6 2.9 %collective-permute-start.16 = (f32[4,264,128]{2,1,0:T(8,128)S(1)}, f32[4,264,128]{2,1,0:T(8,128)S(1)}, u32[]{:S(2)}, u32[]{:S(2)}) collective-permute-start(f32[4,264,128]{2,1,0:T(8,128)S(1)} %combine_points.3), channel_id=1, source_target_pairs={{0,16},{16,0},{32,48},{48,32},{64,80},{80,64},{96,112},{112,96},{1... | collective-permute-start | bytes 1622024 | tf_op jit(solution)/shard_map/ppermute | solution.py:205

commit v4 on v3

--- a/solution.py
+++ b/solution.py
@@ -71,26 +71,11 @@
     out_ref[EXTRA:PACKED_ROWS, :] = extra
 
 
-def combine_kernel(weight_ref, same, beside, far, far_near, far_opposite, out_ref):
-    place = lax.axis_index("ens")
-    chip, core = place // 2, lax.rem(place, 2)
-    ahead = lax.rem(chip + 2, 4)
-    near = lax.rem(chip + 3 - 2 * core, 4)
-    swapped = lax.rem(chip + 1 + 2 * core, 4)
-    tiles = [
-        *[(beside.at[i], 1 + 2 * core, b) for i, b in enumerate((chip, near, swapped, ahead))],
-        (far, 4 * core, chip),
-        (far_near.at[0], 4 * core, near),
-        (far_near.at[1], 4 - 4 * core, near),
-        (far_opposite, 4 * core, ahead),
-        (same.at[1], 2, near),
-        (same.at[3 * core], 2, lax.rem(chip + 2 * core, 4)),
-    ]
-
+def add_tiles(weight_ref, tiles, start_ref, out_ref):
     for band in range(5):
         at = pl.ds(band * 56, 56 if band < 4 else 40)
         for pair in range(2):
-            totals = [None, None]
+            totals = [None if start_ref is None else start_ref[2 * pair + side, at, :] for side in range(2)]
             for ref, offset, block in tiles:
                 tile = ref[at, :]
                 for side in range(2):
@@ -99,6 +84,35 @@
                     totals[side] = term if totals[side] is None else totals[side] + term
             for side in range(2):
                 out_ref[2 * pair + side, at, :] = totals[side]
+
+
+def places():
+    place = lax.axis_index("ens")
+    chip, core = place // 2, lax.rem(place, 2)
+    near = lax.rem(chip + 3 - 2 * core, 4)
+    swapped = lax.rem(chip + 1 + 2 * core, 4)
+    return core, chip, near, swapped, lax.rem(chip + 2, 4)
+
+
+def early_kernel(weight_ref, same, far, far_opposite, out_ref):
+    core, chip, near, _, ahead = places()
+    tiles = [
+        (same.at[1], 2, near),
+        (same.at[3 * core], 2, lax.rem(chip + 2 * core, 4)),
+        (far, 4 * core, chip),
+        (far_opposite, 4 * core, ahead),
+    ]
+    add_tiles(weight_ref, tiles, None, out_ref)
+
+
+def late_kernel(weight_ref, start_ref, beside, far_near, out_ref):
+    core, chip, near, swapped, ahead = places()
+    tiles = [
+        *[(beside.at[i], 1 + 2 * core, b) for i, b in enumerate((chip, near, swapped, ahead))],
+        (far_near.at[0], 4 * core, near),
+        (far_near.at[1], 4 - 4 * core, near),
+    ]
+    add_tiles(weight_ref, tiles, start_ref, out_ref)
 
 
 def unpack_square(packed, diagonal):
@@ -247,10 +261,15 @@
     pull = inverse * lax.dynamic_slice_in_dim(innovations, chip, 1, 0)
     scaled = jnp.concatenate([inverse, pull], axis=0)
     order = (1, 3, 2)
-    sent = [block_of(obs_members, steps) for steps in order]
-    *sent, obs_members = lax.optimization_barrier((*sent, obs_members))
-    parts = [block_of(obs_members, 0)] + [along_x(part, steps) for part, steps in zip(sent, order)]
+    own, *sent = [block_of(obs_members, steps) for steps in (0, *order)]
+    own, *sent, loc_index, counts, block_picks = lax.optimization_barrier(
+        (own, *sent, loc_index, counts, block_picks)
+    )
+    parts = [own] + [along_x(part, steps) for part, steps in zip(sent, order)]
     parts = parts + [other_core(part) for part in parts]
+    own_picks = lax.dynamic_index_in_dim(block_picks, tile, 0, keepdims=False)
+    weight = block_weights(loc_table, counts, own_picks, loc_index[0], tile)
+    scaled, weight = lax.optimization_barrier((scaled, weight))
     whole = pl.pallas_call(
         block_kernel,
         out_shape=jax.ShapeDtypeStruct((PACKED_ROWS, 128), F32),
@@ -260,39 +279,33 @@
         compiler_params=pltpu.CompilerParams(vmem_limit_bytes=16 << 20),
         name="block_matrices",
     )(*parts, scaled)
-    whole, local_index, counts, block_picks = lax.optimization_barrier(
-        (whole, loc_index[0], counts, block_picks)
-    )
     far = both_ways(whole, "dom", 2)
     near = both_ways(whole, "ens", 1)
-    own_picks = lax.dynamic_index_in_dim(block_picks, tile, 0, keepdims=False)
-    later, own_picks = lax.optimization_barrier((whole, own_picks))
-    opposite = along_x(later, 2)
-    weight = block_weights(loc_table, counts, own_picks, local_index, tile)
-    near, far = lax.optimization_barrier((near, far))
+    opposite = along_x(whole, 2)
+    weight = jnp.broadcast_to(weight.reshape(-1, 1), (weight.size, 128))
+    weights = [weight, other_core(weight)]
+    near, far, opposite, weights = lax.optimization_barrier((near, far, opposite, weights))
     near_swapped, far_swapped = other_core(near), other_core(far)
-    weights = [
-        jnp.broadcast_to(part.reshape(-1, 1), (part.size, 128))
-        for part in (weight, other_core(weight))
-    ]
     same = jnp.stack([whole, near, near_swapped, opposite])
     far_both = jnp.stack([far, far_swapped])
-    same, far, far_both, weights = lax.optimization_barrier((same, far, far_both, weights))
+    same, far, far_both = lax.optimization_barrier((same, far, far_both))
     far_opposite = along_x(far, 2)
     far_near = both_ways(far_both, "ens", 1)
     beside = both_ways(same, "dom", 1)
-    combine = pl.pallas_call(
-        combine_kernel,
-        out_shape=jax.ShapeDtypeStruct((4, PACKED_ROWS, 128), F32),
-        in_specs=[vmem] * 6,
-        out_specs=vmem,
-        compiler_params=pltpu.CompilerParams(vmem_limit_bytes=16 << 20),
-        cost_estimate=pl.CostEstimate(flops=6000000, bytes_accessed=2000000, transcendentals=0),
-        name="combine_points",
-    )
-    sources = (same, beside, far, far_near, far_opposite)
-    theirs = other_core(combine(weights[1], *sources))
-    mine = combine(weights[0], *sources)
+    def combine(kernel, flops, *operands):
+        return pl.pallas_call(
+            kernel,
+            out_shape=jax.ShapeDtypeStruct((4, PACKED_ROWS, 128), F32),
+            in_specs=[vmem] * len(operands),
+            out_specs=vmem,
+            compiler_params=pltpu.CompilerParams(vmem_limit_bytes=16 << 20),
+            cost_estimate=pl.CostEstimate(flops=flops, bytes_accessed=2000000, transcendentals=0),
+            name=kernel.__name__,
+        )(*operands)
+
+    started = [combine(early_kernel, 2000000, part, same, far, far_opposite) for part in weights]
+    theirs = other_core(combine(late_kernel, 2000000, weights[1], started[1], beside, far_near))
+    mine = combine(late_kernel, 2000000, weights[0], started[0], beside, far_near)
     points, members, cells = background.shape[1:]
     analysis = pl.pallas_call(
         analysis_kernel,

time: 54.5 us -> 53.4 us (0.980)
  starting transfers between devices: 24.6 us -> 26.3 us
  waiting for transfers between devices: 11.5 us -> 9.85 us
  local copies, waits for them, and re-layouts: 4.34 us -> 3.34 us
    ppermute x4, starting transfers between devices: 11.3 us -> 14.7 us  [both_ways(): return lax.ppermute(value, ('ens', 'dom'), pairs)]
    ppermute x13, waiting for transfers between devices: 11.5 us -> 9.2 us  [along_x(): return lax.ppermute(value, 'ens', pairs)]
    ppermute x13, starting transfers between devices: 13.3 us -> 11.6 us  [along_x(): return lax.ppermute(value, 'ens', pairs)]
    eq x0 -> x2, local copies, waits for them, and re-layouts: none -> 0.9 us  [the longest x1 0.81 us: block_weights(): hit = (loc_index[:, :, None, :, None] == bins) & chosen[None, ..., None]]
    optimization_barrier x2 -> x0, local copies, waits for them, and re-layouts: 0.9 us -> none  [the longest x1 0.8 us: local(): lax.optimization_barrier((whole, loc_index[0], counts, block_picks))]
    squeeze x2 -> x1, local copies, waits for them, and re-layouts: 1.98 us -> 1.14 us  [block_of(): lax.dynamic_index_in_dim(blocks, lax.rem(chip + steps, 4), 0, keepdims=Fa...]
    ppermute x4, waiting for transfers between devices: 0.01 us -> 0.65 us  [both_ways(): return lax.ppermute(value, ('ens', 'dom'), pairs)]
  transfers between devices with their start and end apart: 17 -> 17, of which waited for: 6 -> 8; matrix products, arithmetic and copies ran while one was open for 9% -> 8% of each run, Pallas kernels for 1% -> 1%
where the time goes in v4:
time: 53.4 us; the launch traced here: 53 us
  starting transfers between devices  26.3 us (49%)
  Pallas kernels  11.3 us (21%)
  waiting for transfers between devices  9.85 us (18%)
  local copies, waits for them, and re-layouts  3.34 us (6%)
  other arithmetic  1.97 us (4%)
    ppermute x4, starting transfers between devices, both_ways(): return lax.ppermute(value, ('ens', 'dom'), pairs)  14.7 us
    ppermute x13, starting transfers between devices, along_x(): return lax.ppermute(value, 'ens', pairs)  11.6 us
    pallas_call x1, Pallas kernels, local(): pl.pallas_call(analysis_kernel, out_shape=jax.ShapeDtypeStruct((points, m...  9.4 us
    ppermute x13, waiting for transfers between devices, along_x(): return lax.ppermute(value, 'ens', pairs)  9.2 us
    squeeze x1, local copies, waits for them, and re-layouts, block_of(): lax.dynamic_index_in_dim(blocks, lax.rem(chip + steps, 4), 0, keepdims=Fa...  1.14 us
    pallas_call x1, Pallas kernels, local(): pl.pallas_call(block_kernel, out_shape=jax.ShapeDtypeStruct((PACKED_ROWS,...  1.09 us
  transfers between devices with their start and end apart: 17, of which 8 were waited for; matrix products, arithmetic and copies ran while one was open for 8% of the time, Pallas kernels for 1%

profile of v4, /device:TPU:1, one launch (start us, length us, event | category | flops | bytes accessed | tf_op | source)
XLA Modules:
  0.0 53.0 jit_solution(10573286642139190136)
XLA Ops:
  0.0 1.1 %dynamic-slice_bitcast_fusion = (f32[32,1024]{1,0:T(8,128)S(1)}, f32[32,1024]{1,0:T(8,128)S(1)}, f32[32,1024]{1,0:T(8,128)S(1)}, f32[32,1024]{1,0:T(8,128)S(1)}) fusion(f32[4,32,1024]{2,1,0:T(8,128)} %param.8, s32[]{:T(128)S(6)} %select_n.36, s32[]{:T(128)S(6)} %select_n.34, s32[]{:T(128)S(6)} %select_n.33, s32[]{:T(128)S(6)} %select_n.35), kind=kLoop, calls=%fused_computation.3 | loop fusion | bytes 1048592 | tf_op jit(solution)/shard_map/jit(dynamic_index_in_dim)/squeeze | solution.py:258
  1.1 2.1 %collective-permute-start = (f32[32,1024]{1,0:T(8,128)S(1)}, f32[32,1024]{1,0:T(8,128)S(1)}, u32[]{:S(2)}, u32[]{:S(2)}) collective-permute-start(f32[32,1024]{1,0:T(8,128)S(1)} %get-tuple-element.23), channel_id=1, source_target_pairs={{0,32},{16,48},{32,64},{48,80},{64,96},{80,112},{96,0},{112,16},{1... | collective-permute-start | bytes 393224 | tf_op jit(solution)/shard_map/ppermute | solution.py:219
  3.3 1.3 %collective-permute-start.1 = (f32[32,1024]{1,0:T(8,128)S(1)}, f32[32,1024]{1,0:T(8,128)S(1)}, u32[]{:S(2)}, u32[]{:S(2)}) collective-permute-start(f32[32,1024]{1,0:T(8,128)S(1)} %get-tuple-element.24), channel_id=1, source_target_pairs={{0,96},{16,112},{32,0},{48,16},{64,32},{80,48},{96,64},{112,80},{1... | collective-permute-start | bytes 393224 | tf_op jit(solution)/shard_map/ppermute | solution.py:219
  4.6 1.6 %collective-permute-start.2 = (f32[32,1024]{1,0:T(8,128)S(1)}, f32[32,1024]{1,0:T(8,128)S(1)}, u32[]{:S(2)}, u32[]{:S(2)}) collective-permute-start(f32[32,1024]{1,0:T(8,128)S(1)} %get-tuple-element.25), channel_id=1, source_target_pairs={{0,64},{16,80},{32,96},{48,112},{64,0},{80,16},{96,32},{112,48},{1... | collective-permute-start | bytes 393224 | tf_op jit(solution)/shard_map/ppermute | solution.py:219
  6.3 1.5 %collective-permute-start.3 = (f32[32,1024]{1,0:T(8,128)S(1)}, f32[32,1024]{1,0:T(8,128)S(1)}, u32[]{:S(2)}, u32[]{:S(2)}) collective-permute-start(f32[32,1024]{1,0:T(8,128)S(1)} %get-tuple-element.22.refs_0_), channel_id=1, source_target_pairs={{0,16},{16,0},{32,48},{48,32},{64,80},{80,64},{96,112},{112,96},{1... | collective-permute-start | bytes 393224 | tf_op jit(solution)/shard_map/ppermute | solution.py:219
  7.8 0.9 %dynamic-slice_reduce_fusion = s32[5]{0:T(128)S(1)} fusion(s32[16,5]{0,1:T(8,128)} %param.12, s32[]{:T(128)S(6)} %select_n.38), kind=kLoop, calls=%fused_computation.11 | loop fusion | bytes 44 | tf_op jit(solution)/shard_map/jit(dynamic_index_in_dim)/dynamic_slice | solution.py:239
  9.0 0.8 %copy.15 = s32[4,5,4]{2,1,0:T(8,128)S(1)} copy(s32[4,5,4]{1,2,0:T(4,128)} %bitcast.25) | data formatting | bytes 640 | tf_op jit(solution)/shard_map/eq | solution.py:244
  9.9 1.0 %select_reduce_fusion = f32[4,5,4]{2,1,0:T(8,128)S(1)} fusion(f32[64]{0:T(128)} %param.11, pred[5,4,4]{2,1,0:T(4,128)(4,1)S(1)} %fusion, pred[4,5,4,64]{3,2,1,0:T(4,128)(4,1)S(1)} %iota_compare_fusion), kind=kLoop, calls=%fused_computation.2 | loop fusion | flops 61360 | bytes 5776 | tf_op jit(solution)/shard_map/reduce_sum | solution.py:245
  11.0 0.5 collective-permute-start.5
  11.6 1.4 %collective-permute-start.6 = (f32[32,1024]{1,0:T(8,128)S(1)}, f32[32,1024]{1,0:T(8,128)S(1)}, u32[]{:S(2)}, u32[]{:S(2)}) collective-permute-start(f32[32,1024]{1,0:T(8,128)S(1)} %collective-permute-done.2.refs_3_), channel_id=1, source_target_pairs={{0,16},{16,0},{32,48},{48,32},{64,80},{80,64},{96,112},{112,96},{1... | collective-permute-start | bytes 393224 | tf_op jit(solution)/shard_map/ppermute | solution.py:219
  13.0 0.7 %constant_dynamic-slice_fusion.1 = (f32[1,1024]{1,0:T(1,128)S(1)}, f32[1,1024]{1,0:T(1,128)S(1)}) fusion(f32[4,1024]{1,0:T(4,128)} %param.10, s32[]{:T(128)S(6)} %select_n.37, f32[4,1024]{1,0:T(4,128)} %param.9), kind=kLoop, calls=%fused_computation.15 | loop fusion | flops 1024 | bytes 16388 | tf_op jit(solution)/shard_map/dynamic_slice | solution.py:260
  14.0 1.1 %block_matrices.1 = f32[264,128]{1,0:T(8,128)S(1)} custom-call(f32[32,1024]{1,0:T(8,128)S(1)} %get-tuple-element.22.refs_0_, f32[32,1024]{1,0:T(8,128)S(1)} %collective-permute-done.refs_1_, f32[32,1024]{1,0:T(8,128)S(1)} %collective-permute-done.1.refs_2_, f32[32,1024]{1,0:T(8,128)S(1)} %collective-permute-done.2.refs_3_, ...), custom_call_target="tpu_custom_call" | custom-call | tf_op jit(solution)/shard_map/block_matrices/pallas_call | solution.py:273
  15.1 1.1 %collective-permute-start.9 = (f32[264,128]{1,0:T(8,128)S(1)}, f32[264,128]{1,0:T(8,128)S(1)}, u32[]{:S(2)}, u32[]{:S(2)}) collective-permute-start(f32[264,128]{1,0:T(8,128)S(1)} %block_matrices.1), channel_id=1, source_target_pairs={{0,64},{16,80},{32,96},{48,112},{64,0},{80,16},{96,32},{112,48},{1... | collective-permute-start | bytes 405512 | tf_op jit(solution)/shard_map/ppermute | solution.py:219
  16.1 6.1 %collective-permute-start.8 = (f32[264,128]{1,0:T(8,128)S(1)}, f32[264,128]{1,0:T(8,128)S(1)}, u32[]{:S(2)}, u32[]{:S(2)}) collective-permute-start(f32[264,128]{1,0:T(8,128)S(1)} %block_matrices.1), channel_id=1, source_target_pairs={{0,2},{1,3},{2,4},{3,5},{4,6},{5,7},{6,8},{7,9},{8,10},{9,11},{10,... | collective-permute-start | bytes 405512 | tf_op jit(solution)/shard_map/ppermute | solution.py:235
  22.2 2.3 %collective-permute-start.7 = (f32[264,128]{1,0:T(8,128)S(1)}, f32[264,128]{1,0:T(8,128)S(1)}, u32[]{:S(2)}, u32[]{:S(2)}) collective-permute-start(f32[264,128]{1,0:T(8,128)S(1)} %block_matrices.1), channel_id=1, source_target_pairs={{0,32},{1,33},{2,34},{3,35},{4,36},{5,37},{6,38},{7,39},{8,40},{9,... | collective-permute-start | bytes 405512 | tf_op jit(solution)/shard_map/ppermute | solution.py:235
  24.6 1.2 %collective-permute-done.10.weight_ref = f32[80,128]{1,0:T(8,128)S(1)} collective-permute-done((f32[80,128]{1,0:T(8,128)S(1)}, f32[80,128]{1,0:T(8,128)S(1)}, u32[]{:S(2)}, u32[]{:S(2)}) %collective-permute-start.10) | collective-permute-done | bytes 40992 | tf_op jit(solution)/shard_map/ppermute | solution.py:219
  25.8 0.6 %collective-permute-done.7 = f32[264,128]{1,0:T(8,128)S(1)} collective-permute-done((f32[264,128]{1,0:T(8,128)S(1)}, f32[264,128]{1,0:T(8,128)S(1)}, u32[]{:S(2)}, u32[]{:S(2)}) %collective-permute-start.7) | collective-permute-done | bytes 135200 | tf_op jit(solution)/shard_map/ppermute | solution.py:235
  27.0 0.9 %collective-permute-done.12 = f32[264,128]{1,0:T(8,128)S(1)} collective-permute-done((f32[264,128]{1,0:T(8,128)S(1)}, f32[264,128]{1,0:T(8,128)S(1)}, u32[]{:S(2)}, u32[]{:S(2)}) %collective-permute-start.12) | collective-permute-done | bytes 135200 | tf_op jit(solution)/shard_map/ppermute | solution.py:219
  28.3 4.1 %collective-permute-start.14 = (f32[4,264,128]{2,1,0:T(8,128)S(1)}, f32[4,264,128]{2,1,0:T(8,128)S(1)}, u32[]{:S(2)}, u32[]{:S(2)}) collective-permute-start(f32[4,264,128]{2,1,0:T(8,128)S(1)} %pad_maximum_fusion.same), channel_id=1, source_target_pairs={{0,1},{1,2},{2,3},{3,4},{4,5},{5,6},{6,7},{7,8},{8,9},{9,10},{10,1... | collective-permute-start | bytes 1622024 | tf_op jit(solution)/shard_map/ppermute | solution.py:235
  32.4 2.3 %collective-permute-start.15 = (f32[2,264,128]{2,1,0:T(8,128)S(1)}, f32[2,264,128]{2,1,0:T(8,128)S(1)}, u32[]{:S(2)}, u32[]{:S(2)}) collective-permute-start(f32[2,264,128]{2,1,0:T(8,128)S(1)} %pad_maximum_fusion.1), channel_id=1, source_target_pairs={{0,32},{1,33},{2,34},{3,35},{4,36},{5,37},{6,38},{7,39},{8,40},{9,... | collective-permute-start | bytes 811016 | tf_op jit(solution)/shard_map/ppermute | solution.py:235
  34.7 1.0 %collective-permute-start.13 = (f32[264,128]{1,0:T(8,128)S(1)}, f32[264,128]{1,0:T(8,128)S(1)}, u32[]{:S(2)}, u32[]{:S(2)}) collective-permute-start(f32[264,128]{1,0:T(8,128)S(1)} %collective-permute-done.8.far), channel_id=1, source_target_pairs={{0,64},{16,80},{32,96},{48,112},{64,0},{80,16},{96,32},{112,48},{1... | collective-permute-start | bytes 405512 | tf_op jit(solution)/shard_map/ppermute | solution.py:219
  35.7 5.2 %collective-permute-done.13.far_opposite = f32[264,128]{1,0:T(8,128)S(1)} collective-permute-done((f32[264,128]{1,0:T(8,128)S(1)}, f32[264,128]{1,0:T(8,128)S(1)}, u32[]{:S(2)}, u32[]{:S(2)}) %collective-permute-start.13) | collective-permute-done | bytes 135200 | tf_op jit(solution)/shard_map/ppermute | solution.py:219
  42.1 1.4 %collective-permute-done.16.theirs_ref = f32[4,264,128]{2,1,0:T(8,128)S(1)} collective-permute-done((f32[4,264,128]{2,1,0:T(8,128)S(1)}, f32[4,264,128]{2,1,0:T(8,128)S(1)}, u32[]{:S(2)}, u32[]{:S(2)}) %collective-permute-start.16) | collective-permute-done | bytes 540704 | tf_op jit(solution)/shard_map/ppermute | solution.py:219
  43.5 9.4 %root_and_analysis.1 = f32[4,256,1024]{2,1,0:T(8,128)} custom-call(f32[4,264,128]{2,1,0:T(8,128)S(1)} %late_kernel.2.mine_ref, f32[4,264,128]{2,1,0:T(8,128)S(1)} %collective-permute-done.16.theirs_ref, f32[4,256,1024]{2,1,0:T(8,128)} %bitcast.20), custom_call_target="tpu_custom_call" | custom-call | tf_op jit(solution)/shard_map/root_and_analysis/pallas_call | solution.py:310
  (35 shorter events, 3.1 us)
Async XLA Ops:
  0.0 8.7 %copy-start = (s32[16,5,4]{0,2,1:T(4,128)S(1)}, s32[16,5,4]{0,2,1:T(4,128)}, u32[]{:S(2)}) copy-start(s32[16,5,4]{0,2,1:T(4,128)} %param.13) | copy-start | bytes 3844
  1.1 9.8 %collective-permute-start = (f32[32,1024]{1,0:T(8,128)S(1)}, f32[32,1024]{1,0:T(8,128)S(1)}, u32[]{:S(2)}, u32[]{:S(2)}) collective-permute-start(f32[32,1024]{1,0:T(8,128)S(1)} %get-tuple-element.23), channel_id=1, source_target_pairs={{0,32},{16,48},{32,64},{48,80},{64,96},{80,112},{96,0},{112,16},{1... | collective-permute-start | bytes 393224 | tf_op jit(solution)/shard_map/ppermute | solution.py:219
  3.3 7.8 %collective-permute-start.1 = (f32[32,1024]{1,0:T(8,128)S(1)}, f32[32,1024]{1,0:T(8,128)S(1)}, u32[]{:S(2)}, u32[]{:S(2)}) collective-permute-start(f32[32,1024]{1,0:T(8,128)S(1)} %get-tuple-element.24), channel_id=1, source_target_pairs={{0,96},{16,112},{32,0},{48,16},{64,32},{80,48},{96,64},{112,80},{1... | collective-permute-start | bytes 393224 | tf_op jit(solution)/shard_map/ppermute | solution.py:219
  4.6 7.0 %collective-permute-start.2 = (f32[32,1024]{1,0:T(8,128)S(1)}, f32[32,1024]{1,0:T(8,128)S(1)}, u32[]{:S(2)}, u32[]{:S(2)}) collective-permute-start(f32[32,1024]{1,0:T(8,128)S(1)} %get-tuple-element.25), channel_id=1, source_target_pairs={{0,64},{16,80},{32,96},{48,112},{64,0},{80,16},{96,32},{112,48},{1... | collective-permute-start | bytes 393224 | tf_op jit(solution)/shard_map/ppermute | solution.py:219
  6.3 7.6 %collective-permute-start.3 = (f32[32,1024]{1,0:T(8,128)S(1)}, f32[32,1024]{1,0:T(8,128)S(1)}, u32[]{:S(2)}, u32[]{:S(2)}) collective-permute-start(f32[32,1024]{1,0:T(8,128)S(1)} %get-tuple-element.22.refs_0_), channel_id=1, source_target_pairs={{0,16},{16,0},{32,48},{48,32},{64,80},{80,64},{96,112},{112,96},{1... | collective-permute-start | bytes 393224 | tf_op jit(solution)/shard_map/ppermute | solution.py:219
  10.9 2.9 %collective-permute-start.4 = (f32[32,1024]{1,0:T(8,128)S(1)}, f32[32,1024]{1,0:T(8,128)S(1)}, u32[]{:S(2)}, u32[]{:S(2)}) collective-permute-start(f32[32,1024]{1,0:T(8,128)S(1)} %collective-permute-done.refs_1_), channel_id=1, source_target_pairs={{0,16},{16,0},{32,48},{48,32},{64,80},{80,64},{96,112},{112,96},{1... | collective-permute-start | bytes 393224 | tf_op jit(solution)/shard_map/ppermute | solution.py:219
  11.0 2.8 %collective-permute-start.5 = (f32[32,1024]{1,0:T(8,128)S(1)}, f32[32,1024]{1,0:T(8,128)S(1)}, u32[]{:S(2)}, u32[]{:S(2)}) collective-permute-start(f32[32,1024]{1,0:T(8,128)S(1)} %collective-permute-done.1.refs_2_), channel_id=1, source_target_pairs={{0,16},{16,0},{32,48},{48,32},{64,80},{80,64},{96,112},{112,96},{1... | collective-permute-start | bytes 393224 | tf_op jit(solution)/shard_map/ppermute | solution.py:219
  11.6 2.4 %collective-permute-start.6 = (f32[32,1024]{1,0:T(8,128)S(1)}, f32[32,1024]{1,0:T(8,128)S(1)}, u32[]{:S(2)}, u32[]{:S(2)}) collective-permute-start(f32[32,1024]{1,0:T(8,128)S(1)} %collective-permute-done.2.refs_3_), channel_id=1, source_target_pairs={{0,16},{16,0},{32,48},{48,32},{64,80},{80,64},{96,112},{112,96},{1... | collective-permute-start | bytes 393224 | tf_op jit(solution)/shard_map/ppermute | solution.py:219
  15.1 10.8 %collective-permute-start.9 = (f32[264,128]{1,0:T(8,128)S(1)}, f32[264,128]{1,0:T(8,128)S(1)}, u32[]{:S(2)}, u32[]{:S(2)}) collective-permute-start(f32[264,128]{1,0:T(8,128)S(1)} %block_matrices.1), channel_id=1, source_target_pairs={{0,64},{16,80},{32,96},{48,112},{64,0},{80,16},{96,32},{112,48},{1... | collective-permute-start | bytes 405512 | tf_op jit(solution)/shard_map/ppermute | solution.py:219
  16.1 9.7 %collective-permute-start.8 = (f32[264,128]{1,0:T(8,128)S(1)}, f32[264,128]{1,0:T(8,128)S(1)}, u32[]{:S(2)}, u32[]{:S(2)}) collective-permute-start(f32[264,128]{1,0:T(8,128)S(1)} %block_matrices.1), channel_id=1, source_target_pairs={{0,2},{1,3},{2,4},{3,5},{4,6},{5,7},{6,8},{7,9},{8,10},{9,11},{10,... | collective-permute-start | bytes 405512 | tf_op jit(solution)/shard_map/ppermute | solution.py:235
  22.2 4.3 %collective-permute-start.7 = (f32[264,128]{1,0:T(8,128)S(1)}, f32[264,128]{1,0:T(8,128)S(1)}, u32[]{:S(2)}, u32[]{:S(2)}) collective-permute-start(f32[264,128]{1,0:T(8,128)S(1)} %block_matrices.1), channel_id=1, source_target_pairs={{0,32},{1,33},{2,34},{3,35},{4,36},{5,37},{6,38},{7,39},{8,40},{9,... | collective-permute-start | bytes 405512 | tf_op jit(solution)/shard_map/ppermute | solution.py:235
  24.6 1.2 %collective-permute-start.10 = (f32[80,128]{1,0:T(8,128)S(1)}, f32[80,128]{1,0:T(8,128)S(1)}, u32[]{:S(2)}, u32[]{:S(2)}) collective-permute-start(f32[80,128]{1,0:T(8,128)S(1)} %broadcast_in_dim.28.weight_ref), channel_id=1, source_target_pairs={{0,16},{16,0},{32,48},{48,32},{64,80},{80,64},{96,112},{112,96},{1... | collective-permute-start | bytes 122888 | tf_op jit(solution)/shard_map/ppermute | solution.py:219
  26.5 1.4 %collective-permute-start.12 = (f32[264,128]{1,0:T(8,128)S(1)}, f32[264,128]{1,0:T(8,128)S(1)}, u32[]{:S(2)}, u32[]{:S(2)}) collective-permute-start(f32[264,128]{1,0:T(8,128)S(1)} %collective-permute-done.8.far), channel_id=1, source_target_pairs={{0,16},{16,0},{32,48},{48,32},{64,80},{80,64},{96,112},{112,96},{1... | collective-permute-start | bytes 405512 | tf_op jit(solution)/shard_map/ppermute | solution.py:219
  26.9 1.4 %collective-permute-start.11 = (f32[264,128]{1,0:T(8,128)S(1)}, f32[264,128]{1,0:T(8,128)S(1)}, u32[]{:S(2)}, u32[]{:S(2)}) collective-permute-start(f32[264,128]{1,0:T(8,128)S(1)} %collective-permute-done.7), channel_id=1, source_target_pairs={{0,16},{16,0},{32,48},{48,32},{64,80},{80,64},{96,112},{112,96},{1... | collective-permute-start | bytes 405512 | tf_op jit(solution)/shard_map/ppermute | solution.py:219
  28.3 12.8 %collective-permute-start.14 = (f32[4,264,128]{2,1,0:T(8,128)S(1)}, f32[4,264,128]{2,1,0:T(8,128)S(1)}, u32[]{:S(2)}, u32[]{:S(2)}) collective-permute-start(f32[4,264,128]{2,1,0:T(8,128)S(1)} %pad_maximum_fusion.same), channel_id=1, source_target_pairs={{0,1},{1,2},{2,3},{3,4},{4,5},{5,6},{6,7},{7,8},{8,9},{9,10},{10,1... | collective-permute-start | bytes 1622024 | tf_op jit(solution)/shard_map/ppermute | solution.py:235
  32.4 8.6 %collective-permute-start.15 = (f32[2,264,128]{2,1,0:T(8,128)S(1)}, f32[2,264,128]{2,1,0:T(8,128)S(1)}, u32[]{:S(2)}, u32[]{:S(2)}) collective-permute-start(f32[2,264,128]{2,1,0:T(8,128)S(1)} %pad_maximum_fusion.1), channel_id=1, source_target_pairs={{0,32},{1,33},{2,34},{3,35},{4,36},{5,37},{6,38},{7,39},{8,40},{9,... | collective-permute-start | bytes 811016 | tf_op jit(solution)/shard_map/ppermute | solution.py:235
  34.7 6.2 %collective-permute-start.13 = (f32[264,128]{1,0:T(8,128)S(1)}, f32[264,128]{1,0:T(8,128)S(1)}, u32[]{:S(2)}, u32[]{:S(2)}) collective-permute-start(f32[264,128]{1,0:T(8,128)S(1)} %collective-permute-done.8.far), channel_id=1, source_target_pairs={{0,64},{16,80},{32,96},{48,112},{64,0},{80,16},{96,32},{112,48},{1... | collective-permute-start | bytes 405512 | tf_op jit(solution)/shard_map/ppermute | solution.py:219
  41.3 2.2 %collective-permute-start.16 = (f32[4,264,128]{2,1,0:T(8,128)S(1)}, f32[4,264,128]{2,1,0:T(8,128)S(1)}, u32[]{:S(2)}, u32[]{:S(2)}) collective-permute-start(f32[4,264,128]{2,1,0:T(8,128)S(1)} %late_kernel.3), channel_id=1, source_target_pairs={{0,16},{16,0},{32,48},{48,32},{64,80},{80,64},{96,112},{112,96},{1... | collective-permute-start | bytes 1622024 | tf_op jit(solution)/shard_map/ppermute | solution.py:219

commit v5 on v4

--- a/solution.py
+++ b/solution.py
@@ -172,7 +172,7 @@
         system = 255.0 * identity + gram
         inverse_norm = lax.rsqrt(jnp.sum(system * system, axis=(0, 1), keepdims=True))
         system_pair = split2(system)
-        squares.append(dot3(system_pair, system_pair) * (inverse_norm * inverse_norm))
+        squares.append(dot3_rows(system_pair, system_pair) * (inverse_norm * inverse_norm))
         start.append(system * inverse_norm)
         scale.append(inverse_norm)
         drives.append(jnp.concatenate([extra[1:2], extra[3:4]], axis=1))
@@ -183,23 +183,23 @@
             split2(1.6875 * identity - 0.5625 * value[i] + 0.0625 * squared[i]) for i in every
         ]
         return [
-            dot3(squared_pair[i], rest[i]) + (2.25 * identity - 2.4375 * value[i]) for i in every
+            dot3_rows(squared_pair[i], rest[i]) + (2.25 * identity - 2.4375 * value[i]) for i in every
         ]
 
     pair = [split2(start[i]) for i in every]
     root = two_steps(start, squares)
     root_pair = [split2(root[i]) for i in every]
-    value = [dot3(split2(dot3(pair[i], root_pair[i])), root_pair[i]) for i in every]
+    value = [dot3_rows(split2(dot3_rows(pair[i], root_pair[i])), root_pair[i]) for i in every]
     pair = [split2(value[i]) for i in every]
-    factor_pair = [split2(f) for f in two_steps(value, [dot3(pair[i], pair[i]) for i in every])]
-    root_pair = [split2(dot3(factor_pair[i], root_pair[i])) for i in every]
-    value = [dot3(split2(dot3(pair[i], factor_pair[i])), factor_pair[i]) for i in every]
+    factor_pair = [split2(f) for f in two_steps(value, [dot3_rows(pair[i], pair[i]) for i in every])]
+    root_pair = [split2(dot3_rows(factor_pair[i], root_pair[i])) for i in every]
+    value = [dot3_rows(split2(dot3_rows(pair[i], factor_pair[i])), factor_pair[i]) for i in every]
     pair = [split2(value[i]) for i in every]
     for point in every:
         for chunk in chunks():
             fetch(point, *chunk).wait()
-    factor_pair = [split2(f) for f in two_steps(value, [dot3(pair[i], pair[i]) for i in every])]
-    root = [dot3(factor_pair[i], root_pair[i]) for i in every]
+    factor_pair = [split2(f) for f in two_steps(value, [dot3_rows(pair[i], pair[i]) for i in every])]
+    root = [dot3_rows(factor_pair[i], root_pair[i]) for i in every]
     for point in every:
         inner = jnp.sum(root[point] * drives[point], axis=1, keepdims=True)
         mean = jnp.sum(root[point] * inner, axis=0, keepdims=True) * scale[point]
@@ -292,6 +292,7 @@
     far_opposite = along_x(far, 2)
     far_near = both_ways(far_both, "ens", 1)
     beside = both_ways(same, "dom", 1)
+    far_near, beside, far_opposite = lax.optimization_barrier((far_near, beside, far_opposite))
     def combine(kernel, flops, *operands):
         return pl.pallas_call(
             kernel,

time: 53.4 us -> 53.4 us (level)
  no operation moved by 1% of the time
where the time goes in v5:
time: 53.4 us; the launch traced here: 53 us
  starting transfers between devices  26.5 us (50%)
  Pallas kernels  11.3 us (21%)
  waiting for transfers between devices  9.69 us (18%)
  local copies, waits for them, and re-layouts  3.34 us (6%)
  other arithmetic  1.98 us (4%)
    ppermute x4, starting transfers between devices, both_ways(): return lax.ppermute(value, ('ens', 'dom'), pairs)  14.7 us
    ppermute x13, starting transfers between devices, along_x(): return lax.ppermute(value, 'ens', pairs)  11.8 us
    pallas_call x1, Pallas kernels, local(): pl.pallas_call(analysis_kernel, out_shape=jax.ShapeDtypeStruct((points, m...  9.37 us
    ppermute x13, waiting for transfers between devices, along_x(): return lax.ppermute(value, 'ens', pairs)  9.04 us
    squeeze x1, local copies, waits for them, and re-layouts, block_of(): lax.dynamic_index_in_dim(blocks, lax.rem(chip + steps, 4), 0, keepdims=Fa...  1.14 us
    pallas_call x1, Pallas kernels, local(): pl.pallas_call(block_kernel, out_shape=jax.ShapeDtypeStruct((PACKED_ROWS,...  1.09 us
  transfers between devices with their start and end apart: 17, of which 8 were waited for; matrix products, arithmetic and copies ran while one was open for 8% of the time, Pallas kernels for 1%

profile of v5, /device:TPU:1, one launch (start us, length us, event | category | flops | bytes accessed | tf_op | source)
XLA Modules:
  0.0 53.0 jit_solution(654848004588716670)
XLA Ops:
  0.0 1.1 %dynamic-slice_bitcast_fusion = (f32[32,1024]{1,0:T(8,128)S(1)}, f32[32,1024]{1,0:T(8,128)S(1)}, f32[32,1024]{1,0:T(8,128)S(1)}, f32[32,1024]{1,0:T(8,128)S(1)}) fusion(f32[4,32,1024]{2,1,0:T(8,128)} %param.8, s32[]{:T(128)S(6)} %select_n.36, s32[]{:T(128)S(6)} %select_n.34, s32[]{:T(128)S(6)} %select_n.33, s32[]{:T(128)S(6)} %select_n.35), kind=kLoop, calls=%fused_computation.3 | loop fusion | bytes 1048592 | tf_op jit(solution)/shard_map/jit(dynamic_index_in_dim)/squeeze | solution.py:258
  1.1 2.1 %collective-permute-start = (f32[32,1024]{1,0:T(8,128)S(1)}, f32[32,1024]{1,0:T(8,128)S(1)}, u32[]{:S(2)}, u32[]{:S(2)}) collective-permute-start(f32[32,1024]{1,0:T(8,128)S(1)} %get-tuple-element.26), channel_id=1, source_target_pairs={{0,32},{16,48},{32,64},{48,80},{64,96},{80,112},{96,0},{112,16},{1... | collective-permute-start | bytes 393224 | tf_op jit(solution)/shard_map/ppermute | solution.py:219
  3.3 1.3 %collective-permute-start.1 = (f32[32,1024]{1,0:T(8,128)S(1)}, f32[32,1024]{1,0:T(8,128)S(1)}, u32[]{:S(2)}, u32[]{:S(2)}) collective-permute-start(f32[32,1024]{1,0:T(8,128)S(1)} %get-tuple-element.27), channel_id=1, source_target_pairs={{0,96},{16,112},{32,0},{48,16},{64,32},{80,48},{96,64},{112,80},{1... | collective-permute-start | bytes 393224 | tf_op jit(solution)/shard_map/ppermute | solution.py:219
  4.6 1.6 %collective-permute-start.2 = (f32[32,1024]{1,0:T(8,128)S(1)}, f32[32,1024]{1,0:T(8,128)S(1)}, u32[]{:S(2)}, u32[]{:S(2)}) collective-permute-start(f32[32,1024]{1,0:T(8,128)S(1)} %get-tuple-element.28), channel_id=1, source_target_pairs={{0,64},{16,80},{32,96},{48,112},{64,0},{80,16},{96,32},{112,48},{1... | collective-permute-start | bytes 393224 | tf_op jit(solution)/shard_map/ppermute | solution.py:219
  6.3 1.5 %collective-permute-start.3 = (f32[32,1024]{1,0:T(8,128)S(1)}, f32[32,1024]{1,0:T(8,128)S(1)}, u32[]{:S(2)}, u32[]{:S(2)}) collective-permute-start(f32[32,1024]{1,0:T(8,128)S(1)} %get-tuple-element.25.refs_0_), channel_id=1, source_target_pairs={{0,16},{16,0},{32,48},{48,32},{64,80},{80,64},{96,112},{112,96},{1... | collective-permute-start | bytes 393224 | tf_op jit(solution)/shard_map/ppermute | solution.py:219
  7.8 0.9 %dynamic-slice_reduce_fusion = s32[5]{0:T(128)S(1)} fusion(s32[16,5]{0,1:T(8,128)} %param.12, s32[]{:T(128)S(6)} %select_n.38), kind=kLoop, calls=%fused_computation.11 | loop fusion | bytes 44 | tf_op jit(solution)/shard_map/jit(dynamic_index_in_dim)/dynamic_slice | solution.py:239
  9.0 0.8 %copy.15 = s32[4,5,4]{2,1,0:T(8,128)S(1)} copy(s32[4,5,4]{1,2,0:T(4,128)} %bitcast.25) | data formatting | bytes 640 | tf_op jit(solution)/shard_map/eq | solution.py:244
  9.9 1.0 %select_reduce_fusion = f32[4,5,4]{2,1,0:T(8,128)S(1)} fusion(f32[64]{0:T(128)} %param.11, pred[5,4,4]{2,1,0:T(4,128)(4,1)S(1)} %fusion, pred[4,5,4,64]{3,2,1,0:T(4,128)(4,1)S(1)} %iota_compare_fusion), kind=kLoop, calls=%fused_computation.2 | loop fusion | flops 61360 | bytes 5776 | tf_op jit(solution)/shard_map/reduce_sum | solution.py:245
  11.6 1.4 %collective-permute-start.6 = (f32[32,1024]{1,0:T(8,128)S(1)}, f32[32,1024]{1,0:T(8,128)S(1)}, u32[]{:S(2)}, u32[]{:S(2)}) collective-permute-start(f32[32,1024]{1,0:T(8,128)S(1)} %collective-permute-done.2.refs_3_), channel_id=1, source_target_pairs={{0,16},{16,0},{32,48},{48,32},{64,80},{80,64},{96,112},{112,96},{1... | collective-permute-start | bytes 393224 | tf_op jit(solution)/shard_map/ppermute | solution.py:219
  13.0 0.7 %constant_dynamic-slice_fusion.1 = (f32[1,1024]{1,0:T(1,128)S(1)}, f32[1,1024]{1,0:T(1,128)S(1)}) fusion(f32[4,1024]{1,0:T(4,128)} %param.10, s32[]{:T(128)S(6)} %select_n.37, f32[4,1024]{1,0:T(4,128)} %param.9), kind=kLoop, calls=%fused_computation.15 | loop fusion | flops 1024 | bytes 16388 | tf_op jit(solution)/shard_map/dynamic_slice | solution.py:260
  14.0 1.1 %block_matrices.1 = f32[264,128]{1,0:T(8,128)S(1)} custom-call(f32[32,1024]{1,0:T(8,128)S(1)} %get-tuple-element.25.refs_0_, f32[32,1024]{1,0:T(8,128)S(1)} %collective-permute-done.refs_1_, f32[32,1024]{1,0:T(8,128)S(1)} %collective-permute-done.1.refs_2_, f32[32,1024]{1,0:T(8,128)S(1)} %collective-permute-done.2.refs_3_, ...), custom_call_target="tpu_custom_call" | custom-call | tf_op jit(solution)/shard_map/block_matrices/pallas_call | solution.py:273
  15.1 1.1 %collective-permute-start.9 = (f32[264,128]{1,0:T(8,128)S(1)}, f32[264,128]{1,0:T(8,128)S(1)}, u32[]{:S(2)}, u32[]{:S(2)}) collective-permute-start(f32[264,128]{1,0:T(8,128)S(1)} %block_matrices.1), channel_id=1, source_target_pairs={{0,64},{16,80},{32,96},{48,112},{64,0},{80,16},{96,32},{112,48},{1... | collective-permute-start | bytes 405512 | tf_op jit(solution)/shard_map/ppermute | solution.py:219
  16.1 6.1 %collective-permute-start.8 = (f32[264,128]{1,0:T(8,128)S(1)}, f32[264,128]{1,0:T(8,128)S(1)}, u32[]{:S(2)}, u32[]{:S(2)}) collective-permute-start(f32[264,128]{1,0:T(8,128)S(1)} %block_matrices.1), channel_id=1, source_target_pairs={{0,2},{1,3},{2,4},{3,5},{4,6},{5,7},{6,8},{7,9},{8,10},{9,11},{10,... | collective-permute-start | bytes 405512 | tf_op jit(solution)/shard_map/ppermute | solution.py:235
  22.2 2.3 %collective-permute-start.7 = (f32[264,128]{1,0:T(8,128)S(1)}, f32[264,128]{1,0:T(8,128)S(1)}, u32[]{:S(2)}, u32[]{:S(2)}) collective-permute-start(f32[264,128]{1,0:T(8,128)S(1)} %block_matrices.1), channel_id=1, source_target_pairs={{0,32},{1,33},{2,34},{3,35},{4,36},{5,37},{6,38},{7,39},{8,40},{9,... | collective-permute-start | bytes 405512 | tf_op jit(solution)/shard_map/ppermute | solution.py:235
  24.6 1.2 %collective-permute-done.10.weight_ref = f32[80,128]{1,0:T(8,128)S(1)} collective-permute-done((f32[80,128]{1,0:T(8,128)S(1)}, f32[80,128]{1,0:T(8,128)S(1)}, u32[]{:S(2)}, u32[]{:S(2)}) %collective-permute-start.10) | collective-permute-done | bytes 40992 | tf_op jit(solution)/shard_map/ppermute | solution.py:219
  25.8 0.6 %collective-permute-done.7 = f32[264,128]{1,0:T(8,128)S(1)} collective-permute-done((f32[264,128]{1,0:T(8,128)S(1)}, f32[264,128]{1,0:T(8,128)S(1)}, u32[]{:S(2)}, u32[]{:S(2)}) %collective-permute-start.7) | collective-permute-done | bytes 135200 | tf_op jit(solution)/shard_map/ppermute | solution.py:235
  27.0 0.9 %collective-permute-done.12 = f32[264,128]{1,0:T(8,128)S(1)} collective-permute-done((f32[264,128]{1,0:T(8,128)S(1)}, f32[264,128]{1,0:T(8,128)S(1)}, u32[]{:S(2)}, u32[]{:S(2)}) %collective-permute-start.12) | collective-permute-done | bytes 135200 | tf_op jit(solution)/shard_map/ppermute | solution.py:219
  28.3 4.1 %collective-permute-start.14 = (f32[4,264,128]{2,1,0:T(8,128)S(1)}, f32[4,264,128]{2,1,0:T(8,128)S(1)}, u32[]{:S(2)}, u32[]{:S(2)}) collective-permute-start(f32[4,264,128]{2,1,0:T(8,128)S(1)} %pad_maximum_fusion.same), channel_id=1, source_target_pairs={{0,1},{1,2},{2,3},{3,4},{4,5},{5,6},{6,7},{7,8},{8,9},{9,10},{10,1... | collective-permute-start | bytes 1622024 | tf_op jit(solution)/shard_map/ppermute | solution.py:235
  32.4 2.3 %collective-permute-start.13 = (f32[2,264,128]{2,1,0:T(8,128)S(1)}, f32[2,264,128]{2,1,0:T(8,128)S(1)}, u32[]{:S(2)}, u32[]{:S(2)}) collective-permute-start(f32[2,264,128]{2,1,0:T(8,128)S(1)} %pad_maximum_fusion.1), channel_id=1, source_target_pairs={{0,32},{1,33},{2,34},{3,35},{4,36},{5,37},{6,38},{7,39},{8,40},{9,... | collective-permute-start | bytes 811016 | tf_op jit(solution)/shard_map/ppermute | solution.py:235
  34.7 1.0 %collective-permute-start.15 = (f32[264,128]{1,0:T(8,128)S(1)}, f32[264,128]{1,0:T(8,128)S(1)}, u32[]{:S(2)}, u32[]{:S(2)}) collective-permute-start(f32[264,128]{1,0:T(8,128)S(1)} %collective-permute-done.8.far), channel_id=1, source_target_pairs={{0,64},{16,80},{32,96},{48,112},{64,0},{80,16},{96,32},{112,48},{1... | collective-permute-start | bytes 405512 | tf_op jit(solution)/shard_map/ppermute | solution.py:219
  35.7 5.2 %collective-permute-done.15.far_opposite = f32[264,128]{1,0:T(8,128)S(1)} collective-permute-done((f32[264,128]{1,0:T(8,128)S(1)}, f32[264,128]{1,0:T(8,128)S(1)}, u32[]{:S(2)}, u32[]{:S(2)}) %collective-permute-start.15) | collective-permute-done | bytes 135200 | tf_op jit(solution)/shard_map/ppermute | solution.py:219
  41.3 0.6 %collective-permute-start.16 = (f32[4,264,128]{2,1,0:T(8,128)S(1)}, f32[4,264,128]{2,1,0:T(8,128)S(1)}, u32[]{:S(2)}, u32[]{:S(2)}) collective-permute-start(f32[4,264,128]{2,1,0:T(8,128)S(1)} %late_kernel.3), channel_id=1, source_target_pairs={{0,16},{16,0},{32,48},{48,32},{64,80},{80,64},{96,112},{112,96},{1... | collective-permute-start | bytes 1622024 | tf_op jit(solution)/shard_map/ppermute | solution.py:219
  42.3 1.2 %collective-permute-done.16.theirs_ref = f32[4,264,128]{2,1,0:T(8,128)S(1)} collective-permute-done((f32[4,264,128]{2,1,0:T(8,128)S(1)}, f32[4,264,128]{2,1,0:T(8,128)S(1)}, u32[]{:S(2)}, u32[]{:S(2)}) %collective-permute-start.16) | collective-permute-done | bytes 540704 | tf_op jit(solution)/shard_map/ppermute | solution.py:219
  43.5 9.4 %root_and_analysis.1 = f32[4,256,1024]{2,1,0:T(8,128)} custom-call(f32[4,264,128]{2,1,0:T(8,128)S(1)} %late_kernel.2.mine_ref, f32[4,264,128]{2,1,0:T(8,128)S(1)} %collective-permute-done.16.theirs_ref, f32[4,256,1024]{2,1,0:T(8,128)} %bitcast.20), custom_call_target="tpu_custom_call" | custom-call | tf_op jit(solution)/shard_map/root_and_analysis/pallas_call | solution.py:311
  (35 shorter events, 3.2 us)
Async XLA Ops:
  0.0 8.7 %copy-start = (s32[16,5,4]{0,2,1:T(4,128)S(1)}, s32[16,5,4]{0,2,1:T(4,128)}, u32[]{:S(2)}) copy-start(s32[16,5,4]{0,2,1:T(4,128)} %param.13) | copy-start | bytes 3844
  1.1 9.8 %collective-permute-start = (f32[32,1024]{1,0:T(8,128)S(1)}, f32[32,1024]{1,0:T(8,128)S(1)}, u32[]{:S(2)}, u32[]{:S(2)}) collective-permute-start(f32[32,1024]{1,0:T(8,128)S(1)} %get-tuple-element.26), channel_id=1, source_target_pairs={{0,32},{16,48},{32,64},{48,80},{64,96},{80,112},{96,0},{112,16},{1... | collective-permute-start | bytes 393224 | tf_op jit(solution)/shard_map/ppermute | solution.py:219
  3.3 7.8 %collective-permute-start.1 = (f32[32,1024]{1,0:T(8,128)S(1)}, f32[32,1024]{1,0:T(8,128)S(1)}, u32[]{:S(2)}, u32[]{:S(2)}) collective-permute-start(f32[32,1024]{1,0:T(8,128)S(1)} %get-tuple-element.27), channel_id=1, source_target_pairs={{0,96},{16,112},{32,0},{48,16},{64,32},{80,48},{96,64},{112,80},{1... | collective-permute-start | bytes 393224 | tf_op jit(solution)/shard_map/ppermute | solution.py:219
  4.6 7.0 %collective-permute-start.2 = (f32[32,1024]{1,0:T(8,128)S(1)}, f32[32,1024]{1,0:T(8,128)S(1)}, u32[]{:S(2)}, u32[]{:S(2)}) collective-permute-start(f32[32,1024]{1,0:T(8,128)S(1)} %get-tuple-element.28), channel_id=1, source_target_pairs={{0,64},{16,80},{32,96},{48,112},{64,0},{80,16},{96,32},{112,48},{1... | collective-permute-start | bytes 393224 | tf_op jit(solution)/shard_map/ppermute | solution.py:219
  6.3 7.6 %collective-permute-start.3 = (f32[32,1024]{1,0:T(8,128)S(1)}, f32[32,1024]{1,0:T(8,128)S(1)}, u32[]{:S(2)}, u32[]{:S(2)}) collective-permute-start(f32[32,1024]{1,0:T(8,128)S(1)} %get-tuple-element.25.refs_0_), channel_id=1, source_target_pairs={{0,16},{16,0},{32,48},{48,32},{64,80},{80,64},{96,112},{112,96},{1... | collective-permute-start | bytes 393224 | tf_op jit(solution)/shard_map/ppermute | solution.py:219
  10.9 2.9 %collective-permute-start.4 = (f32[32,1024]{1,0:T(8,128)S(1)}, f32[32,1024]{1,0:T(8,128)S(1)}, u32[]{:S(2)}, u32[]{:S(2)}) collective-permute-start(f32[32,1024]{1,0:T(8,128)S(1)} %collective-permute-done.refs_1_), channel_id=1, source_target_pairs={{0,16},{16,0},{32,48},{48,32},{64,80},{80,64},{96,112},{112,96},{1... | collective-permute-start | bytes 393224 | tf_op jit(solution)/shard_map/ppermute | solution.py:219
  11.0 2.8 %collective-permute-start.5 = (f32[32,1024]{1,0:T(8,128)S(1)}, f32[32,1024]{1,0:T(8,128)S(1)}, u32[]{:S(2)}, u32[]{:S(2)}) collective-permute-start(f32[32,1024]{1,0:T(8,128)S(1)} %collective-permute-done.1.refs_2_), channel_id=1, source_target_pairs={{0,16},{16,0},{32,48},{48,32},{64,80},{80,64},{96,112},{112,96},{1... | collective-permute-start | bytes 393224 | tf_op jit(solution)/shard_map/ppermute | solution.py:219
  11.6 2.4 %collective-permute-start.6 = (f32[32,1024]{1,0:T(8,128)S(1)}, f32[32,1024]{1,0:T(8,128)S(1)}, u32[]{:S(2)}, u32[]{:S(2)}) collective-permute-start(f32[32,1024]{1,0:T(8,128)S(1)} %collective-permute-done.2.refs_3_), channel_id=1, source_target_pairs={{0,16},{16,0},{32,48},{48,32},{64,80},{80,64},{96,112},{112,96},{1... | collective-permute-start | bytes 393224 | tf_op jit(solution)/shard_map/ppermute | solution.py:219
  15.1 10.8 %collective-permute-start.9 = (f32[264,128]{1,0:T(8,128)S(1)}, f32[264,128]{1,0:T(8,128)S(1)}, u32[]{:S(2)}, u32[]{:S(2)}) collective-permute-start(f32[264,128]{1,0:T(8,128)S(1)} %block_matrices.1), channel_id=1, source_target_pairs={{0,64},{16,80},{32,96},{48,112},{64,0},{80,16},{96,32},{112,48},{1... | collective-permute-start | bytes 405512 | tf_op jit(solution)/shard_map/ppermute | solution.py:219
  16.1 9.7 %collective-permute-start.8 = (f32[264,128]{1,0:T(8,128)S(1)}, f32[264,128]{1,0:T(8,128)S(1)}, u32[]{:S(2)}, u32[]{:S(2)}) collective-permute-start(f32[264,128]{1,0:T(8,128)S(1)} %block_matrices.1), channel_id=1, source_target_pairs={{0,2},{1,3},{2,4},{3,5},{4,6},{5,7},{6,8},{7,9},{8,10},{9,11},{10,... | collective-permute-start | bytes 405512 | tf_op jit(solution)/shard_map/ppermute | solution.py:235
  22.2 4.3 %collective-permute-start.7 = (f32[264,128]{1,0:T(8,128)S(1)}, f32[264,128]{1,0:T(8,128)S(1)}, u32[]{:S(2)}, u32[]{:S(2)}) collective-permute-start(f32[264,128]{1,0:T(8,128)S(1)} %block_matrices.1), channel_id=1, source_target_pairs={{0,32},{1,33},{2,34},{3,35},{4,36},{5,37},{6,38},{7,39},{8,40},{9,... | collective-permute-start | bytes 405512 | tf_op jit(solution)/shard_map/ppermute | solution.py:235
  24.6 1.2 %collective-permute-start.10 = (f32[80,128]{1,0:T(8,128)S(1)}, f32[80,128]{1,0:T(8,128)S(1)}, u32[]{:S(2)}, u32[]{:S(2)}) collective-permute-start(f32[80,128]{1,0:T(8,128)S(1)} %broadcast_in_dim.28.weight_ref), channel_id=1, source_target_pairs={{0,16},{16,0},{32,48},{48,32},{64,80},{80,64},{96,112},{112,96},{1... | collective-permute-start | bytes 122888 | tf_op jit(solution)/shard_map/ppermute | solution.py:219
  26.5 1.4 %collective-permute-start.12 = (f32[264,128]{1,0:T(8,128)S(1)}, f32[264,128]{1,0:T(8,128)S(1)}, u32[]{:S(2)}, u32[]{:S(2)}) collective-permute-start(f32[264,128]{1,0:T(8,128)S(1)} %collective-permute-done.8.far), channel_id=1, source_target_pairs={{0,16},{16,0},{32,48},{48,32},{64,80},{80,64},{96,112},{112,96},{1... | collective-permute-start | bytes 405512 | tf_op jit(solution)/shard_map/ppermute | solution.py:219
  26.9 1.4 %collective-permute-start.11 = (f32[264,128]{1,0:T(8,128)S(1)}, f32[264,128]{1,0:T(8,128)S(1)}, u32[]{:S(2)}, u32[]{:S(2)}) collective-permute-start(f32[264,128]{1,0:T(8,128)S(1)} %collective-permute-done.7), channel_id=1, source_target_pairs={{0,16},{16,0},{32,48},{48,32},{64,80},{80,64},{96,112},{112,96},{1... | collective-permute-start | bytes 405512 | tf_op jit(solution)/shard_map/ppermute | solution.py:219
  28.3 12.6 %collective-permute-start.14 = (f32[4,264,128]{2,1,0:T(8,128)S(1)}, f32[4,264,128]{2,1,0:T(8,128)S(1)}, u32[]{:S(2)}, u32[]{:S(2)}) collective-permute-start(f32[4,264,128]{2,1,0:T(8,128)S(1)} %pad_maximum_fusion.same), channel_id=1, source_target_pairs={{0,1},{1,2},{2,3},{3,4},{4,5},{5,6},{6,7},{7,8},{8,9},{9,10},{10,1... | collective-permute-start | bytes 1622024 | tf_op jit(solution)/shard_map/ppermute | solution.py:235
  32.4 8.5 %collective-permute-start.13 = (f32[2,264,128]{2,1,0:T(8,128)S(1)}, f32[2,264,128]{2,1,0:T(8,128)S(1)}, u32[]{:S(2)}, u32[]{:S(2)}) collective-permute-start(f32[2,264,128]{2,1,0:T(8,128)S(1)} %pad_maximum_fusion.1), channel_id=1, source_target_pairs={{0,32},{1,33},{2,34},{3,35},{4,36},{5,37},{6,38},{7,39},{8,40},{9,... | collective-permute-start | bytes 811016 | tf_op jit(solution)/shard_map/ppermute | solution.py:235
  34.7 6.2 %collective-permute-start.15 = (f32[264,128]{1,0:T(8,128)S(1)}, f32[264,128]{1,0:T(8,128)S(1)}, u32[]{:S(2)}, u32[]{:S(2)}) collective-permute-start(f32[264,128]{1,0:T(8,128)S(1)} %collective-permute-done.8.far), channel_id=1, source_target_pairs={{0,64},{16,80},{32,96},{48,112},{64,0},{80,16},{96,32},{112,48},{1... | collective-permute-start | bytes 405512 | tf_op jit(solution)/shard_map/ppermute | solution.py:219
  41.3 2.2 %collective-permute-start.16 = (f32[4,264,128]{2,1,0:T(8,128)S(1)}, f32[4,264,128]{2,1,0:T(8,128)S(1)}, u32[]{:S(2)}, u32[]{:S(2)}) collective-permute-start(f32[4,264,128]{2,1,0:T(8,128)S(1)} %late_kernel.3), channel_id=1, source_target_pairs={{0,16},{16,0},{32,48},{48,32},{64,80},{80,64},{96,112},{112,96},{1... | collective-permute-start | bytes 1622024 | tf_op jit(solution)/shard_map/ppermute | solution.py:219
